TPU v7x, 32 devices: a whole 2x2x4 slice. The times are simulated.
32 devices in a mesh: dp: 4 (over x, core), fsdp: 8 (over z, y).
Axes of the slice: x: 2, y: 2, z: 4, core: 2. Of those that a mesh axis runs over, the one named last changes fastest.
Arguments:
- attn_heads: bfloat16 [64, 4096], P('dp', 'fsdp'), may hold values from -6 to 6
- out_proj: bfloat16 [4096, 4608], P('fsdp'), may hold values from -0.09375 to 0.09375
- resid_pre: bfloat16 [64, 4608], P(('dp', 'fsdp')), may hold values from -25 to 25
- post_gain: float32 [4608], replicated, may hold values from 0.5 to 1.5
- enc_weight: bfloat16 [4608, 65536], P(None, ('dp', 'fsdp')), may hold values from -0.09375 to 0.09375
- enc_bias: float32 [65536], P(('dp', 'fsdp')), may hold values from -3 to 3
- dec_weight: bfloat16 [65536, 4608], P(('dp', 'fsdp')), may hold values from -0.046875 to 0.046875
- dec_bias: float32 [4608], replicated, may hold values from -3 to 3
Outputs:
- enc_grad: bfloat16 [4608, 65536], P(None, ('dp', 'fsdp'))
- enc_bias_grad: float32 [65536], P(('dp', 'fsdp'))
- dec_grad: bfloat16 [65536, 4608], P(('dp', 'fsdp'))
- dec_bias_grad: float32 [4608], replicated
- loss: float32 [], replicated
All inputs are finite; a program needn't handle non-finite values.
Results may differ from a plain program's by a relative error of at most 0.013.
Values may be sent and summed in bfloat16 or wider, within the bound.
No kernel may reach another device: no remote copies, remote signals or barrier semaphores. Data moves between devices by JAX's collectives and lax.ppermute only.
A program may use at most 128 MiB of HBM per device.

v0:
```python
import jax
import jax.numpy as jnp
from jax import lax
from jax.sharding import PartitionSpec as P

SPARSITY = 0.25
SMOOTHING = 0.1
EPSILON = 1e-06


def finish(summed, resid_rows, post_gain):
    scale = lax.rsqrt(jnp.mean(summed * summed, axis=-1, keepdims=True) + EPSILON)
    return (resid_rows.astype(jnp.float32) + summed * scale * post_gain).astype(jnp.bfloat16)


def body(attn_heads, out_proj, resid_pre, post_gain, enc_weight, enc_bias, dec_weight, dec_bias):
    block = attn_heads
    summed = lax.psum_scatter(
        jnp.dot(block, out_proj, preferred_element_type=jnp.float32),
        "fsdp",
        scatter_dimension=0,
        tiled=True,
    )
    resid_own = finish(summed, resid_pre, post_gain)
    resid_all = lax.all_gather(resid_own, ("dp", "fsdp"), axis=0, tiled=True)
    preact = jnp.dot(resid_all, enc_weight, preferred_element_type=jnp.float32) + enc_bias
    latents = jnp.maximum(preact, 0.0)
    latents_b = latents.astype(jnp.bfloat16)
    row_norms = jnp.sqrt(jnp.sum(jnp.square(dec_weight.astype(jnp.float32)), axis=1) + EPSILON)
    penalty_local = jnp.sum(latents * row_norms)
    penalty_total = lax.psum(penalty_local, ("dp", "fsdp"))
    block = latents_b
    recon = lax.psum_scatter(
        jnp.dot(block, dec_weight, preferred_element_type=jnp.float32),
        ("dp", "fsdp"),
        scatter_dimension=0,
        tiled=True,
    )
    recon = recon + dec_bias
    error = recon - resid_own.astype(jnp.float32)
    error_local = jnp.sum(error * error)
    error_total = lax.psum(error_local, ("dp", "fsdp"))
    loss = (0.5 * error_total + SPARSITY * penalty_total) / (
        resid_all.shape[0] * resid_all.shape[1]
    )
    error_b = error.astype(jnp.bfloat16)
    error_all = lax.all_gather(error_b, ("dp", "fsdp"), axis=0, tiled=True)
    dec_bias_grad = jnp.sum(error_all, axis=0, dtype=jnp.float32)
    usage = jnp.sum(latents, axis=0)
    dec_grad = lax.dot_general(
        latents_b, error_all, (((0,), (0,)), ((), ())), preferred_element_type=jnp.float32
    )
    dec_grad = (
        dec_grad + SPARSITY * (usage / row_norms)[:, None] * dec_weight.astype(jnp.float32)
    ).astype(jnp.bfloat16)
    latent_grad = lax.dot_general(
        error_all, dec_weight, (((1,), (1,)), ((), ())), preferred_element_type=jnp.float32
    )
    latent_grad = latent_grad + SPARSITY * row_norms
    preact_grad = latent_grad * jax.nn.sigmoid(preact / SMOOTHING)
    enc_bias_grad = jnp.sum(preact_grad, axis=0)
    enc_grad = lax.dot_general(
        resid_all,
        preact_grad.astype(jnp.bfloat16),
        (((0,), (0,)), ((), ())),
        preferred_element_type=jnp.float32,
    ).astype(jnp.bfloat16)
    return (enc_grad, enc_bias_grad, dec_grad, dec_bias_grad, loss)


def solution(mesh):
    placed = (
        P("dp", "fsdp"),
        P("fsdp", None),
        P(("dp", "fsdp"), None),
        P(),
        P(None, ("dp", "fsdp")),
        P(("dp", "fsdp")),
        P(("dp", "fsdp"), None),
        P(),
    )
    return jax.shard_map(
        body,
        mesh=mesh,
        in_specs=placed,
        out_specs=(P(None, ("dp", "fsdp")), P(("dp", "fsdp")), P(("dp", "fsdp"), None), P(), P()),
        check_vma=False,
    )
```

profile of v0, /device:TPU:0, one launch (start us, length us, event | category | flops | bytes accessed | tf_op | source)
XLA Modules:
  0.0 457.7 jit_solution(5183424245226375187)
XLA Ops:
  7.2 0.0 copy-start
  7.2 0.0 copy-start.6
  7.2 0.0 copy-start.2
  7.2 0.0 copy-start.4
  7.2 0.0 copy-start.5
  7.2 0.0 all-reduce.6.cloned.1.call-start
  7.3 0.6 copy-done
  7.9 3.8 fusion.10
  11.7 0.0 all-reduce.6.cloned.1.call-update
  11.7 0.0 all-reduce.8.cloned.1.call-start
  11.7 8.0 %fusion = f32[2048]{0:T(1024)S(1)} fusion(bf16[2048,4608]{1,0:T(8,128)(2,1)} %param.14), kind=kLoop, calls=%fused_computation.2 | loop fusion | flops 28309504 | bytes 18882560 | tf_op jit(solution)/shard_map/reduce_sum | solution.py:29
  19.8 0.0 copy-done.6
  19.8 0.6 dynamic-slice
  21.0 64.5 %all-reduce.6.cloned.1.call-done = f32[16,4608]{1,0:T(8,128)} async-done(((f32[16,4608]{1,0:T(8,128)}), f32[16,4608]{1,0:T(8,128)}) %all-reduce.6.cloned.1.call-update) | async-done | bytes 294928
  85.5 1.1 multiply_reduce_fusion.2
  86.6 0.0 copy-done.2
  86.6 0.0 copy-done.4
  86.6 1.0 add_convert_fusion
  87.6 67.8 %all-gather = bf16[32,2,4608]{2,1,0:T(2,128)(2,1)S(1)} all-gather(bf16[1,2,4608]{2,1,0:T(2,128)(2,1)S(1)} %bitcast.14), channel_id=1, replica_groups=mesh['dp'=4,'fsdp'=8] {'dp','fsdp'}, dimensions={0}, use_global_device_ids=true | all-gather | bytes 608256 | tf_op jit(solution)/shard_map/all_gather | solution.py:25
  155.4 0.2 reshape.38
  155.7 0.0 copy-done.5
  155.7 8.8 %multiply_reduce_fusion = (f32[]{:T(128)}, f32[2048]{0:T(1024)S(1)}, f32[64,2048]{1,0:T(8,128)S(1)}) fusion(f32[2048]{0:T(1024)S(1)} %add_sqrt_fusion, f32[2048]{0:T(1024)S(1)} %copy-done.5, bf16[64,4608]{1,0:T(8,128)(2,1)S(1)} %reshape.38, bf16[4608,2048]{1,0:T(8,128)(2,1)} %param.12), kind=kOutput, calls=%fused_computation.10 | convolution fusion | flops 1208612864 | bytes 20013060 | tf_op jit(solution)/shard_map/dot_general | solution.py:26
  164.5 0.0 copy-start.3
  164.5 10.7 %fusion.5 = f32[64,4608]{1,0:T(8,128)} fusion(bf16[2048,4608]{1,0:T(8,128)(2,1)} %param.14, f32[64,2048]{1,0:T(8,128)S(1)} %get-tuple-element.13), kind=kOutput, calls=%fused_computation.14 | convolution fusion | flops 1208221696 | bytes 20578304 | tf_op jit(solution)/shard_map/dot_general | solution.py:34
  175.2 0.0 all-reduce.8.cloned.1.call-update
  175.2 129.2 %all-reduce.8.cloned.1.call-done = f32[64,4608]{1,0:T(8,128)} async-done(((f32[64,4608]{1,0:T(8,128)}), f32[64,4608]{1,0:T(8,128)}) %all-reduce.8.cloned.1.call-update) | async-done | bytes 1179664
  304.4 0.0 copy-done.3
  304.4 1.6 multiply_reduce_fusion.1
  306.1 68.8 %all-gather.1 = bf16[32,2,4608]{2,1,0:T(2,128)(2,1)S(1)} all-gather(bf16[1,2,4608]{2,1,0:T(2,128)(2,1)S(1)} %get-tuple-element.10), channel_id=1, replica_groups=mesh['dp'=4,'fsdp'=8] {'dp','fsdp'}, dimensions={0}, use_global_device_ids=true | all-gather | bytes 608256 | tf_op jit(solution)/shard_map/all_gather | solution.py:47
  374.8 0.2 reshape.40
  375.1 0.7 convert_reduce_fusion
  375.8 12.7 %fusion.9 = (f32[2048]{0:T(1024)}, bf16[64,2048]{1,0:T(8,128)(2,1)S(1)}) fusion(f32[64,2048]{1,0:T(8,128)S(1)} %get-tuple-element.13, f32[2048]{0:T(1024)S(1)} %get-tuple-element.12, bf16[64,4608]{1,0:T(8,128)(2,1)S(1)} %reshape.40, bf16[2048,4608]{1,0:T(8,128)(2,1)} %param.14), kind=kOutput, calls=%fused_computation.27 | convolution fusion | flops 1209006080 | bytes 20267008 | tf_op jit(solution)/shard_map/dot_general | solution.py:56
  388.5 0.0 copy-start.1
  388.5 13.2 %fusion.2 = bf16[2048,4608]{1,0:T(8,128)(2,1)} fusion(bf16[2048,4608]{1,0:T(8,128)(2,1)} %param.14, bf16[64,4608]{1,0:T(8,128)(2,1)S(1)} %reshape.40, f32[2048]{0:T(1024)S(1)} %get-tuple-element.11, f32[64,2048]{1,0:T(8,128)S(1)} %get-tuple-element.13), kind=kOutput, calls=%fused_computation.4 | convolution fusion | flops 1245970432 | bytes 38871040 | tf_op jit(solution)/shard_map/dot_general | solution.py:50
  401.7 9.5 %convolution_convert_fusion = bf16[4608,2048]{1,0:T(8,128)(2,1)} fusion(bf16[64,4608]{1,0:T(8,128)(2,1)S(1)} %reshape.38, bf16[64,2048]{1,0:T(8,128)(2,1)S(1)} %get-tuple-element.15), kind=kOutput, calls=%fused_computation.5 | convolution fusion | flops 1217396736 | bytes 19726336 | tf_op jit(solution)/shard_map/dot_general | solution.py:62
  411.2 37.1 %all-reduce.2 = (f32[]{:T(128)}, f32[]{:T(128)}) all-reduce(f32[]{:T(128)} %get-tuple-element.9, f32[]{:T(128)} %get-tuple-element.5), channel_id=1, replica_groups=mesh['dp'=4,'fsdp'=8] {'dp','fsdp'}, use_global_device_ids=true, to_apply=%region_8.0 | all-reduce | flops 2 | bytes 16 | tf_op jit(solution)/shard_map/psum | solution.py:42
  449.7 0.0 copy-done.1
  (3 shorter events, 0.0 us)
Async XLA Ops:
  7.2 0.7 copy-start
  7.2 12.6 %copy-start.6 = (u32[32]{0:T(128)S(1)}, u32[32]{0:T(128)}, u32[]{:S(2)}) copy-start(u32[32]{0:T(128)} %constant.26) | copy-start | bytes 388
  7.2 79.4 %copy-start.2 = (f32[4608]{0:T(1024)S(1)}, f32[4608]{0:T(1024)}, u32[]{:S(2)}) copy-start(f32[4608]{0:T(1024)} %param.11) | copy-start | bytes 55300
  7.2 79.4 %copy-start.4 = (bf16[2,4608]{1,0:T(2,128)(2,1)S(1)}, bf16[2,4608]{1,0:T(2,128)(2,1)}, u32[]{:S(2)}) copy-start(bf16[2,4608]{1,0:T(2,128)(2,1)} %param.10) | copy-start | bytes 55300
  7.2 148.5 %copy-start.5 = (f32[2048]{0:T(1024)S(1)}, f32[2048]{0:T(1024)}, u32[]{:S(2)}) copy-start(f32[2048]{0:T(1024)} %param.13) | copy-start | bytes 24580
  7.2 78.3 %all-reduce.6.cloned.1.call-start = ((), (), s32[]{:S(2)}) async-start(), calls=%async_computation | async-start | bytes 589824
  11.7 292.7 %all-reduce.8.cloned.1.call-start = ((), (), s32[]{:S(2)}) async-start(), calls=%async_computation.1 | async-start | bytes 2359296
  164.5 140.0 %copy-start.3 = (f32[4608]{0:T(1024)S(1)}, f32[4608]{0:T(1024)}, u32[]{:S(2)}) copy-start(f32[4608]{0:T(1024)} %param.15) | copy-start | bytes 55300
  388.5 61.2 %copy-start.1 = (bf16[16,512]{1,0:T(8,128)(2,1)S(1)}, bf16[16,512]{1,0:T(8,128)(2,1)}, u32[]{:S(2)}) copy-start(bf16[16,512]{1,0:T(8,128)(2,1)} %param.8) | copy-start | bytes 49156
Sparse Core Ops, SparseCore 0:
  12.0 73.5 all-reduce.5
  175.3 129.0 all-reduce.7
where the time goes:
time: 459 us; the launch traced here: 458 us
  waiting for transfers between devices  194 us (42%)
  blocking collectives  174 us (38%)
  matrix products  58.7 us (13%)
  between operations  17.3 us (4%)
  other arithmetic  12.5 us (3%)
    unnamed x4, waiting for transfers between devices  194 us
    all_gather x1, blocking collectives, body(): error_all = lax.all_gather(error_b, ('dp', 'fsdp'), axis=0, tiled=True)  68.8 us
    all_gather x1, blocking collectives, body(): resid_all = lax.all_gather(resid_own, ('dp', 'fsdp'), axis=0, tiled=True)  67.8 us
    psum x1, blocking collectives, body(): error_total = lax.psum(error_local, ('dp', 'fsdp'))  37.1 us
    dot_general x1, matrix products, body(): lax.dot_general(latents_b, error_all, (((0,), (0,)), ((), ())), preferred...  13.2 us
    dot_general x1, matrix products, body(): lax.dot_general(error_all, dec_weight, (((1,), (1,)), ((), ())), preferre...  12.7 us
    dot_general x1, matrix products, body(): jnp.dot(block, dec_weight, preferred_element_type=jnp.float32)  10.7 us
    dot_general x1, matrix products, body(): lax.dot_general(resid_all, preact_grad.astype(jnp.bfloat16), (((0,), (0,)...  9.49 us
  transfers between devices with their start and end apart: 2, of which 2 were waited for; matrix products, arithmetic and copies ran while one was open for 2% of the time, Pallas kernels for 0%

commit v1 on v0

v1 whole, which is shorter than its diff:
```python
import jax
import jax.numpy as jnp
from jax import lax
from jax.sharding import PartitionSpec as P

SPARSITY = 0.25
SMOOTHING = 0.1
EPSILON = 1e-06
F32 = jnp.float32
BF16 = jnp.bfloat16


class Split:
    def __init__(self, axis, length, inner, size):
        self.axis, self.length, self.inner, self.size = axis, length, inner, size

    def place(self):
        return (lax.axis_index(self.axis) // self.inner) % self.size

    def swap(self, x, k):
        pairs = []
        for i in range(self.length):
            a = (i // self.inner) % self.size
            pairs.append((i, i + ((a ^ k) - a) * self.inner))
        return lax.ppermute(x, self.axis, pairs)

    def scatter_sum(self, x):
        rows = x.shape[0] // self.size
        total = x[:rows].astype(F32)
        for k in range(1, self.size):
            total = total + self.swap(x[k * rows : (k + 1) * rows].astype(BF16), k).astype(F32)
        return total

    def gather(self, x):
        return jnp.concatenate([x] + [self.swap(x, k) for k in range(1, self.size)], axis=0)


def splits(mesh):
    dp, fsdp = mesh.shape["dp"], mesh.shape["fsdp"]
    cores = 2 if dp % 2 == 0 else 1
    deep = 4 if fsdp % 4 == 0 else 1
    return (
        Split("dp", dp, 1, cores),
        Split("dp", dp, cores, dp // cores),
        Split("fsdp", fsdp, fsdp // deep, deep),
        Split("fsdp", fsdp, 1, fsdp // deep),
    )


def all_sum(split, x):
    rows = x.shape[0] // split.size
    mine = x.astype(BF16)
    parts = [mine.astype(F32).reshape(split.size, rows, -1)]
    for k in range(1, split.size):
        got = split.swap(mine, k).astype(F32).reshape(split.size, rows, -1)
        parts.append(jnp.concatenate([got[j ^ k][None] for j in range(split.size)], axis=0))
    while len(parts) > 1:
        half = len(parts) // 2
        parts = [parts[i] + parts[i + half] for i in range(half)]
    return parts[0].reshape(x.shape)


def make_body(mesh):
    core, across, deep, side = splits(mesh)

    def body(attn_heads, out_proj, resid_pre, post_gain, enc_weight, enc_bias, dec_weight, dec_bias):
        own = resid_pre.shape[0]
        heads = attn_heads.reshape(deep.size, side.size, own, -1)
        heads = jnp.take(heads, jnp.arange(deep.size) ^ deep.place(), axis=0)
        heads = jnp.take(heads, jnp.arange(side.size) ^ side.place(), axis=1)
        heads = heads.reshape(attn_heads.shape)
        resid_rows = side.gather(resid_pre)
        partial = jnp.dot(heads, out_proj, preferred_element_type=F32)
        projected = all_sum(side, deep.scatter_sum(partial))
        scale = lax.rsqrt(jnp.mean(projected * projected, axis=-1, keepdims=True) + EPSILON)
        resid_own = (resid_rows.astype(F32) + projected * scale * post_gain).astype(BF16)
        resid_all = core.gather(across.gather(deep.gather(resid_own)))

        preact = jnp.dot(resid_all, enc_weight, preferred_element_type=F32) + enc_bias
        latents = jnp.maximum(preact, 0.0)
        latents_b = latents.astype(BF16)
        row_norms = jnp.sqrt(jnp.sum(jnp.square(dec_weight.astype(F32)), axis=1) + EPSILON)
        penalty = jnp.full((8, 128), jnp.sum(latents * row_norms), F32)
        for split in (core, across, deep, side):
            k = 1
            while k < split.size:
                penalty = penalty + split.swap(penalty, k)
                k *= 2

        recon = jnp.dot(latents_b, dec_weight, preferred_element_type=F32)
        recon = all_sum(side, deep.scatter_sum(across.scatter_sum(core.scatter_sum(recon))))
        error_own = (recon + dec_bias - resid_own.astype(F32)).astype(BF16)
        error_b = core.gather(across.gather(deep.gather(error_own)))
        error_f = error_b.astype(F32)
        order = error_f.reshape(core.size, across.size, deep.size, side.size, own, -1)
        total = order
        for split in (core, across, deep, side):
            n = split.size
            while n > 1:
                total = total[: n // 2] + total[n // 2 :]
                n //= 2
            total = total[0]
        columns = jnp.sum(total, axis=0)
        squares = order * order
        for split in (core, across, deep, side):
            n = split.size
            while n > 1:
                squares = squares[: n // 2] + squares[n // 2 :]
                n //= 2
            squares = squares[0]
        loss = (0.5 * jnp.sum(squares) + SPARSITY * penalty[0, 0]) / error_b.size

        usage = jnp.sum(latents, axis=0)
        dec_grad = lax.dot_general(latents_b, error_b, (((0,), (0,)), ((), ())), preferred_element_type=F32)
        dec_grad = (dec_grad + SPARSITY * (usage / row_norms)[:, None] * dec_weight.astype(F32)).astype(BF16)
        latent_grad = lax.dot_general(error_b, dec_weight, (((1,), (1,)), ((), ())), preferred_element_type=F32)
        latent_grad = latent_grad + SPARSITY * row_norms
        preact_grad = latent_grad * jax.nn.sigmoid(preact / SMOOTHING)
        enc_bias_grad = jnp.sum(preact_grad, axis=0)
        enc_grad = lax.dot_general(
            resid_all, preact_grad.astype(BF16), (((0,), (0,)), ((), ())), preferred_element_type=F32
        ).astype(BF16)
        return (enc_grad, enc_bias_grad, dec_grad, columns, loss)

    return body


def solution(mesh):
    placed = (
        P("dp", "fsdp"),
        P("fsdp", None),
        P(("dp", "fsdp"), None),
        P(),
        P(None, ("dp", "fsdp")),
        P(("dp", "fsdp")),
        P(("dp", "fsdp"), None),
        P(),
    )
    return jax.shard_map(
        make_body(mesh),
        mesh=mesh,
        in_specs=placed,
        out_specs=(P(None, ("dp", "fsdp")), P(("dp", "fsdp")), P(("dp", "fsdp"), None), P(), P()),
        check_vma=False,
    )
```

time: 459 us -> 154 us (0.34)
  blocking collectives: 174 us -> 0 us
  waiting for transfers between devices: 194 us -> 40.7 us
  starting transfers between devices: 0.08 us -> 30.8 us
  between operations: 17.3 us -> 3.51 us
    unnamed x4 -> x0, waiting for transfers between devices: 194 us -> none
    all_gather x2 -> x0, blocking collectives: 137 us -> none  [the longest x1 68.8 us: body(): error_all = lax.all_gather(error_b, ('dp', 'fsdp'), axis=0, tiled=True)]
    ppermute x0 -> x26, waiting for transfers between devices: none -> 40.7 us  [swap(): return lax.ppermute(x, self.axis, pairs)]
    psum x1 -> x0, blocking collectives: 37.1 us -> none  [body(): error_total = lax.psum(error_local, ('dp', 'fsdp'))]
    ppermute x0 -> x26, starting transfers between devices: none -> 30.8 us  [swap(): return lax.ppermute(x, self.axis, pairs)]
  transfers between devices with their start and end apart: 2 -> 26, of which waited for: 2 -> 21; matrix products, arithmetic and copies ran while one was open for 2% -> 7% of each run, Pallas kernels for 0% -> 0%
where the time goes in v1:
time: 154 us
  matrix products  56.2 us (36%)
  waiting for transfers between devices  40.7 us (26%)
  starting transfers between devices  30.8 us (20%)
  other arithmetic  16.4 us (11%)
  local copies, waits for them, and re-layouts  6.13 us (4%)
  between operations  3.51 us (2%)
    ppermute x26, waiting for transfers between devices, swap(): return lax.ppermute(x, self.axis, pairs)  40.7 us
    ppermute x26, starting transfers between devices, swap(): return lax.ppermute(x, self.axis, pairs)  30.8 us
    dot_general x1, matrix products, body(): lax.dot_general(error_b, dec_weight, (((1,), (1,)), ((), ())), preferred_...  13.4 us
    dot_general x1, matrix products, body(): lax.dot_general(latents_b, error_b, (((0,), (0,)), ((), ())), preferred_e...  13.2 us
    dot_general x1, matrix products, body(): lax.dot_general(resid_all, preact_grad.astype(BF16), (((0,), (0,)), ((),...  9.5 us
    dot_general x1, matrix products, body(): jnp.dot(resid_all, enc_weight, preferred_element_type=F32) + enc_bias  8.77 us
    dot_general x1, matrix products, body(): recon = jnp.dot(latents_b, dec_weight, preferred_element_type=F32)  8.12 us
    reduce_sum x1, other arithmetic, body(): jnp.sum(jnp.square(dec_weight.astype(F32)), axis=1) + EPSILON  8.03 us
  transfers between devices with their start and end apart: 26, of which 21 were waited for; matrix products, arithmetic and copies ran while one was open for 7% of the time, Pallas kernels for 0%

profile of v1, /device:TPU:0, one launch (start us, length us, event | category | flops | bytes accessed | tf_op | source)
XLA Modules:
  0.0 153.7 jit_solution(12720255540554736494)
XLA Ops:
  0.9 0.7 reshape.207
  3.0 3.1 %fusion.30 = (bf16[16,4608]{1,0:T(8,128)(2,1)S(1)}, f32[16,4608]{1,0:T(8,128)S(1)}) fusion(bf16[512,4608]{1,0:T(8,128)(2,1)} %param.9, bf16[16,512]{1,0:T(8,128)(2,1)S(1)} %gather.12, pred[16]{0:T(512)(128)(4,1)S(1)} %broadcast_in_dim.35), kind=kOutput, calls=%fused_computation.83 | convolution fusion | flops 75579392 | bytes 5177360 | tf_op jit(solution)/shard_map/dot_general | solution.py:73
  6.1 3.1 %collective-permute-start.1 = (bf16[4,4608]{1,0:T(4,128)(2,1)S(1)}, bf16[4,4608]{1,0:T(4,128)(2,1)S(1)}, u32[]{:S(2)}, u32[]{:S(2)}) collective-permute-start(bf16[4,4608]{1,0:T(4,128)(2,1)S(1)} %get-tuple-element.12), channel_id=1, source_target_pairs={{0,2},{1,3},{2,0},{3,1},{4,6},{5,7},{6,4},{7,5},{8,10},{9,11},{10,... | collective-permute-start | bytes 110600 | tf_op jit(solution)/shard_map/ppermute | solution.py:25
  9.2 2.5 %collective-permute-start.3 = (bf16[4,4608]{1,0:T(4,128)(2,1)S(1)}, bf16[4,4608]{1,0:T(4,128)(2,1)S(1)}, u32[]{:S(2)}, u32[]{:S(2)}) collective-permute-start(bf16[4,4608]{1,0:T(4,128)(2,1)S(1)} %get-tuple-element.13), channel_id=1, source_target_pairs={{0,6},{1,7},{2,4},{3,5},{4,2},{5,3},{6,0},{7,1},{8,14},{9,15},{10,... | collective-permute-start | bytes 110600 | tf_op jit(solution)/shard_map/ppermute | solution.py:25
  11.8 3.7 %collective-permute-done.3 = bf16[4,4608]{1,0:T(4,128)(2,1)S(1)} collective-permute-done((bf16[4,4608]{1,0:T(4,128)(2,1)S(1)}, bf16[4,4608]{1,0:T(4,128)(2,1)S(1)}, u32[]{:S(2)}, u32[]{:S(2)}) %collective-permute-start.3) | collective-permute-done | bytes 36896 | tf_op jit(solution)/shard_map/ppermute | solution.py:25
  15.5 1.5 collective-permute-done.2
  17.0 1.6 %collective-permute-start.4 = (bf16[4,4608]{1,0:T(4,128)(2,1)S(1)}, bf16[4,4608]{1,0:T(4,128)(2,1)S(1)}, u32[]{:S(2)}, u32[]{:S(2)}) collective-permute-start(bf16[4,4608]{1,0:T(4,128)(2,1)S(1)} %fusion.15), channel_id=1, source_target_pairs={{0,1},{1,0},{2,3},{3,2},{4,5},{5,4},{6,7},{7,6},{8,9},{9,8},{10,11... | collective-permute-start | bytes 110600 | tf_op jit(solution)/shard_map/ppermute | solution.py:25
  19.1 1.9 %collective-permute-done.4 = bf16[4,4608]{1,0:T(4,128)(2,1)S(1)} collective-permute-done((bf16[4,4608]{1,0:T(4,128)(2,1)S(1)}, bf16[4,4608]{1,0:T(4,128)(2,1)S(1)}, u32[]{:S(2)}, u32[]{:S(2)}) %collective-permute-start.4) | collective-permute-done | bytes 36896 | tf_op jit(solution)/shard_map/ppermute | solution.py:25
  21.4 1.2 collective-permute-done
  22.6 0.8 add_convert_fusion
  23.4 1.5 collective-permute-start.7
  25.3 2.5 %collective-permute-start.5 = (bf16[4,4608]{1,0:T(4,128)(2,1)S(1)}, bf16[4,4608]{1,0:T(4,128)(2,1)S(1)}, u32[]{:S(2)}, u32[]{:S(2)}) collective-permute-start(bf16[4,4608]{1,0:T(4,128)(2,1)S(1)} %add_convert_fusion), channel_id=1, source_target_pairs={{0,2},{1,3},{2,0},{3,1},{4,6},{5,7},{6,4},{7,5},{8,10},{9,11},{10,... | collective-permute-start | bytes 110600 | tf_op jit(solution)/shard_map/ppermute | solution.py:25
  27.8 1.4 collective-permute-done.7
  29.2 0.9 collective-permute-done.6
  30.3 1.6 %collective-permute-start.8 = (bf16[16,4608]{1,0:T(8,128)(2,1)S(1)}, bf16[16,4608]{1,0:T(8,128)(2,1)S(1)}, u32[]{:S(2)}, u32[]{:S(2)}) collective-permute-start(bf16[16,4608]{1,0:T(8,128)(2,1)S(1)} %pad_maximum_fusion), channel_id=1, source_target_pairs={{0,16},{8,24},{16,0},{24,8},{1,17},{9,25},{17,1},{25,9},{2,18},{10... | collective-permute-start | bytes 442376 | tf_op jit(solution)/shard_map/ppermute | solution.py:25
  31.8 3.7 %collective-permute-done.8 = bf16[16,4608]{1,0:T(8,128)(2,1)S(1)} collective-permute-done((bf16[16,4608]{1,0:T(8,128)(2,1)S(1)}, bf16[16,4608]{1,0:T(8,128)(2,1)S(1)}, u32[]{:S(2)}, u32[]{:S(2)}) %collective-permute-start.8) | collective-permute-done | bytes 147488 | tf_op jit(solution)/shard_map/ppermute | solution.py:25
  35.8 8.0 %fusion = f32[2048]{0:T(1024)S(1)} fusion(bf16[2048,4608]{1,0:T(8,128)(2,1)} %param.14), kind=kLoop, calls=%fused_computation.4 | loop fusion | flops 28309504 | bytes 18882560 | tf_op jit(solution)/shard_map/reduce_sum | solution.py:82
  44.2 8.8 %multiply_reduce_fusion = (f32[]{:T(128)}, f32[2048]{0:T(1024)S(1)}, f32[64,2048]{1,0:T(8,128)S(1)}) fusion(f32[2048]{0:T(1024)S(1)} %add_sqrt_fusion, f32[2048]{0:T(1024)S(1)} %copy-done.2, bf16[64,4608]{1,0:T(8,128)(2,1)S(1)} %concatenate.40, bf16[4608,2048]{1,0:T(8,128)(2,1)} %param.12), kind=kOutput, calls=%fused_computation.15 | convolution fusion | flops 1208612864 | bytes 20013060 | tf_op jit(solution)/shard_map/dot_general | solution.py:79
  52.9 8.1 %fusion.7 = f32[64,4608]{1,0:T(8,128)S(1)} fusion(bf16[2048,4608]{1,0:T(8,128)(2,1)} %param.14, f32[64,2048]{1,0:T(8,128)S(1)} %get-tuple-element.23), kind=kOutput, calls=%fused_computation.30 | convolution fusion | flops 1208221696 | bytes 20578304 | tf_op jit(solution)/shard_map/dot_general | solution.py:90
  61.7 1.2 collective-permute-done.10
  62.9 1.6 %collective-permute-start.11 = (bf16[16,4608]{1,0:T(8,128)(2,1)S(1)}, bf16[16,4608]{1,0:T(8,128)(2,1)S(1)}, u32[]{:S(2)}, u32[]{:S(2)}) collective-permute-start(bf16[16,4608]{1,0:T(8,128)(2,1)S(1)} %slice.287), channel_id=1, source_target_pairs={{0,16},{8,24},{16,0},{24,8},{1,17},{9,25},{17,1},{25,9},{2,18},{10... | collective-permute-start | bytes 442376 | tf_op jit(solution)/shard_map/ppermute | solution.py:25
  64.5 4.6 %collective-permute-done.11 = bf16[16,4608]{1,0:T(8,128)(2,1)S(1)} collective-permute-done((bf16[16,4608]{1,0:T(8,128)(2,1)S(1)}, bf16[16,4608]{1,0:T(8,128)(2,1)S(1)}, u32[]{:S(2)}, u32[]{:S(2)}) %collective-permute-start.11) | collective-permute-done | bytes 147488 | tf_op jit(solution)/shard_map/ppermute | solution.py:25
  69.2 1.7 %collective-permute-start.12 = (bf16[4,4608]{1,0:T(4,128)(2,1)S(1)}, bf16[4,4608]{1,0:T(4,128)(2,1)S(1)}, u32[]{:S(2)}, u32[]{:S(2)}) collective-permute-start(bf16[4,4608]{1,0:T(4,128)(2,1)S(1)} %get-tuple-element.9), channel_id=1, source_target_pairs={{0,2},{1,3},{2,0},{3,1},{4,6},{5,7},{6,4},{7,5},{8,10},{9,11},{10,... | collective-permute-start | bytes 110600 | tf_op jit(solution)/shard_map/ppermute | solution.py:25
  70.9 1.5 collective-permute-start.14
  73.2 3.4 %collective-permute-done.14 = bf16[4,4608]{1,0:T(4,128)(2,1)S(1)} collective-permute-done((bf16[4,4608]{1,0:T(4,128)(2,1)S(1)}, bf16[4,4608]{1,0:T(4,128)(2,1)S(1)}, u32[]{:S(2)}, u32[]{:S(2)}) %collective-permute-start.14) | collective-permute-done | bytes 36896 | tf_op jit(solution)/shard_map/ppermute | solution.py:25
  76.7 0.8 collective-permute-done.13
  78.1 3.5 %collective-permute-done.15 = bf16[4,4608]{1,0:T(4,128)(2,1)S(1)} collective-permute-done((bf16[4,4608]{1,0:T(4,128)(2,1)S(1)}, bf16[4,4608]{1,0:T(4,128)(2,1)S(1)}, u32[]{:S(2)}, u32[]{:S(2)}) %collective-permute-start.15) | collective-permute-done | bytes 36896 | tf_op jit(solution)/shard_map/ppermute | solution.py:25
  81.8 2.2 %collective-permute-start.18 = (bf16[4,4608]{1,0:T(4,128)(2,1)S(1)}, bf16[4,4608]{1,0:T(4,128)(2,1)S(1)}, u32[]{:S(2)}, u32[]{:S(2)}) collective-permute-start(bf16[4,4608]{1,0:T(4,128)(2,1)S(1)} %subtract_convert_fusion), channel_id=1, source_target_pairs={{0,6},{1,7},{2,4},{3,5},{4,2},{5,3},{6,0},{7,1},{8,14},{9,15},{10,... | collective-permute-start | bytes 110600 | tf_op jit(solution)/shard_map/ppermute | solution.py:25
  84.0 2.2 %collective-permute-start.16 = (bf16[4,4608]{1,0:T(4,128)(2,1)S(1)}, bf16[4,4608]{1,0:T(4,128)(2,1)S(1)}, u32[]{:S(2)}, u32[]{:S(2)}) collective-permute-start(bf16[4,4608]{1,0:T(4,128)(2,1)S(1)} %subtract_convert_fusion), channel_id=1, source_target_pairs={{0,2},{1,3},{2,0},{3,1},{4,6},{5,7},{6,4},{7,5},{8,10},{9,11},{10,... | collective-permute-start | bytes 110600 | tf_op jit(solution)/shard_map/ppermute | solution.py:25
  86.2 0.6 broadcast_in_dim.40
  87.6 1.2 collective-permute-done.17
  88.9 1.6 %collective-permute-start.19 = (bf16[16,4608]{1,0:T(8,128)(2,1)S(1)}, bf16[16,4608]{1,0:T(8,128)(2,1)S(1)}, u32[]{:S(2)}, u32[]{:S(2)}) collective-permute-start(bf16[16,4608]{1,0:T(8,128)(2,1)S(1)} %pad_maximum_fusion.1), channel_id=1, source_target_pairs={{0,16},{8,24},{16,0},{24,8},{1,17},{9,25},{17,1},{25,9},{2,18},{10... | collective-permute-start | bytes 442376 | tf_op jit(solution)/shard_map/ppermute | solution.py:25
  90.5 0.6 broadcast_add_fusion
  91.7 2.4 %collective-permute-done.19 = bf16[16,4608]{1,0:T(8,128)(2,1)S(1)} collective-permute-done((bf16[16,4608]{1,0:T(8,128)(2,1)S(1)}, bf16[16,4608]{1,0:T(8,128)(2,1)S(1)}, u32[]{:S(2)}, u32[]{:S(2)}) %collective-permute-start.19) | collective-permute-done | bytes 147488 | tf_op jit(solution)/shard_map/ppermute | solution.py:25
  94.8 0.6 fusion.41
  95.5 1.4 collective-permute-start.23
  96.9 2.3 %collective-permute-done.23 = f32[8,128]{1,0:T(8,128)S(1)} collective-permute-done((f32[8,128]{1,0:T(8,128)S(1)}, f32[8,128]{1,0:T(8,128)S(1)}, u32[]{:S(2)}, u32[]{:S(2)}) %collective-permute-start.23) | collective-permute-done | bytes 4128 | tf_op jit(solution)/shard_map/ppermute | solution.py:25
  99.1 2.0 %collective-permute-start.24 = (f32[8,128]{1,0:T(8,128)S(1)}, f32[8,128]{1,0:T(8,128)S(1)}, u32[]{:S(2)}, u32[]{:S(2)}) collective-permute-start(f32[8,128]{1,0:T(8,128)S(1)} %add.275), channel_id=1, source_target_pairs={{0,4},{1,5},{2,6},{3,7},{4,0},{5,1},{6,2},{7,3},{8,12},{9,13},{10,... | collective-permute-start | bytes 12296 | tf_op jit(solution)/shard_map/ppermute | solution.py:25
  101.2 2.5 %collective-permute-done.24 = f32[8,128]{1,0:T(8,128)S(1)} collective-permute-done((f32[8,128]{1,0:T(8,128)S(1)}, f32[8,128]{1,0:T(8,128)S(1)}, u32[]{:S(2)}, u32[]{:S(2)}) %collective-permute-start.24) | collective-permute-done | bytes 4128 | tf_op jit(solution)/shard_map/ppermute | solution.py:25
  104.2 3.1 %collective-permute-done.25 = f32[8,128]{1,0:T(8,128)S(1)} collective-permute-done((f32[8,128]{1,0:T(8,128)S(1)}, f32[8,128]{1,0:T(8,128)S(1)}, u32[]{:S(2)}, u32[]{:S(2)}) %collective-permute-start.25) | collective-permute-done | bytes 4128 | tf_op jit(solution)/shard_map/ppermute | solution.py:25
  108.8 1.1 convert_multiply_fusion.2
  109.9 13.4 %fusion.31 = (f32[2048]{0:T(1024)}, bf16[64,2048]{1,0:T(8,128)(2,1)}) fusion(f32[64,2048]{1,0:T(8,128)S(1)} %get-tuple-element.23, f32[2048]{0:T(1024)S(1)} %get-tuple-element.20, bf16[64,4608]{1,0:T(8,128)(2,1)S(1)} %concatenate.45, bf16[2048,4608]{1,0:T(8,128)(2,1)} %param.14), kind=kOutput, calls=%fused_computation.84 | convolution fusion | flops 1209006080 | bytes 20267008 | tf_op jit(solution)/shard_map/dot_general | solution.py:116
  123.4 1.3 slice_add_fusion
  124.7 1.2 add.266
  125.8 1.2 fusion.4
  128.5 0.7 fusion.17
  129.2 13.2 %fusion.2 = bf16[2048,4608]{1,0:T(8,128)(2,1)} fusion(bf16[2048,4608]{1,0:T(8,128)(2,1)} %param.14, bf16[64,4608]{1,0:T(8,128)(2,1)S(1)} %concatenate.45, f32[2048]{0:T(1024)S(1)} %get-tuple-element.19, f32[64,2048]{1,0:T(8,128)S(1)} %get-tuple-element.23), kind=kOutput, calls=%fused_computation.6 | convolution fusion | flops 1245970432 | bytes 38871040 | tf_op jit(solution)/shard_map/dot_general | solution.py:114
  142.4 9.5 %convolution_convert_fusion = bf16[4608,2048]{1,0:T(8,128)(2,1)} fusion(bf16[64,4608]{1,0:T(8,128)(2,1)S(1)} %concatenate.40, bf16[64,2048]{1,0:T(8,128)(2,1)S(1)} %copy-done), kind=kOutput, calls=%fused_computation.7 | convolution fusion | flops 1217396736 | bytes 19726336 | tf_op jit(solution)/shard_map/dot_general | solution.py:120
  (81 shorter events, 11.0 us)
Async XLA Ops:
  0.6 43.5 %copy-start.2 = (f32[2048]{0:T(1024)S(1)}, f32[2048]{0:T(1024)}, u32[]{:S(2)}) copy-start(f32[2048]{0:T(1024)} %param.13) | copy-start | bytes 24580
  6.1 5.7 %collective-permute-start.1 = (bf16[4,4608]{1,0:T(4,128)(2,1)S(1)}, bf16[4,4608]{1,0:T(4,128)(2,1)S(1)}, u32[]{:S(2)}, u32[]{:S(2)}) collective-permute-start(bf16[4,4608]{1,0:T(4,128)(2,1)S(1)} %get-tuple-element.12), channel_id=1, source_target_pairs={{0,2},{1,3},{2,0},{3,1},{4,6},{5,7},{6,4},{7,5},{8,10},{9,11},{10,... | collective-permute-start | bytes 110600 | tf_op jit(solution)/shard_map/ppermute | solution.py:25
  9.2 6.2 %collective-permute-start.3 = (bf16[4,4608]{1,0:T(4,128)(2,1)S(1)}, bf16[4,4608]{1,0:T(4,128)(2,1)S(1)}, u32[]{:S(2)}, u32[]{:S(2)}) collective-permute-start(bf16[4,4608]{1,0:T(4,128)(2,1)S(1)} %get-tuple-element.13), channel_id=1, source_target_pairs={{0,6},{1,7},{2,4},{3,5},{4,2},{5,3},{6,0},{7,1},{8,14},{9,15},{10,... | collective-permute-start | bytes 110600 | tf_op jit(solution)/shard_map/ppermute | solution.py:25
  11.7 5.3 %collective-permute-start.2 = (bf16[4,4608]{1,0:T(4,128)(2,1)S(1)}, bf16[4,4608]{1,0:T(4,128)(2,1)S(1)}, u32[]{:S(2)}, u32[]{:S(2)}) collective-permute-start(bf16[4,4608]{1,0:T(4,128)(2,1)S(1)} %get-tuple-element.14), channel_id=1, source_target_pairs={{0,4},{1,5},{2,6},{3,7},{4,0},{5,1},{6,2},{7,3},{8,12},{9,13},{10,... | collective-permute-start | bytes 110600 | tf_op jit(solution)/shard_map/ppermute | solution.py:25
  17.0 4.0 %collective-permute-start.4 = (bf16[4,4608]{1,0:T(4,128)(2,1)S(1)}, bf16[4,4608]{1,0:T(4,128)(2,1)S(1)}, u32[]{:S(2)}, u32[]{:S(2)}) collective-permute-start(bf16[4,4608]{1,0:T(4,128)(2,1)S(1)} %fusion.15), channel_id=1, source_target_pairs={{0,1},{1,0},{2,3},{3,2},{4,5},{5,4},{6,7},{7,6},{8,9},{9,8},{10,11... | collective-permute-start | bytes 110600 | tf_op jit(solution)/shard_map/ppermute | solution.py:25
  18.6 4.0 %collective-permute-start = (bf16[2,4608]{1,0:T(2,128)(2,1)}, bf16[2,4608]{1,0:T(2,128)(2,1)S(1)}, u32[]{:S(2)}, u32[]{:S(2)}) collective-permute-start(bf16[2,4608]{1,0:T(2,128)(2,1)} %param.10), channel_id=1, source_target_pairs={{0,1},{1,0},{2,3},{3,2},{4,5},{5,4},{6,7},{7,6},{8,9},{9,8},{10,11... | collective-permute-start | bytes 55304 | tf_op jit(solution)/shard_map/ppermute | solution.py:25
  23.4 5.8 %collective-permute-start.7 = (bf16[4,4608]{1,0:T(4,128)(2,1)S(1)}, bf16[4,4608]{1,0:T(4,128)(2,1)S(1)}, u32[]{:S(2)}, u32[]{:S(2)}) collective-permute-start(bf16[4,4608]{1,0:T(4,128)(2,1)S(1)} %add_convert_fusion), channel_id=1, source_target_pairs={{0,6},{1,7},{2,4},{3,5},{4,2},{5,3},{6,0},{7,1},{8,14},{9,15},{10,... | collective-permute-start | bytes 110600 | tf_op jit(solution)/shard_map/ppermute | solution.py:25
  24.9 5.2 %collective-permute-start.6 = (bf16[4,4608]{1,0:T(4,128)(2,1)S(1)}, bf16[4,4608]{1,0:T(4,128)(2,1)S(1)}, u32[]{:S(2)}, u32[]{:S(2)}) collective-permute-start(bf16[4,4608]{1,0:T(4,128)(2,1)S(1)} %add_convert_fusion), channel_id=1, source_target_pairs={{0,4},{1,5},{2,6},{3,7},{4,0},{5,1},{6,2},{7,3},{8,12},{9,13},{10,... | collective-permute-start | bytes 110600 | tf_op jit(solution)/shard_map/ppermute | solution.py:25
  25.3 4.9 %collective-permute-start.5 = (bf16[4,4608]{1,0:T(4,128)(2,1)S(1)}, bf16[4,4608]{1,0:T(4,128)(2,1)S(1)}, u32[]{:S(2)}, u32[]{:S(2)}) collective-permute-start(bf16[4,4608]{1,0:T(4,128)(2,1)S(1)} %add_convert_fusion), channel_id=1, source_target_pairs={{0,2},{1,3},{2,0},{3,1},{4,6},{5,7},{6,4},{7,5},{8,10},{9,11},{10,... | collective-permute-start | bytes 110600 | tf_op jit(solution)/shard_map/ppermute | solution.py:25
  30.3 5.2 %collective-permute-start.8 = (bf16[16,4608]{1,0:T(8,128)(2,1)S(1)}, bf16[16,4608]{1,0:T(8,128)(2,1)S(1)}, u32[]{:S(2)}, u32[]{:S(2)}) collective-permute-start(bf16[16,4608]{1,0:T(8,128)(2,1)S(1)} %pad_maximum_fusion), channel_id=1, source_target_pairs={{0,16},{8,24},{16,0},{24,8},{1,17},{9,25},{17,1},{25,9},{2,18},{10... | collective-permute-start | bytes 442376 | tf_op jit(solution)/shard_map/ppermute | solution.py:25
  35.7 8.1 %collective-permute-start.9 = (bf16[32,4608]{1,0:T(8,128)(2,1)S(1)}, bf16[32,4608]{1,0:T(8,128)(2,1)S(1)}, u32[]{:S(2)}, u32[]{:S(2)}) collective-permute-start(bf16[32,4608]{1,0:T(8,128)(2,1)S(1)} %concatenate.39), channel_id=1, source_target_pairs={{0,8},{8,0},{16,24},{24,16},{1,9},{9,1},{17,25},{25,17},{2,10},{10... | collective-permute-start | bytes 884744 | tf_op jit(solution)/shard_map/ppermute | solution.py:25
  52.9 28.8 %copy-start.1 = (f32[4608]{0:T(1024)S(1)}, f32[4608]{0:T(1024)}, u32[]{:S(2)}) copy-start(f32[4608]{0:T(1024)} %param.15) | copy-start | bytes 55300
  61.1 1.8 %collective-permute-start.10 = (bf16[32,4608]{1,0:T(8,128)(2,1)S(1)}, bf16[32,4608]{1,0:T(8,128)(2,1)S(1)}, u32[]{:S(2)}, u32[]{:S(2)}) collective-permute-start(bf16[32,4608]{1,0:T(8,128)(2,1)S(1)} %slice.286), channel_id=1, source_target_pairs={{0,8},{8,0},{16,24},{24,16},{1,9},{9,1},{17,25},{25,17},{2,10},{10... | collective-permute-start | bytes 884744 | tf_op jit(solution)/shard_map/ppermute | solution.py:25
  62.9 6.2 %collective-permute-start.11 = (bf16[16,4608]{1,0:T(8,128)(2,1)S(1)}, bf16[16,4608]{1,0:T(8,128)(2,1)S(1)}, u32[]{:S(2)}, u32[]{:S(2)}) collective-permute-start(bf16[16,4608]{1,0:T(8,128)(2,1)S(1)} %slice.287), channel_id=1, source_target_pairs={{0,16},{8,24},{16,0},{24,8},{1,17},{9,25},{17,1},{25,9},{2,18},{10... | collective-permute-start | bytes 442376 | tf_op jit(solution)/shard_map/ppermute | solution.py:25
  69.2 4.0 %collective-permute-start.12 = (bf16[4,4608]{1,0:T(4,128)(2,1)S(1)}, bf16[4,4608]{1,0:T(4,128)(2,1)S(1)}, u32[]{:S(2)}, u32[]{:S(2)}) collective-permute-start(bf16[4,4608]{1,0:T(4,128)(2,1)S(1)} %get-tuple-element.9), channel_id=1, source_target_pairs={{0,2},{1,3},{2,0},{3,1},{4,6},{5,7},{6,4},{7,5},{8,10},{9,11},{10,... | collective-permute-start | bytes 110600 | tf_op jit(solution)/shard_map/ppermute | solution.py:25
  70.9 5.8 %collective-permute-start.14 = (bf16[4,4608]{1,0:T(4,128)(2,1)S(1)}, bf16[4,4608]{1,0:T(4,128)(2,1)S(1)}, u32[]{:S(2)}, u32[]{:S(2)}) collective-permute-start(bf16[4,4608]{1,0:T(4,128)(2,1)S(1)} %get-tuple-element.10), channel_id=1, source_target_pairs={{0,6},{1,7},{2,4},{3,5},{4,2},{5,3},{6,0},{7,1},{8,14},{9,15},{10,... | collective-permute-start | bytes 110600 | tf_op jit(solution)/shard_map/ppermute | solution.py:25
  72.4 5.1 %collective-permute-start.13 = (bf16[4,4608]{1,0:T(4,128)(2,1)S(1)}, bf16[4,4608]{1,0:T(4,128)(2,1)S(1)}, u32[]{:S(2)}, u32[]{:S(2)}) collective-permute-start(bf16[4,4608]{1,0:T(4,128)(2,1)S(1)} %get-tuple-element.11), channel_id=1, source_target_pairs={{0,4},{1,5},{2,6},{3,7},{4,0},{5,1},{6,2},{7,3},{8,12},{9,13},{10,... | collective-permute-start | bytes 110600 | tf_op jit(solution)/shard_map/ppermute | solution.py:25
  77.5 4.0 %collective-permute-start.15 = (bf16[4,4608]{1,0:T(4,128)(2,1)S(1)}, bf16[4,4608]{1,0:T(4,128)(2,1)S(1)}, u32[]{:S(2)}, u32[]{:S(2)}) collective-permute-start(bf16[4,4608]{1,0:T(4,128)(2,1)S(1)} %fusion.12), channel_id=1, source_target_pairs={{0,1},{1,0},{2,3},{3,2},{4,5},{5,4},{6,7},{7,6},{8,9},{9,8},{10,11... | collective-permute-start | bytes 110600 | tf_op jit(solution)/shard_map/ppermute | solution.py:25
  81.8 5.8 %collective-permute-start.18 = (bf16[4,4608]{1,0:T(4,128)(2,1)S(1)}, bf16[4,4608]{1,0:T(4,128)(2,1)S(1)}, u32[]{:S(2)}, u32[]{:S(2)}) collective-permute-start(bf16[4,4608]{1,0:T(4,128)(2,1)S(1)} %subtract_convert_fusion), channel_id=1, source_target_pairs={{0,6},{1,7},{2,4},{3,5},{4,2},{5,3},{6,0},{7,1},{8,14},{9,15},{10,... | collective-permute-start | bytes 110600 | tf_op jit(solution)/shard_map/ppermute | solution.py:25
  84.0 4.9 %collective-permute-start.17 = (bf16[4,4608]{1,0:T(4,128)(2,1)S(1)}, bf16[4,4608]{1,0:T(4,128)(2,1)S(1)}, u32[]{:S(2)}, u32[]{:S(2)}) collective-permute-start(bf16[4,4608]{1,0:T(4,128)(2,1)S(1)} %subtract_convert_fusion), channel_id=1, source_target_pairs={{0,4},{1,5},{2,6},{3,7},{4,0},{5,1},{6,2},{7,3},{8,12},{9,13},{10,... | collective-permute-start | bytes 110600 | tf_op jit(solution)/shard_map/ppermute | solution.py:25
  84.0 4.9 %collective-permute-start.16 = (bf16[4,4608]{1,0:T(4,128)(2,1)S(1)}, bf16[4,4608]{1,0:T(4,128)(2,1)S(1)}, u32[]{:S(2)}, u32[]{:S(2)}) collective-permute-start(bf16[4,4608]{1,0:T(4,128)(2,1)S(1)} %subtract_convert_fusion), channel_id=1, source_target_pairs={{0,2},{1,3},{2,0},{3,1},{4,6},{5,7},{6,4},{7,5},{8,10},{9,11},{10,... | collective-permute-start | bytes 110600 | tf_op jit(solution)/shard_map/ppermute | solution.py:25
  86.9 3.6 %collective-permute-start.21 = (f32[8,128]{1,0:T(8,128)S(1)}, f32[8,128]{1,0:T(8,128)S(1)}, u32[]{:S(2)}, u32[]{:S(2)}) collective-permute-start(f32[8,128]{1,0:T(8,128)S(1)} %broadcast_in_dim.40), channel_id=1, source_target_pairs={{0,8},{8,0},{16,24},{24,16},{1,9},{9,1},{17,25},{25,17},{2,10},{10... | collective-permute-start | bytes 12296 | tf_op jit(solution)/shard_map/ppermute | solution.py:25
  88.9 5.2 %collective-permute-start.19 = (bf16[16,4608]{1,0:T(8,128)(2,1)S(1)}, bf16[16,4608]{1,0:T(8,128)(2,1)S(1)}, u32[]{:S(2)}, u32[]{:S(2)}) collective-permute-start(bf16[16,4608]{1,0:T(8,128)(2,1)S(1)} %pad_maximum_fusion.1), channel_id=1, source_target_pairs={{0,16},{8,24},{16,0},{24,8},{1,17},{9,25},{17,1},{25,9},{2,18},{10... | collective-permute-start | bytes 442376 | tf_op jit(solution)/shard_map/ppermute | solution.py:25
  91.1 3.7 %collective-permute-start.22 = (f32[8,128]{1,0:T(8,128)S(1)}, f32[8,128]{1,0:T(8,128)S(1)}, u32[]{:S(2)}, u32[]{:S(2)}) collective-permute-start(f32[8,128]{1,0:T(8,128)S(1)} %broadcast_add_fusion), channel_id=1, source_target_pairs={{0,16},{8,24},{16,0},{24,8},{1,17},{9,25},{17,1},{25,9},{2,18},{10... | collective-permute-start | bytes 12296 | tf_op jit(solution)/shard_map/ppermute | solution.py:25
  94.3 14.1 %collective-permute-start.20 = (bf16[32,4608]{1,0:T(8,128)(2,1)S(1)}, bf16[32,4608]{1,0:T(8,128)(2,1)S(1)}, u32[]{:S(2)}, u32[]{:S(2)}) collective-permute-start(bf16[32,4608]{1,0:T(8,128)(2,1)S(1)} %concatenate.44), channel_id=1, source_target_pairs={{0,8},{8,0},{16,24},{24,16},{1,9},{9,1},{17,25},{25,17},{2,10},{10... | collective-permute-start | bytes 884744 | tf_op jit(solution)/shard_map/ppermute | solution.py:25
  95.5 3.7 %collective-permute-start.23 = (f32[8,128]{1,0:T(8,128)S(1)}, f32[8,128]{1,0:T(8,128)S(1)}, u32[]{:S(2)}, u32[]{:S(2)}) collective-permute-start(f32[8,128]{1,0:T(8,128)S(1)} %fusion.41), channel_id=1, source_target_pairs={{0,2},{1,3},{2,0},{3,1},{4,6},{5,7},{6,4},{7,5},{8,10},{9,11},{10,... | collective-permute-start | bytes 12296 | tf_op jit(solution)/shard_map/ppermute | solution.py:25
  99.1 4.5 %collective-permute-start.24 = (f32[8,128]{1,0:T(8,128)S(1)}, f32[8,128]{1,0:T(8,128)S(1)}, u32[]{:S(2)}, u32[]{:S(2)}) collective-permute-start(f32[8,128]{1,0:T(8,128)S(1)} %add.275), channel_id=1, source_target_pairs={{0,4},{1,5},{2,6},{3,7},{4,0},{5,1},{6,2},{7,3},{8,12},{9,13},{10,... | collective-permute-start | bytes 12296 | tf_op jit(solution)/shard_map/ppermute | solution.py:25
  103.6 3.6 %collective-permute-start.25 = (f32[8,128]{1,0:T(8,128)S(1)}, f32[8,128]{1,0:T(8,128)S(1)}, u32[]{:S(2)}, u32[]{:S(2)}) collective-permute-start(f32[8,128]{1,0:T(8,128)S(1)} %add.276), channel_id=1, source_target_pairs={{0,1},{1,0},{2,3},{3,2},{4,5},{5,4},{6,7},{7,6},{8,9},{9,8},{10,11... | collective-permute-start | bytes 12296 | tf_op jit(solution)/shard_map/ppermute | solution.py:25
  129.2 13.2 %copy-start = (bf16[64,2048]{1,0:T(8,128)(2,1)S(1)}, bf16[64,2048]{1,0:T(8,128)(2,1)}, u32[]{:S(2)}) copy-start(bf16[64,2048]{1,0:T(8,128)(2,1)} %get-tuple-element.25) | copy-start | bytes 786436

commit v2 on v0

v2 whole, which is shorter than its diff:
```python
import functools
import itertools
import math

import jax
import jax.numpy as jnp
from jax import lax
from jax.experimental import pallas as pl
from jax.experimental.pallas import tpu as pltpu
from jax.sharding import PartitionSpec as P

SPARSITY = 0.25
SMOOTHING = 0.1
EPSILON = 1e-06
F32 = jnp.float32
BF16 = jnp.bfloat16
LANES = 128
PIECES = 4


class Split:
    def __init__(self, axis, inner, size):
        self.axis, self.inner, self.size = axis, inner, size

    def place(self):
        return (lax.axis_index(self.axis) // self.inner) % self.size


class Group:
    def __init__(self, mesh, *splits):
        self.lengths = {axis: mesh.shape[axis] for axis in ("dp", "fsdp")}
        self.splits = splits
        self.size = math.prod(s.size for s in splits)
        self.keys = list(itertools.product(*(range(s.size) for s in splits)))

    def swap(self, x, key):
        pairs = []
        for d in range(self.lengths["dp"]):
            for f in range(self.lengths["fsdp"]):
                to = {"dp": d, "fsdp": f}
                for split, k in zip(self.splits, key):
                    a = (to[split.axis] // split.inner) % split.size
                    to[split.axis] += ((a ^ k) - a) * split.inner
                width = self.lengths["fsdp"]
                pairs.append((d * width + f, to["dp"] * width + to["fsdp"]))
        return lax.ppermute(x, ("dp", "fsdp"), pairs)

    def swaps(self, pieces):
        return [self.swap(p, key) for p, key in zip(pieces, self.keys[1:])]

    def spread(self, x):
        return [x] + [self.swap(x, key) for key in self.keys[1:]]


def block_of(total, most):
    return max(b for b in range(LANES, most + 1, LANES) if total % b == 0)


def resident(count):
    return [pl.BlockSpec(memory_space=pltpu.VMEM)] * count


def anywhere(count):
    return [pl.BlockSpec(memory_space=pl.ANY)] * count


def in_hbm(x):
    return pltpu.with_memory_space_constraint(x, pltpu.HBM)


def in_vmem(x):
    return pltpu.with_memory_space_constraint(x, pltpu.VMEM)


def params(megabytes):
    return pltpu.CompilerParams(vmem_limit_bytes=megabytes * 1024 * 1024)


def cost(flops, count):
    return pl.CostEstimate(flops=flops, bytes_accessed=count, transcendentals=0)


def struct(shape, kind):
    return jax.ShapeDtypeStruct(shape, kind)


def small(kernel, outs, *args, name):
    count = sum(x.size * x.dtype.itemsize for x in args) + sum(o.size * o.dtype.itemsize for o in outs)
    return pl.pallas_call(
        kernel,
        in_specs=resident(len(args)),
        out_specs=resident(len(outs)),
        out_shape=list(outs),
        compiler_params=params(6),
        cost_estimate=cost(count, count),
        name=name,
    )(*args)


def project(heads, weight, resid, gain, bias, deep, side):
    tokens = heads.shape[0]
    features = weight.shape[1]
    rows = tokens // side.size
    own = rows // deep.size
    quarter = features // deep.size
    shift = own.bit_length() - 1

    def kernel(heads, weight, resid, gain, bias, packed, gain_row, bias_row, keep, *send):
        to = lax.broadcasted_iota(jnp.int32, (tokens, tokens), 0)
        source = lax.broadcasted_iota(jnp.int32, (tokens, tokens), 1)
        across = lax.shift_right_logical(to, (rows.bit_length() - 1)) ^ side.place()
        down = (lax.shift_right_logical(to, shift) & (deep.size - 1)) ^ deep.place()
        wanted = (down * side.size + across) * own + (to & (own - 1))
        pick = jnp.where(source == wanted, 1.0, 0.0).astype(BF16)
        turned = jnp.dot(pick, heads[...], preferred_element_type=F32).astype(BF16)
        part = jnp.dot(turned, weight[...], preferred_element_type=F32)
        keep[...] = part[:rows]
        for k in range(1, side.size):
            send[k - 1][...] = part[k * rows : (k + 1) * rows].astype(BF16)

        @pl.when(pl.program_id(0) == 0)
        def _():
            values = resid[...].astype(F32)
            pieces = [values[:, q * quarter : (q + 1) * quarter] for q in range(deep.size)]
            packed[...] = jnp.concatenate(pieces, axis=0).astype(BF16)
            gain_row[...] = gain[...].reshape(1, features)
            bias_row[...] = bias[...].reshape(1, features)

    wide = block_of(features, 1536)
    fixed = lambda shape: pl.BlockSpec(shape, lambda i: (0,) * len(shape))
    spec = pl.BlockSpec((rows, wide), lambda i: (0, i))
    return pl.pallas_call(
        kernel,
        grid=(features // wide,),
        in_specs=[
            fixed(heads.shape),
            pl.BlockSpec((weight.shape[0], wide), lambda i: (0, i)),
            fixed(resid.shape),
            fixed(gain.shape),
            fixed(bias.shape),
        ],
        out_specs=[fixed((rows, quarter)), fixed((1, features)), fixed((1, features))] + [spec] * side.size,
        out_shape=[struct((rows, quarter), BF16), struct((1, features), F32), struct((1, features), F32)]
        + [struct((rows, features), F32)]
        + [struct((rows, features), BF16)] * (side.size - 1),
        compiler_params=params(12),
        cost_estimate=cost(2 * tokens * weight.size, 2 * weight.size),
        name="project",
    )(in_hbm(heads), in_hbm(weight), in_hbm(resid), in_hbm(gain), in_hbm(bias))


def add_up(keep, got, parts, kind, name, beside=None, after=()):
    rows, columns = keep.shape
    part = rows // parts
    extra = [] if beside is None else [beside]
    width = columns + sum(b.shape[1] for b in extra)

    def kernel(*refs):
        ins, outs = refs[: 1 + len(got)], refs[-parts:]
        for p in range(parts):
            at = slice(p * part, (p + 1) * part)
            total = ins[0][at, :]
            for g in ins[1:]:
                total = total + g[at, :].astype(F32)
            outs[p][:, :columns] = total.astype(outs[p].dtype)
        if extra:
            outs[0][:, columns:] = refs[1 + len(got)][...]

    outs = [struct((part, width), kind)] + [struct((part, columns), BF16)] * (parts - 1)
    return small(kernel, outs, keep, *got, *extra, *after, name=name)


def group_sum(parts, own):
    size = len(parts)
    terms = []
    for k, part in enumerate(parts):
        pieces = [part[(j ^ k) * own : ((j ^ k) + 1) * own, :] for j in range(size)]
        terms.append(jnp.concatenate(pieces, axis=0) if size > 1 else part)
    while len(terms) > 1:
        half = len(terms) // 2
        terms = [terms[i] + terms[i + half] for i in range(half)]
    return terms[0]


def residual(parts, gain, after):
    rows = parts[0].shape[0]
    features = gain.shape[1]
    count = len(parts)
    own, quarter = rows // count, features // count

    def kernel(*refs):
        sums, gain, out = refs[:count], refs[count], refs[-1]
        projected = group_sum([p[:, :features].astype(F32) for p in sums], own)
        scale = lax.rsqrt(jnp.mean(projected * projected, axis=-1, keepdims=True) + EPSILON)
        packed = [p[:, features:].astype(F32) for p in sums]
        for q in range(count):
            at = slice(q * quarter, (q + 1) * quarter)
            before = jnp.concatenate([p[q * own : (q + 1) * own, :] for p in packed], axis=0)
            out[:, at] = (before + projected[:, at] * scale * gain[:, at]).astype(BF16)

    return small(kernel, [struct((rows, features), BF16)], *parts, gain, *after, name="residual")[0]


def error_of(parts, resid, bias):
    rows, columns = parts[0].shape
    features = resid.shape[1]
    own = rows // len(parts)

    def kernel(*refs):
        sums, resid, bias, out = refs[: len(parts)], refs[-3], refs[-2], refs[-1]
        total = group_sum([p[...].astype(F32) for p in sums], own)
        out[:, :features] = (total[:, :features] + bias[...] - resid[...].astype(F32)).astype(BF16)
        out[:, features:] = total[:, features:].astype(BF16)

    return small(kernel, [struct((rows, columns), BF16)], *parts, resid, bias, name="error")[0]


def stack(pieces, name):
    rows, columns = pieces[0].shape

    def kernel(*refs):
        for i, ref in enumerate(refs[:-1]):
            refs[-1][i * rows : (i + 1) * rows, :] = ref[...]

    return small(kernel, [struct((rows * len(pieces), columns), pieces[0].dtype)], *pieces, name=name)[0]


def gather(stages, x):
    pieces = [x]
    for group in reversed(stages):
        if len(pieces) > 4:
            pieces = [stack(pieces, "gathered")]
        pieces = pieces + [group.swap(p, key) for key in group.keys[1:] for p in pieces]
    return pieces


def load(items, after, name):
    chunks = []
    for n, (_, first, rows, _) in enumerate(items):
        step = block_of(rows, 384) if rows % LANES == 0 else rows
        chunks += [(n, first + r, r, step) for r in range(0, rows, step)]
    outs, places = [], []
    for source, _, rows, norms in items:
        places.append(len(outs))
        outs.append(pltpu.VMEM((rows, source.shape[1]), source.dtype))
        if norms:
            outs += [struct((rows, 1), F32), struct((1, rows), F32)]
    outs.append(struct((8, LANES), F32))

    def kernel(*refs):
        sources, results, sems = refs[: len(items)], refs[len(items) + 1 : -1], refs[-1]
        copies = []
        for i, (n, at, to, step) in enumerate(chunks):
            copies.append(
                pltpu.make_async_copy(
                    sources[n].at[pl.ds(at, step)], results[places[n]].at[pl.ds(to, step)], sems.at[i]
                )
            )
            copies[-1].start()
        for copy, (n, _, to, step) in zip(copies, chunks):
            copy.wait()
            if items[n][3]:
                row_norms(*results[places[n] : places[n] + 3], to, step)
        results[-1][...] = jnp.zeros_like(results[-1])

    found = pl.pallas_call(
        kernel,
        in_specs=anywhere(len(items)) + resident(1),
        out_specs=resident(len(outs)),
        out_shape=outs,
        scratch_shapes=[pltpu.SemaphoreType.DMA((len(chunks),))],
        compiler_params=params(4),
        cost_estimate=cost(0, sum(2 * rows * source.shape[1] for source, _, rows, _ in items)),
        name=name,
    )(*[in_hbm(item[0]) for item in items], after)
    return found


def row_norms(weight, norm, norm_row, first, rows):
    features = weight.shape[1]
    at = slice(first, first + rows)
    squares = jnp.zeros((rows, LANES), F32)
    for c in range(0, features, LANES):
        w = weight[at, c : c + LANES].astype(F32)
        squares = squares + w * w
    value = jnp.sqrt(jnp.sum(squares, axis=1, keepdims=True) + EPSILON)
    norm[at, :] = value
    norm_row[:, at] = jnp.broadcast_to(value, (rows, LANES)).T[:1, :]


def encode(parts, early, weight, bias):
    rows = parts[0].shape[0]
    tokens = sum(p.shape[0] for p in parts)
    features, latents = weight.shape
    depth = features // PIECES
    late = PIECES - len(early)
    wide = block_of(latents, 256)

    def kernel(*refs):
        parts_in, early_in = refs[: len(parts)], refs[len(parts) : len(parts) + len(early)]
        weight, bias, preact, resid, held, sems = refs[len(parts) + len(early) :]
        copies = []
        for i in range(late):
            at = pl.ds((len(early) + i) * depth, depth)
            copies.append(pltpu.make_async_copy(weight.at[at], held.at[i], sems.at[i]))
            copies[-1].start()
        for i, part in enumerate(parts_in):
            resid[i * rows : (i + 1) * rows, :] = part[...]
        row = bias[...].reshape(1, latents)
        for c in range(0, latents, wide):
            at = slice(c, c + wide)
            total = row[:, at]
            for i, w in enumerate(early_in):
                total = total + jnp.dot(
                    resid[:, i * depth : (i + 1) * depth], w[:, at], preferred_element_type=F32
                )
            preact[:, at] = jnp.broadcast_to(total, (tokens, wide))
        for i, copy in enumerate(copies):
            copy.wait()
            k = len(early) + i
            for c in range(0, latents, wide):
                at = slice(c, c + wide)
                preact[:, at] += jnp.dot(
                    resid[:, k * depth : (k + 1) * depth], held[i, :, at], preferred_element_type=F32
                )

    return pl.pallas_call(
        kernel,
        in_specs=resident(len(parts) + len(early)) + anywhere(1) + resident(1),
        out_specs=resident(2),
        out_shape=[struct((tokens, latents), F32), struct((tokens, features), BF16)],
        scratch_shapes=[pltpu.VMEM((max(late, 1), depth, latents), BF16), pltpu.SemaphoreType.DMA((max(late, 1),))],
        compiler_params=params(18),
        cost_estimate=cost(2 * tokens * features * latents, 2 * tokens * features),
        name="encode",
    )(*parts, *[in_vmem(e) for e in early], in_hbm(weight), bias)


def decode_kernel(count, preact, *refs):
    weights, norm_cols, norm_rows = refs[:count], refs[count : 2 * count], refs[2 * count : 3 * count]
    keep, send, latents_t, coef, latents_b = refs[3 * count :]
    tokens = preact.shape[0]
    features = weights[0].shape[1]
    half = keep.shape[0]
    penalty = jnp.zeros((tokens, 1), F32)
    spans, start = [], 0
    for p in range(count):
        piece = weights[p].shape[0]
        spans.append(slice(start, start + piece))
        rows = block_of(piece, 256) if piece % LANES == 0 else piece
        for r in range(0, piece, rows):
            at, inside = slice(start + r, start + r + rows), slice(r, r + rows)
            latents = jnp.maximum(preact[:, at], 0.0)
            latents_b[:, at] = latents.astype(BF16)
            turned = latents.T
            latents_t[at, :] = turned.astype(BF16)
            coef[at, :] = SPARSITY * (jnp.sum(turned, axis=1, keepdims=True) / norm_cols[p][inside, :])
            penalty = penalty + jnp.sum(latents * norm_rows[p][:, inside], axis=1, keepdims=True)
        start += piece
    keep[:, features:] = jnp.broadcast_to(penalty[:half], (half, LANES))
    if half < tokens:
        send[:, features:] = jnp.broadcast_to(penalty[half:], (tokens - half, LANES)).astype(BF16)
    wide = block_of(features, 512)
    for c in range(0, features, wide):
        at = slice(c, c + wide)
        part = jnp.dot(latents_b[:, spans[0]], weights[0][:, at], preferred_element_type=F32)
        for p in range(1, count):
            part = part + jnp.dot(latents_b[:, spans[p]], weights[p][:, at], preferred_element_type=F32)
        keep[:, at] = part[:half]
        if half < tokens:
            send[:, at] = part[half:].astype(BF16)


def decode(preact, weights, norm_cols, norm_rows, parts):
    tokens, latents = preact.shape
    features = weights[0].shape[1]
    kept = tokens // parts
    sent = max(tokens - kept, 8)
    return pl.pallas_call(
        functools.partial(decode_kernel, len(weights)),
        in_specs=resident(1 + 3 * len(weights)),
        out_specs=resident(4),
        out_shape=[
            struct((kept, features + LANES), F32),
            struct((sent, features + LANES), BF16),
            struct((latents, tokens), BF16),
            struct((latents, 1), F32),
        ],
        scratch_shapes=[pltpu.VMEM((tokens, latents), BF16)],
        compiler_params=params(12),
        cost_estimate=cost(2 * tokens * features * latents, 6 * tokens * features),
        name="decode",
    )(preact, *[in_vmem(w) for w in weights], *norm_cols, *norm_rows)


def turn(x, after):
    def kernel(x, after, out):
        out[...] = x[...].astype(F32).T.astype(BF16)

    return small(kernel, [struct(x.shape[::-1], BF16)], x, after, name="turn")[0]


def fold(x):
    n = x.shape[0]
    while n > 1 and n % 2 == 0:
        n //= 2
        x = x[:n] + x[n:]
    return x if n == 1 else jnp.sum(x, axis=0, keepdims=True)


def grad_kernel(pieces, count, *refs):
    parts, weights, norm_rows = refs[:pieces], refs[pieces : pieces + count], refs[pieces + count : pieces + 2 * count]
    (resid_t, preact, latents_t, coef, dec_grad, enc_grad, bias_grad, column_sum, loss,
     error, error_t, dec_stage, enc_stage, dec_sem, enc_sem) = refs[pieces + 2 * count :]
    height = parts[0].shape[0]
    for i, part in enumerate(parts):
        error[i * height : (i + 1) * height, :] = part[...]
    tokens = error.shape[0]
    latents = latents_t.shape[0]
    features = weights[0].shape[1]
    dec_slots, rows = dec_stage.shape[:2]
    enc_slots, deep, span = enc_stage.shape
    wide = block_of(features, 512)
    where = [(p, r) for p in range(count) for r in range(0, weights[p].shape[0], rows)]
    dec_copies, enc_copies = [], []

    def outer(i):
        p, r = where[i]
        at, inside = slice(i * rows, (i + 1) * rows), slice(r, r + rows)
        if i >= dec_slots:
            dec_copies[i - dec_slots].wait()
        slot = i % dec_slots
        scale = coef[at, :]
        for c in range(0, features, wide):
            over = slice(c, c + wide)
            product = jnp.dot(latents_t[at, :], error[:, over], preferred_element_type=F32)
            product = product + scale * weights[p][inside, over].astype(F32)
            dec_stage[slot, :, over] = product.astype(BF16)
        copy = pltpu.make_async_copy(dec_stage.at[slot], dec_grad.at[pl.ds(i * rows, rows)], dec_sem.at[slot])
        copy.start()
        dec_copies.append(copy)

    def pull(i):
        p, r = where[i]
        at, inside = slice(i * rows, (i + 1) * rows), slice(r, r + rows)
        back = jnp.dot(weights[p][inside, :], error_t[...], preferred_element_type=F32).T
        back = (back + SPARSITY * norm_rows[p][:, inside]) * jax.nn.sigmoid(preact[:, at] / SMOOTHING)
        bias_grad[:, at] = jnp.sum(back, axis=0, keepdims=True)
        return back.astype(BF16)

    def spread(first, pulled):
        for j in range(0, features, deep):
            n = len(enc_copies)
            if n >= enc_slots:
                enc_copies[n - enc_slots].wait()
            slot = n % enc_slots
            enc_stage[slot] = jnp.dot(resid_t[j : j + deep, :], pulled, preferred_element_type=F32).astype(BF16)
            copy = pltpu.make_async_copy(
                enc_stage.at[slot], enc_grad.at[pl.ds(j, deep), pl.ds(first, span)], enc_sem.at[slot]
            )
            copy.start()
            enc_copies.append(copy)

    outer(0)
    error_t[...] = error[:, :features].astype(F32).T.astype(BF16)
    each = span // rows
    for i in range(0, latents // rows, each):
        pulled = []
        for k in range(i, i + each):
            if k:
                outer(k)
            pulled.append(pull(k))
        spread(i * rows, jnp.concatenate(pulled, axis=1) if each > 1 else pulled[0])

    squares = jnp.zeros((1, wide), F32)
    for c in range(0, features, wide):
        e = error[:, c : c + wide].astype(F32)
        column_sum[:, c : c + wide] = fold(e)
        squares = squares + fold(e * e)
    squared = jnp.sum(squares, axis=1, keepdims=True)
    penalty = fold(error[:, features:].astype(F32))
    loss[...] = (0.5 * squared + SPARSITY * penalty) / (tokens * features)
    for copy in dec_copies[-dec_slots:] + enc_copies[-enc_slots:]:
        copy.wait()


def gradients(parts, resid_t, preact, latents_t, coef, weights, norm_rows):
    tokens, latents = preact.shape
    features = weights[0].shape[1]
    rows = math.gcd(*[w.shape[0] for w in weights], 256)
    span = math.gcd(latents, 512)
    deep = block_of(features, 1152)
    return pl.pallas_call(
        functools.partial(grad_kernel, len(parts), len(weights)),
        in_specs=resident(len(parts) + 2 * len(weights) + 4),
        out_specs=anywhere(2) + resident(3),
        out_shape=[
            struct((latents, features), BF16),
            struct((features, latents), BF16),
            struct((1, latents), F32),
            struct((1, features), F32),
            struct((1, LANES), F32),
        ],
        scratch_shapes=[
            pltpu.VMEM((tokens, features + LANES), BF16),
            pltpu.VMEM((features, tokens), BF16),
            pltpu.VMEM((3, rows, features), BF16),
            pltpu.VMEM((4, deep, span), BF16),
            pltpu.SemaphoreType.DMA((3,)),
            pltpu.SemaphoreType.DMA((4,)),
        ],
        compiler_params=params(24),
        cost_estimate=cost(6 * tokens * features * latents, 4 * features * latents),
        name="gradients",
    )(*parts, *[in_vmem(w) for w in weights], *norm_rows, resid_t, preact, latents_t, coef)


def make_body(mesh):
    dp, fsdp = mesh.shape["dp"], mesh.shape["fsdp"]
    cores = 2 if dp % 2 == 0 else 1
    depth = 4 if fsdp % 4 == 0 else 1
    core_split, across_split = Split("dp", 1, cores), Split("dp", cores, dp // cores)
    deep_split, side_split = Split("fsdp", fsdp // depth, depth), Split("fsdp", 1, fsdp // depth)
    core, deep, side = Group(mesh, core_split), Group(mesh, deep_split), Group(mesh, side_split)
    if across_split.size * side_split.size <= 4:
        plane = [Group(mesh, across_split, side_split)]
    else:
        plane = [Group(mesh, across_split), side]
    stages = [core] + plane

    def body(attn_heads, out_proj, resid_pre, post_gain, enc_weight, enc_bias, dec_weight, dec_bias):
        latents, depth = dec_weight.shape[0], dec_weight.shape[1] // PIECES
        unit = 256 if latents % 2048 == 0 else LANES
        cut = max(latents // unit * 3 // 8, 1) * unit
        packed, gain, bias, keep, *send = project(
            attn_heads, out_proj, resid_pre, post_gain, dec_bias, deep_split, side_split
        )
        got = side.swaps(send)
        first = load([(dec_weight, 0, cut, True)], send[0] if send else keep, "load_first")
        summed = add_up(keep, got, 1, BF16, "heads_y", packed, first[-1:])[0]
        sums = deep.spread(summed)
        second = load(
            [(dec_weight, cut, latents - cut, True), (enc_weight, 0, depth, False)], summed, "load_second"
        )
        resid_own = residual(sums, gain, second[-1:])
        resid_parts = gather(stages, resid_own)
        third = load([(enc_weight, depth, depth, False)], resid_own, "load_third")
        early = [second[3], third[0]]
        held, norm_cols, norm_rows = [list(pair) for pair in zip(first[:3], second[:3])]

        preact, resid_all = encode(resid_parts, early, enc_weight, enc_bias)
        keep, send, latents_t, coef = decode(preact, held, norm_cols, norm_rows, core.size)
        send = [send]
        for i, group in enumerate(stages):
            last = i + 1 == len(stages)
            parts = 1 if last else stages[i + 1].size
            got = group.swaps(send)
            after = []
            if last:
                resid_t = turn(resid_all, send[0])
                after = [resid_t]
            keep, *send = add_up(keep, got, parts, BF16 if last else F32, "recon", None, after)
        error_own = error_of(deep.spread(keep), resid_own, bias)
        error_parts = gather(stages, error_own)

        dec_grad, enc_grad, bias_grad, column_sum, loss = gradients(
            error_parts, resid_t, preact, latents_t, coef, held, norm_rows
        )
        return (enc_grad, bias_grad.reshape(-1), dec_grad, column_sum.reshape(-1), loss[0, 0])

    return body


def solution(mesh):
    placed = (
        P("dp", "fsdp"),
        P("fsdp", None),
        P(("dp", "fsdp"), None),
        P(),
        P(None, ("dp", "fsdp")),
        P(("dp", "fsdp")),
        P(("dp", "fsdp"), None),
        P(),
    )
    return jax.shard_map(
        make_body(mesh),
        mesh=mesh,
        in_specs=placed,
        out_specs=(P(None, ("dp", "fsdp")), P(("dp", "fsdp")), P(("dp", "fsdp"), None), P(), P()),
        check_vma=False,
    )
```

time: 459 us -> 90.6 us (0.20)
  waiting for transfers between devices: 194 us -> 18 us
  blocking collectives: 174 us -> 0 us
  matrix products: 58.7 us -> 0 us
  Pallas kernels: 0 us -> 47 us
  starting transfers between devices: 0.08 us -> 24.1 us
  between operations: 17.3 us -> 0.79 us
  other arithmetic: 12.5 us -> 0.65 us
    unnamed x4 -> x0, waiting for transfers between devices: 194 us -> none
    all_gather x2 -> x0, blocking collectives: 137 us -> none  [the longest x1 68.8 us: body(): error_all = lax.all_gather(error_b, ('dp', 'fsdp'), axis=0, tiled=True)]
    dot_general x6 -> x0, matrix products: 58.7 us -> none  [the longest x1 13.2 us: body(): lax.dot_general(latents_b, error_all, (((0,), (0,)), ((), ())), preferred...]
    pallas_call x0 -> x13, Pallas kernels: none -> 47 us  [the longest x1 21.2 us: gradients(): pl.pallas_call(functools.partial(grad_kernel, len(parts), len(weights)),...]
    psum x1 -> x0, blocking collectives: 37.1 us -> none  [body(): error_total = lax.psum(error_local, ('dp', 'fsdp'))]
    ppermute x0 -> x25, starting transfers between devices: none -> 24.1 us  [swap(): return lax.ppermute(x, ('dp', 'fsdp'), pairs)]
    ppermute x0 -> x25, waiting for transfers between devices: none -> 18 us  [swap(): return lax.ppermute(x, ('dp', 'fsdp'), pairs)]
    reduce_sum x4 -> x0, other arithmetic: 11.4 us -> none  [the longest x1 8.03 us: body(): jnp.sum(jnp.square(dec_weight.astype(jnp.float32)), axis=1) + EPSILON]
  transfers between devices with their start and end apart: 2 -> 25, of which waited for: 2 -> 15; matrix products, arithmetic and copies ran while one was open for 2% -> 0% of each run, Pallas kernels for 0% -> 14%
where the time goes in v2:
time: 90.6 us; the launch traced here: 90.5 us
  Pallas kernels  47 us (52%)
  starting transfers between devices  24.1 us (27%)
  waiting for transfers between devices  18 us (20%)
    ppermute x25, starting transfers between devices, swap(): return lax.ppermute(x, ('dp', 'fsdp'), pairs)  24.1 us
    pallas_call x1, Pallas kernels, gradients(): pl.pallas_call(functools.partial(grad_kernel, len(parts), len(weights)),...  21.2 us
    ppermute x25, waiting for transfers between devices, swap(): return lax.ppermute(x, ('dp', 'fsdp'), pairs)  18 us
    pallas_call x3, Pallas kernels, load(): pl.pallas_call(kernel, in_specs=anywhere(len(items)) + resident(1), out_s...  12.7 us
    pallas_call x1, Pallas kernels, encode(): pl.pallas_call(kernel, in_specs=resident(len(parts) + len(early)) + anywh...  5.04 us
    pallas_call x1, Pallas kernels, project(): pl.pallas_call(kernel, grid=(features // wide,), in_specs=[fixed(heads.sh...  3.71 us
    pallas_call x1, Pallas kernels, decode(): pl.pallas_call(functools.partial(decode_kernel, len(weights)), in_specs=r...  3.45 us
  transfers between devices with their start and end apart: 25, of which 15 were waited for; matrix products, arithmetic and copies ran while one was open for 0% of the time, Pallas kernels for 14%

profile of v2, /device:TPU:0, one launch (start us, length us, event | category | flops | bytes accessed | tf_op | source)
XLA Modules:
  0.0 90.5 jit_solution(10154658987326135680)
XLA Ops:
  0.6 3.7 %project.1 = (bf16[8,1152]{1,0:T(8,128)(2,1)S(1)}, f32[1,4608]{1,0:T(1,128)S(1)}, f32[1,4608]{1,0:T(1,128)S(1)}, f32[8,4608]{1,0:T(8,128)S(1)}, bf16[8,4608]{1,0:T(8,128)(2,1)S(1)}) custom-call(bf16[16,512]{1,0:T(8,128)(2,1)} %heads.1, bf16[512,4608]{1,0:T(8,128)(2,1)} %weight.1, bf16[2,4608]{1,0:T(2,128)(2,1)} %resid.1, f32[4608]{0:T(1024)} %gain.1, f32[4608]{0:T(1024)} %bias.1), custom_call_target="tpu_custom_call" | custom-call | flops 75497472 | bytes 4718592 | tf_op jit(solution)/shard_map/project/pallas_call | solution.py:132
  4.3 3.0 %collective-permute-start = (bf16[8,4608]{1,0:T(8,128)(2,1)S(1)}, bf16[8,4608]{1,0:T(8,128)(2,1)S(1)}, u32[]{:S(2)}, u32[]{:S(2)}) collective-permute-start(bf16[8,4608]{1,0:T(8,128)(2,1)S(1)} %get-tuple-element.36.refs_1_), channel_id=1, source_target_pairs={{0,1},{1,0},{2,3},{3,2},{4,5},{5,4},{6,7},{7,6},{8,9},{9,8},{10,11... | collective-permute-start | bytes 221192 | tf_op jit(solution)/shard_map/ppermute | solution.py:46
  7.3 3.9 %load_first.1 = (bf16[768,4608]{1,0:T(8,128)(2,1)S(1)}, f32[768,1]{1,0:T(8,128)S(1)}, f32[1,768]{1,0:T(1,128)S(1)}, f32[8,128]{1,0:T(8,128)S(1)}) custom-call(bf16[2048,4608]{1,0:T(8,128)(2,1)} %refs_0_.4, bf16[8,4608]{1,0:T(8,128)(2,1)S(1)} %get-tuple-element.36.refs_1_), custom_call_target="tpu_custom_call" | custom-call | bytes 7077888 | tf_op jit(solution)/shard_map/load_first/pallas_call | solution.py:266
  11.3 0.0 collective-permute-done.refs_1_
  11.3 3.7 %collective-permute-start.3 = (bf16[8,5760]{1,0:T(8,128)(2,1)S(1)}, bf16[8,5760]{1,0:T(8,128)(2,1)S(1)}, u32[]{:S(2)}, u32[]{:S(2)}) collective-permute-start(bf16[8,5760]{1,0:T(8,128)(2,1)S(1)} %heads_y.1.refs_2_.refs_0_), channel_id=1, source_target_pairs={{0,6},{1,7},{2,4},{3,5},{4,2},{5,3},{6,0},{7,1},{8,14},{9,15},{10,... | collective-permute-start | bytes 276488 | tf_op jit(solution)/shard_map/ppermute | solution.py:46
  15.0 0.0 collective-permute-start.2
  15.0 0.8 collective-permute-start.1
  15.7 5.8 %load_second.1 = (bf16[1280,4608]{1,0:T(8,128)(2,1)S(1)}, f32[1280,1]{1,0:T(8,128)S(1)}, f32[1,1280]{1,0:T(1,128)S(1)}, bf16[1152,2048]{1,0:T(8,128)(2,1)S(1)}, f32[8,128]{1,0:T(8,128)S(1)}) custom-call(bf16[2048,4608]{1,0:T(8,128)(2,1)} %refs_0_.4, bf16[4608,2048]{1,0:T(8,128)(2,1)} %refs_10_.1, bf16[8,5760]{1,0:T(8,128)(2,1)S(1)} %heads_y.1.refs_2_.refs_0_), custom_call_target="tpu_custom_call" | custom-call | bytes 16515072 | tf_op jit(solution)/shard_map/load_second/pallas_call | solution.py:266
  21.6 0.0 copy-start
  21.6 0.8 collective-permute-done.2.refs_2_
  22.4 0.2 residual.1.refs_1_.refs_0_.refs_4_
  22.7 1.5 %collective-permute-start.6 = (bf16[8,4608]{1,0:T(8,128)(2,1)S(1)}, bf16[8,4608]{1,0:T(8,128)(2,1)S(1)}, u32[]{:S(2)}, u32[]{:S(2)}) collective-permute-start(bf16[8,4608]{1,0:T(8,128)(2,1)S(1)} %residual.1.refs_1_.refs_0_.refs_4_), channel_id=1, source_target_pairs={{0,17},{1,16},{2,19},{3,18},{4,21},{5,20},{6,23},{7,22},{8,25},{9,... | collective-permute-start | bytes 221192 | tf_op jit(solution)/shard_map/ppermute | solution.py:46
  24.2 0.5 collective-permute-start.5
  24.7 1.5 %collective-permute-start.4 = (bf16[8,4608]{1,0:T(8,128)(2,1)S(1)}, bf16[8,4608]{1,0:T(8,128)(2,1)S(1)}, u32[]{:S(2)}, u32[]{:S(2)}) collective-permute-start(bf16[8,4608]{1,0:T(8,128)(2,1)S(1)} %residual.1.refs_1_.refs_0_.refs_4_), channel_id=1, source_target_pairs={{0,1},{1,0},{2,3},{3,2},{4,5},{5,4},{6,7},{7,6},{8,9},{9,8},{10,11... | collective-permute-start | bytes 221192 | tf_op jit(solution)/shard_map/ppermute | solution.py:46
  26.2 2.2 %collective-permute-done.6.refs_3_ = bf16[8,4608]{1,0:T(8,128)(2,1)S(1)} collective-permute-done((bf16[8,4608]{1,0:T(8,128)(2,1)S(1)}, bf16[8,4608]{1,0:T(8,128)(2,1)S(1)}, u32[]{:S(2)}, u32[]{:S(2)}) %collective-permute-start.6) | collective-permute-done | bytes 73760 | tf_op jit(solution)/shard_map/ppermute | solution.py:46
  28.4 0.0 collective-permute-start.10
  28.4 0.1 collective-permute-done.5.refs_2_
  28.5 0.4 collective-permute-start.9
  28.9 0.3 collective-permute-done.4.refs_1_
  29.2 3.0 %load_third.1 = (bf16[1152,2048]{1,0:T(8,128)(2,1)S(1)}, f32[8,128]{1,0:T(8,128)}) custom-call(bf16[4608,2048]{1,0:T(8,128)(2,1)} %refs_10_.1, bf16[8,4608]{1,0:T(8,128)(2,1)S(1)} %residual.1.refs_1_.refs_0_.refs_4_), custom_call_target="tpu_custom_call" | custom-call | bytes 4718592 | tf_op jit(solution)/shard_map/load_third/pallas_call | solution.py:266
  32.2 5.0 %encode.1 = (f32[64,2048]{1,0:T(8,128)S(1)}, bf16[64,4608]{1,0:T(8,128)(2,1)S(1)}) custom-call(bf16[8,4608]{1,0:T(8,128)(2,1)S(1)} %residual.1.refs_1_.refs_0_.refs_4_, bf16[8,4608]{1,0:T(8,128)(2,1)S(1)} %collective-permute-done.4.refs_1_, bf16[8,4608]{1,0:T(8,128)(2,1)S(1)} %collective-permute-done.5.refs_2_, ...), custom_call_target="tpu_custom_call" | custom-call | flops 1207959552 | bytes 589824 | tf_op jit(solution)/shard_map/encode/pallas_call | solution.py:327
  37.3 3.4 %decode.1 = (f32[32,4736]{1,0:T(8,128)S(1)}, bf16[32,4736]{1,0:T(8,128)(2,1)S(1)}, bf16[2048,64]{1,0:T(8,128)(2,1)S(1)}, f32[2048,1]{1,0:T(8,128)S(1)}) custom-call(f32[64,2048]{1,0:T(8,128)S(1)} %get-tuple-element.43.preact.refs_13_, bf16[768,4608]{1,0:T(8,128)(2,1)S(1)} %get-tuple-element.44.refs_0_.refs_8_, ...), custom_call_target="tpu_custom_call" | custom-call | flops 1207959552 | bytes 1769472 | tf_op jit(solution)/shard_map/decode/pallas_call | solution.py:379
  40.7 0.6 collective-permute-start.11
  41.3 1.2 %collective-permute-done.11.refs_1_ = bf16[32,4736]{1,0:T(8,128)(2,1)S(1)} collective-permute-done((bf16[32,4736]{1,0:T(8,128)(2,1)S(1)}, bf16[32,4736]{1,0:T(8,128)(2,1)S(1)}, u32[]{:S(2)}, u32[]{:S(2)}) %collective-permute-start.11) | collective-permute-done | bytes 303136 | tf_op jit(solution)/shard_map/ppermute | solution.py:46
  42.5 0.1 recon.2
  42.6 1.4 %collective-permute-start.13 = (bf16[8,4736]{1,0:T(8,128)(2,1)S(1)}, bf16[8,4736]{1,0:T(8,128)(2,1)S(1)}, u32[]{:S(2)}, u32[]{:S(2)}) collective-permute-start(bf16[8,4736]{1,0:T(8,128)(2,1)S(1)} %get-tuple-element.54), channel_id=1, source_target_pairs={{0,16},{1,17},{2,18},{3,19},{4,20},{5,21},{6,22},{7,23},{8,24},{9,... | collective-permute-start | bytes 227336 | tf_op jit(solution)/shard_map/ppermute | solution.py:46
  44.0 1.5 %collective-permute-start.14 = (bf16[8,4736]{1,0:T(8,128)(2,1)S(1)}, bf16[8,4736]{1,0:T(8,128)(2,1)S(1)}, u32[]{:S(2)}, u32[]{:S(2)}) collective-permute-start(bf16[8,4736]{1,0:T(8,128)(2,1)S(1)} %get-tuple-element.55), channel_id=1, source_target_pairs={{0,17},{1,16},{2,19},{3,18},{4,21},{5,20},{6,23},{7,22},{8,25},{9,... | collective-permute-start | bytes 227336 | tf_op jit(solution)/shard_map/ppermute | solution.py:46
  45.5 0.7 collective-permute-start.12
  46.2 0.4 turn.1.refs_4_.refs_12_
  46.6 0.7 collective-permute-done.13.refs_2_
  47.3 2.5 %collective-permute-done.14.refs_3_ = bf16[8,4736]{1,0:T(8,128)(2,1)S(1)} collective-permute-done((bf16[8,4736]{1,0:T(8,128)(2,1)S(1)}, bf16[8,4736]{1,0:T(8,128)(2,1)S(1)}, u32[]{:S(2)}, u32[]{:S(2)}) %collective-permute-start.14) | collective-permute-done | bytes 75808 | tf_op jit(solution)/shard_map/ppermute | solution.py:46
  49.8 1.2 %collective-permute-done.12.refs_1_ = bf16[8,4736]{1,0:T(8,128)(2,1)S(1)} collective-permute-done((bf16[8,4736]{1,0:T(8,128)(2,1)S(1)}, bf16[8,4736]{1,0:T(8,128)(2,1)S(1)}, u32[]{:S(2)}, u32[]{:S(2)}) %collective-permute-start.12) | collective-permute-done | bytes 75808 | tf_op jit(solution)/shard_map/ppermute | solution.py:46
  51.0 2.9 %collective-permute-start.17 = (bf16[8,4736]{1,0:T(8,128)(2,1)S(1)}, bf16[8,4736]{1,0:T(8,128)(2,1)S(1)}, u32[]{:S(2)}, u32[]{:S(2)}) collective-permute-start(bf16[8,4736]{1,0:T(8,128)(2,1)S(1)} %recon.3.refs_0_), channel_id=1, source_target_pairs={{0,6},{1,7},{2,4},{3,5},{4,2},{5,3},{6,0},{7,1},{8,14},{9,15},{10,... | collective-permute-start | bytes 227336 | tf_op jit(solution)/shard_map/ppermute | solution.py:46
  53.9 1.6 %collective-permute-start.15 = (bf16[8,4736]{1,0:T(8,128)(2,1)S(1)}, bf16[8,4736]{1,0:T(8,128)(2,1)S(1)}, u32[]{:S(2)}, u32[]{:S(2)}) collective-permute-start(bf16[8,4736]{1,0:T(8,128)(2,1)S(1)} %recon.3.refs_0_), channel_id=1, source_target_pairs={{0,2},{1,3},{2,0},{3,1},{4,6},{5,7},{6,4},{7,5},{8,10},{9,11},{10,... | collective-permute-start | bytes 227336 | tf_op jit(solution)/shard_map/ppermute | solution.py:46
  55.5 2.2 %collective-permute-done.17.refs_3_ = bf16[8,4736]{1,0:T(8,128)(2,1)S(1)} collective-permute-done((bf16[8,4736]{1,0:T(8,128)(2,1)S(1)}, bf16[8,4736]{1,0:T(8,128)(2,1)S(1)}, u32[]{:S(2)}, u32[]{:S(2)}) %collective-permute-start.17) | collective-permute-done | bytes 75808 | tf_op jit(solution)/shard_map/ppermute | solution.py:46
  57.7 2.7 %collective-permute-done.16.refs_2_ = bf16[8,4736]{1,0:T(8,128)(2,1)S(1)} collective-permute-done((bf16[8,4736]{1,0:T(8,128)(2,1)S(1)}, bf16[8,4736]{1,0:T(8,128)(2,1)S(1)}, u32[]{:S(2)}, u32[]{:S(2)}) %collective-permute-start.16) | collective-permute-done | bytes 75808 | tf_op jit(solution)/shard_map/ppermute | solution.py:46
  60.5 0.1 error.1.refs_0_
  60.6 1.5 %collective-permute-start.20 = (bf16[8,4736]{1,0:T(8,128)(2,1)S(1)}, bf16[8,4736]{1,0:T(8,128)(2,1)S(1)}, u32[]{:S(2)}, u32[]{:S(2)}) collective-permute-start(bf16[8,4736]{1,0:T(8,128)(2,1)S(1)} %error.1.refs_0_), channel_id=1, source_target_pairs={{0,17},{1,16},{2,19},{3,18},{4,21},{5,20},{6,23},{7,22},{8,25},{9,... | collective-permute-start | bytes 227336 | tf_op jit(solution)/shard_map/ppermute | solution.py:46
  62.1 0.7 collective-permute-start.19
  62.8 1.4 %collective-permute-start.18 = (bf16[8,4736]{1,0:T(8,128)(2,1)S(1)}, bf16[8,4736]{1,0:T(8,128)(2,1)S(1)}, u32[]{:S(2)}, u32[]{:S(2)}) collective-permute-start(bf16[8,4736]{1,0:T(8,128)(2,1)S(1)} %error.1.refs_0_), channel_id=1, source_target_pairs={{0,1},{1,0},{2,3},{3,2},{4,5},{5,4},{6,7},{7,6},{8,9},{9,8},{10,11... | collective-permute-start | bytes 227336 | tf_op jit(solution)/shard_map/ppermute | solution.py:46
  64.1 2.6 %collective-permute-done.20.refs_3_ = bf16[8,4736]{1,0:T(8,128)(2,1)S(1)} collective-permute-done((bf16[8,4736]{1,0:T(8,128)(2,1)S(1)}, bf16[8,4736]{1,0:T(8,128)(2,1)S(1)}, u32[]{:S(2)}, u32[]{:S(2)}) %collective-permute-start.20) | collective-permute-done | bytes 75808 | tf_op jit(solution)/shard_map/ppermute | solution.py:46
  66.7 0.5 collective-permute-start.23
  67.2 0.1 collective-permute-done.18.refs_1_
  67.3 0.6 collective-permute-done.24.refs_7_
  68.0 0.2 collective-permute-done.23.refs_6_
  68.1 0.5 collective-permute-done.22.refs_5_
  68.6 21.2 %gradients.1 = (bf16[2048,4608]{1,0:T(8,128)(2,1)}, bf16[4608,2048]{1,0:T(8,128)(2,1)}, f32[1,2048]{1,0:T(1,128)}, f32[1,4608]{1,0:T(1,128)S(1)}, f32[1,128]{1,0:T(1,128)}) custom-call(bf16[8,4736]{1,0:T(8,128)(2,1)S(1)} %error.1.refs_0_, bf16[8,4736]{1,0:T(8,128)(2,1)S(1)} %collective-permute-done.18.refs_1_, ...), custom_call_target="tpu_custom_call" | custom-call | flops 3623878656 | bytes 37748736 | tf_op jit(solution)/shard_map/gradients/pallas_call | solution.py:493
  89.8 0.7 reduce
  (18 shorter events, 0.1 us)
Async XLA Ops:
  4.3 6.9 %collective-permute-start = (bf16[8,4608]{1,0:T(8,128)(2,1)S(1)}, bf16[8,4608]{1,0:T(8,128)(2,1)S(1)}, u32[]{:S(2)}, u32[]{:S(2)}) collective-permute-start(bf16[8,4608]{1,0:T(8,128)(2,1)S(1)} %get-tuple-element.36.refs_1_), channel_id=1, source_target_pairs={{0,1},{1,0},{2,3},{3,2},{4,5},{5,4},{6,7},{7,6},{8,9},{9,8},{10,11... | collective-permute-start | bytes 221192 | tf_op jit(solution)/shard_map/ppermute | solution.py:46
  11.3 10.3 %collective-permute-start.3 = (bf16[8,5760]{1,0:T(8,128)(2,1)S(1)}, bf16[8,5760]{1,0:T(8,128)(2,1)S(1)}, u32[]{:S(2)}, u32[]{:S(2)}) collective-permute-start(bf16[8,5760]{1,0:T(8,128)(2,1)S(1)} %heads_y.1.refs_2_.refs_0_), channel_id=1, source_target_pairs={{0,6},{1,7},{2,4},{3,5},{4,2},{5,3},{6,0},{7,1},{8,14},{9,15},{10,... | collective-permute-start | bytes 276488 | tf_op jit(solution)/shard_map/ppermute | solution.py:46
  15.0 7.5 %collective-permute-start.2 = (bf16[8,5760]{1,0:T(8,128)(2,1)S(1)}, bf16[8,5760]{1,0:T(8,128)(2,1)S(1)}, u32[]{:S(2)}, u32[]{:S(2)}) collective-permute-start(bf16[8,5760]{1,0:T(8,128)(2,1)S(1)} %heads_y.1.refs_2_.refs_0_), channel_id=1, source_target_pairs={{0,4},{1,5},{2,6},{3,7},{4,0},{5,1},{6,2},{7,3},{8,12},{9,13},{10,... | collective-permute-start | bytes 276488 | tf_op jit(solution)/shard_map/ppermute | solution.py:46
  15.0 7.5 %collective-permute-start.1 = (bf16[8,5760]{1,0:T(8,128)(2,1)S(1)}, bf16[8,5760]{1,0:T(8,128)(2,1)S(1)}, u32[]{:S(2)}, u32[]{:S(2)}) collective-permute-start(bf16[8,5760]{1,0:T(8,128)(2,1)S(1)} %heads_y.1.refs_2_.refs_0_), channel_id=1, source_target_pairs={{0,2},{1,3},{2,0},{3,1},{4,6},{5,7},{6,4},{7,5},{8,10},{9,11},{10,... | collective-permute-start | bytes 276488 | tf_op jit(solution)/shard_map/ppermute | solution.py:46
  21.6 10.7 %copy-start = (f32[2048]{0:T(1024)S(1)}, f32[2048]{0:T(1024)}, u32[]{:S(2)}) copy-start(f32[2048]{0:T(1024)} %refs_11_.1) | copy-start | bytes 24580
  22.7 5.8 %collective-permute-start.6 = (bf16[8,4608]{1,0:T(8,128)(2,1)S(1)}, bf16[8,4608]{1,0:T(8,128)(2,1)S(1)}, u32[]{:S(2)}, u32[]{:S(2)}) collective-permute-start(bf16[8,4608]{1,0:T(8,128)(2,1)S(1)} %residual.1.refs_1_.refs_0_.refs_4_), channel_id=1, source_target_pairs={{0,17},{1,16},{2,19},{3,18},{4,21},{5,20},{6,23},{7,22},{8,25},{9,... | collective-permute-start | bytes 221192 | tf_op jit(solution)/shard_map/ppermute | solution.py:46
  24.2 4.4 %collective-permute-start.5 = (bf16[8,4608]{1,0:T(8,128)(2,1)S(1)}, bf16[8,4608]{1,0:T(8,128)(2,1)S(1)}, u32[]{:S(2)}, u32[]{:S(2)}) collective-permute-start(bf16[8,4608]{1,0:T(8,128)(2,1)S(1)} %residual.1.refs_1_.refs_0_.refs_4_), channel_id=1, source_target_pairs={{0,16},{1,17},{2,18},{3,19},{4,20},{5,21},{6,22},{7,23},{8,24},{9,... | collective-permute-start | bytes 221192 | tf_op jit(solution)/shard_map/ppermute | solution.py:46
  24.7 4.5 %collective-permute-start.4 = (bf16[8,4608]{1,0:T(8,128)(2,1)S(1)}, bf16[8,4608]{1,0:T(8,128)(2,1)S(1)}, u32[]{:S(2)}, u32[]{:S(2)}) collective-permute-start(bf16[8,4608]{1,0:T(8,128)(2,1)S(1)} %residual.1.refs_1_.refs_0_.refs_4_), channel_id=1, source_target_pairs={{0,1},{1,0},{2,3},{3,2},{4,5},{5,4},{6,7},{7,6},{8,9},{9,8},{10,11... | collective-permute-start | bytes 221192 | tf_op jit(solution)/shard_map/ppermute | solution.py:46
  26.2 6.0 %collective-permute-start.7 = (bf16[8,4608]{1,0:T(8,128)(2,1)S(1)}, bf16[8,4608]{1,0:T(8,128)(2,1)S(1)}, u32[]{:S(2)}, u32[]{:S(2)}) collective-permute-start(bf16[8,4608]{1,0:T(8,128)(2,1)S(1)} %residual.1.refs_1_.refs_0_.refs_4_), channel_id=1, source_target_pairs={{0,8},{1,9},{2,10},{3,11},{4,12},{5,13},{6,14},{7,15},{8,0},{9,1},... | collective-permute-start | bytes 221192 | tf_op jit(solution)/shard_map/ppermute | solution.py:46
  28.4 3.8 %collective-permute-start.10 = (bf16[8,4608]{1,0:T(8,128)(2,1)S(1)}, bf16[8,4608]{1,0:T(8,128)(2,1)S(1)}, u32[]{:S(2)}, u32[]{:S(2)}) collective-permute-start(bf16[8,4608]{1,0:T(8,128)(2,1)S(1)} %collective-permute-done.6.refs_3_), channel_id=1, source_target_pairs={{0,8},{1,9},{2,10},{3,11},{4,12},{5,13},{6,14},{7,15},{8,0},{9,1},... | collective-permute-start | bytes 221192 | tf_op jit(solution)/shard_map/ppermute | solution.py:46
  28.5 3.7 %collective-permute-start.9 = (bf16[8,4608]{1,0:T(8,128)(2,1)S(1)}, bf16[8,4608]{1,0:T(8,128)(2,1)S(1)}, u32[]{:S(2)}, u32[]{:S(2)}) collective-permute-start(bf16[8,4608]{1,0:T(8,128)(2,1)S(1)} %collective-permute-done.5.refs_2_), channel_id=1, source_target_pairs={{0,8},{1,9},{2,10},{3,11},{4,12},{5,13},{6,14},{7,15},{8,0},{9,1},... | collective-permute-start | bytes 221192 | tf_op jit(solution)/shard_map/ppermute | solution.py:46
  29.2 3.0 %collective-permute-start.8 = (bf16[8,4608]{1,0:T(8,128)(2,1)S(1)}, bf16[8,4608]{1,0:T(8,128)(2,1)S(1)}, u32[]{:S(2)}, u32[]{:S(2)}) collective-permute-start(bf16[8,4608]{1,0:T(8,128)(2,1)S(1)} %collective-permute-done.4.refs_1_), channel_id=1, source_target_pairs={{0,8},{1,9},{2,10},{3,11},{4,12},{5,13},{6,14},{7,15},{8,0},{9,1},... | collective-permute-start | bytes 221192 | tf_op jit(solution)/shard_map/ppermute | solution.py:46
  40.7 1.8 %collective-permute-start.11 = (bf16[32,4736]{1,0:T(8,128)(2,1)S(1)}, bf16[32,4736]{1,0:T(8,128)(2,1)S(1)}, u32[]{:S(2)}, u32[]{:S(2)}) collective-permute-start(bf16[32,4736]{1,0:T(8,128)(2,1)S(1)} %get-tuple-element.51), channel_id=1, source_target_pairs={{0,8},{1,9},{2,10},{3,11},{4,12},{5,13},{6,14},{7,15},{8,0},{9,1},... | collective-permute-start | bytes 909320 | tf_op jit(solution)/shard_map/ppermute | solution.py:46
  42.6 4.7 %collective-permute-start.13 = (bf16[8,4736]{1,0:T(8,128)(2,1)S(1)}, bf16[8,4736]{1,0:T(8,128)(2,1)S(1)}, u32[]{:S(2)}, u32[]{:S(2)}) collective-permute-start(bf16[8,4736]{1,0:T(8,128)(2,1)S(1)} %get-tuple-element.54), channel_id=1, source_target_pairs={{0,16},{1,17},{2,18},{3,19},{4,20},{5,21},{6,22},{7,23},{8,24},{9,... | collective-permute-start | bytes 227336 | tf_op jit(solution)/shard_map/ppermute | solution.py:46
  44.0 5.8 %collective-permute-start.14 = (bf16[8,4736]{1,0:T(8,128)(2,1)S(1)}, bf16[8,4736]{1,0:T(8,128)(2,1)S(1)}, u32[]{:S(2)}, u32[]{:S(2)}) collective-permute-start(bf16[8,4736]{1,0:T(8,128)(2,1)S(1)} %get-tuple-element.55), channel_id=1, source_target_pairs={{0,17},{1,16},{2,19},{3,18},{4,21},{5,20},{6,23},{7,22},{8,25},{9,... | collective-permute-start | bytes 227336 | tf_op jit(solution)/shard_map/ppermute | solution.py:46
  45.5 5.5 %collective-permute-start.12 = (bf16[8,4736]{1,0:T(8,128)(2,1)S(1)}, bf16[8,4736]{1,0:T(8,128)(2,1)S(1)}, u32[]{:S(2)}, u32[]{:S(2)}) collective-permute-start(bf16[8,4736]{1,0:T(8,128)(2,1)S(1)} %get-tuple-element.53.after), channel_id=1, source_target_pairs={{0,1},{1,0},{2,3},{3,2},{4,5},{5,4},{6,7},{7,6},{8,9},{9,8},{10,11... | collective-permute-start | bytes 227336 | tf_op jit(solution)/shard_map/ppermute | solution.py:46
  51.0 6.7 %collective-permute-start.17 = (bf16[8,4736]{1,0:T(8,128)(2,1)S(1)}, bf16[8,4736]{1,0:T(8,128)(2,1)S(1)}, u32[]{:S(2)}, u32[]{:S(2)}) collective-permute-start(bf16[8,4736]{1,0:T(8,128)(2,1)S(1)} %recon.3.refs_0_), channel_id=1, source_target_pairs={{0,6},{1,7},{2,4},{3,5},{4,2},{5,3},{6,0},{7,1},{8,14},{9,15},{10,... | collective-permute-start | bytes 227336 | tf_op jit(solution)/shard_map/ppermute | solution.py:46
  53.9 6.6 %collective-permute-start.16 = (bf16[8,4736]{1,0:T(8,128)(2,1)S(1)}, bf16[8,4736]{1,0:T(8,128)(2,1)S(1)}, u32[]{:S(2)}, u32[]{:S(2)}) collective-permute-start(bf16[8,4736]{1,0:T(8,128)(2,1)S(1)} %recon.3.refs_0_), channel_id=1, source_target_pairs={{0,4},{1,5},{2,6},{3,7},{4,0},{5,1},{6,2},{7,3},{8,12},{9,13},{10,... | collective-permute-start | bytes 227336 | tf_op jit(solution)/shard_map/ppermute | solution.py:46
  53.9 6.6 %collective-permute-start.15 = (bf16[8,4736]{1,0:T(8,128)(2,1)S(1)}, bf16[8,4736]{1,0:T(8,128)(2,1)S(1)}, u32[]{:S(2)}, u32[]{:S(2)}) collective-permute-start(bf16[8,4736]{1,0:T(8,128)(2,1)S(1)} %recon.3.refs_0_), channel_id=1, source_target_pairs={{0,2},{1,3},{2,0},{3,1},{4,6},{5,7},{6,4},{7,5},{8,10},{9,11},{10,... | collective-permute-start | bytes 227336 | tf_op jit(solution)/shard_map/ppermute | solution.py:46
  60.6 6.1 %collective-permute-start.20 = (bf16[8,4736]{1,0:T(8,128)(2,1)S(1)}, bf16[8,4736]{1,0:T(8,128)(2,1)S(1)}, u32[]{:S(2)}, u32[]{:S(2)}) collective-permute-start(bf16[8,4736]{1,0:T(8,128)(2,1)S(1)} %error.1.refs_0_), channel_id=1, source_target_pairs={{0,17},{1,16},{2,19},{3,18},{4,21},{5,20},{6,23},{7,22},{8,25},{9,... | collective-permute-start | bytes 227336 | tf_op jit(solution)/shard_map/ppermute | solution.py:46
  62.1 4.6 %collective-permute-start.19 = (bf16[8,4736]{1,0:T(8,128)(2,1)S(1)}, bf16[8,4736]{1,0:T(8,128)(2,1)S(1)}, u32[]{:S(2)}, u32[]{:S(2)}) collective-permute-start(bf16[8,4736]{1,0:T(8,128)(2,1)S(1)} %error.1.refs_0_), channel_id=1, source_target_pairs={{0,16},{1,17},{2,18},{3,19},{4,20},{5,21},{6,22},{7,23},{8,24},{9,... | collective-permute-start | bytes 227336 | tf_op jit(solution)/shard_map/ppermute | solution.py:46
  62.8 4.6 %collective-permute-start.18 = (bf16[8,4736]{1,0:T(8,128)(2,1)S(1)}, bf16[8,4736]{1,0:T(8,128)(2,1)S(1)}, u32[]{:S(2)}, u32[]{:S(2)}) collective-permute-start(bf16[8,4736]{1,0:T(8,128)(2,1)S(1)} %error.1.refs_0_), channel_id=1, source_target_pairs={{0,1},{1,0},{2,3},{3,2},{4,5},{5,4},{6,7},{7,6},{8,9},{9,8},{10,11... | collective-permute-start | bytes 227336 | tf_op jit(solution)/shard_map/ppermute | solution.py:46
  64.1 3.2 %collective-permute-start.21 = (bf16[8,4736]{1,0:T(8,128)(2,1)S(1)}, bf16[8,4736]{1,0:T(8,128)(2,1)S(1)}, u32[]{:S(2)}, u32[]{:S(2)}) collective-permute-start(bf16[8,4736]{1,0:T(8,128)(2,1)S(1)} %error.1.refs_0_), channel_id=1, source_target_pairs={{0,8},{1,9},{2,10},{3,11},{4,12},{5,13},{6,14},{7,15},{8,0},{9,1},... | collective-permute-start | bytes 227336 | tf_op jit(solution)/shard_map/ppermute | solution.py:46
  66.7 1.3 %collective-permute-start.24 = (bf16[8,4736]{1,0:T(8,128)(2,1)S(1)}, bf16[8,4736]{1,0:T(8,128)(2,1)S(1)}, u32[]{:S(2)}, u32[]{:S(2)}) collective-permute-start(bf16[8,4736]{1,0:T(8,128)(2,1)S(1)} %collective-permute-done.20.refs_3_), channel_id=1, source_target_pairs={{0,8},{1,9},{2,10},{3,11},{4,12},{5,13},{6,14},{7,15},{8,0},{9,1},... | collective-permute-start | bytes 227336 | tf_op jit(solution)/shard_map/ppermute | solution.py:46
  66.7 1.4 %collective-permute-start.23 = (bf16[8,4736]{1,0:T(8,128)(2,1)S(1)}, bf16[8,4736]{1,0:T(8,128)(2,1)S(1)}, u32[]{:S(2)}, u32[]{:S(2)}) collective-permute-start(bf16[8,4736]{1,0:T(8,128)(2,1)S(1)} %collective-permute-done.19.refs_2_), channel_id=1, source_target_pairs={{0,8},{1,9},{2,10},{3,11},{4,12},{5,13},{6,14},{7,15},{8,0},{9,1},... | collective-permute-start | bytes 227336 | tf_op jit(solution)/shard_map/ppermute | solution.py:46
  67.3 1.3 %collective-permute-start.22 = (bf16[8,4736]{1,0:T(8,128)(2,1)S(1)}, bf16[8,4736]{1,0:T(8,128)(2,1)S(1)}, u32[]{:S(2)}, u32[]{:S(2)}) collective-permute-start(bf16[8,4736]{1,0:T(8,128)(2,1)S(1)} %collective-permute-done.18.refs_1_), channel_id=1, source_target_pairs={{0,8},{1,9},{2,10},{3,11},{4,12},{5,13},{6,14},{7,15},{8,0},{9,1},... | collective-permute-start | bytes 227336 | tf_op jit(solution)/shard_map/ppermute | solution.py:46

commit v3 on v0

v3 whole, which is shorter than its diff:
```python
import functools
import itertools
import math

import jax
import jax.numpy as jnp
from jax import lax
from jax.experimental import pallas as pl
from jax.experimental.pallas import tpu as pltpu
from jax.sharding import PartitionSpec as P

SPARSITY = 0.25
SMOOTHING = 0.1
EPSILON = 1e-06
F32 = jnp.float32
BF16 = jnp.bfloat16
LANES = 128


class Split:
    def __init__(self, axis, inner, size):
        self.axis, self.inner, self.size = axis, inner, size

    def place(self):
        return (lax.axis_index(self.axis) // self.inner) % self.size


class Group:
    def __init__(self, mesh, *splits):
        self.lengths = {axis: mesh.shape[axis] for axis in ("dp", "fsdp")}
        self.splits = splits
        self.size = math.prod(s.size for s in splits)
        self.keys = list(itertools.product(*(range(s.size) for s in splits)))

    def swap(self, x, key):
        pairs = []
        for d in range(self.lengths["dp"]):
            for f in range(self.lengths["fsdp"]):
                to = {"dp": d, "fsdp": f}
                for split, k in zip(self.splits, key):
                    a = (to[split.axis] // split.inner) % split.size
                    to[split.axis] += ((a ^ k) - a) * split.inner
                width = self.lengths["fsdp"]
                pairs.append((d * width + f, to["dp"] * width + to["fsdp"]))
        return lax.ppermute(x, ("dp", "fsdp"), pairs)

    def swaps(self, pieces):
        return [self.swap(p, key) for p, key in zip(pieces, self.keys[1:])]

    def spread(self, x):
        return [x] + [self.swap(x, key) for key in self.keys[1:]]


def block_of(total, most):
    return max(b for b in range(LANES, most + 1, LANES) if total % b == 0)


def resident(count):
    return [pl.BlockSpec(memory_space=pltpu.VMEM)] * count


def anywhere(count):
    return [pl.BlockSpec(memory_space=pl.ANY)] * count


def in_hbm(x):
    return pltpu.with_memory_space_constraint(x, pltpu.HBM)


def in_vmem(x):
    return pltpu.with_memory_space_constraint(x, pltpu.VMEM)


def params(megabytes):
    return pltpu.CompilerParams(vmem_limit_bytes=megabytes * 1024 * 1024)


def cost(flops, count):
    return pl.CostEstimate(flops=flops, bytes_accessed=count, transcendentals=0)


def struct(shape, kind):
    return jax.ShapeDtypeStruct(shape, kind)


def small(kernel, outs, *args, name):
    count = sum(x.size * x.dtype.itemsize for x in args) + sum(o.size * o.dtype.itemsize for o in outs)
    return pl.pallas_call(
        kernel,
        in_specs=resident(len(args)),
        out_specs=resident(len(outs)),
        out_shape=list(outs),
        compiler_params=params(6),
        cost_estimate=cost(count, count),
        name=name,
    )(*args)


def project(heads, weight, resid, gain, bias, deep, side):
    tokens = heads.shape[0]
    features = weight.shape[1]
    rows = tokens // side.size
    own = rows // deep.size
    quarter = features // deep.size
    wide = block_of(features, 1152)
    steps = features // wide

    def kernel(*refs):
        sources, outs = refs[:5], refs[5 : 8 + side.size]
        heads, weight, resid, gain, bias, sems = refs[8 + side.size :]
        packed, gain_row, bias_row, keep, *send = outs
        smalls = [
            pltpu.make_async_copy(source, here, sems.at[i])
            for i, (source, here) in enumerate([(sources[0], heads), *zip(sources[2:], (resid, gain, bias))])
        ]
        blocks = []
        for i in range(steps):
            at = pl.ds(i * wide, wide)
            blocks.append(pltpu.make_async_copy(sources[1].at[:, at], weight.at[:, at], sems.at[4 + i]))
        for copy in smalls[:1] + blocks + smalls[1:]:
            copy.start()

        to = lax.broadcasted_iota(jnp.int32, (tokens, tokens), 0)
        source = lax.broadcasted_iota(jnp.int32, (tokens, tokens), 1)
        across = lax.shift_right_logical(to, rows.bit_length() - 1) ^ side.place()
        down = (lax.shift_right_logical(to, own.bit_length() - 1) & (deep.size - 1)) ^ deep.place()
        wanted = (down * side.size + across) * own + (to & (own - 1))
        pick = jnp.where(source == wanted, 1.0, 0.0).astype(BF16)
        smalls[0].wait()
        turned = jnp.dot(pick, heads[...], preferred_element_type=F32).astype(BF16)
        for i, block in enumerate(blocks):
            block.wait()
            at = slice(i * wide, (i + 1) * wide)
            part = jnp.dot(turned, weight[:, at], preferred_element_type=F32)
            keep[:, at] = part[:rows]
            for k in range(1, side.size):
                send[k - 1][:, at] = part[k * rows : (k + 1) * rows].astype(BF16)
        for copy in smalls[1:]:
            copy.wait()
        values = resid[...].astype(F32)
        pieces = [values[:, q * quarter : (q + 1) * quarter] for q in range(deep.size)]
        packed[...] = jnp.concatenate(pieces, axis=0).astype(BF16)
        gain_row[...] = gain[...].reshape(1, features)
        bias_row[...] = bias[...].reshape(1, features)

    args = (heads, weight, resid, gain, bias)
    return pl.pallas_call(
        kernel,
        in_specs=anywhere(5),
        out_specs=resident(3 + side.size),
        out_shape=[struct((rows, quarter), BF16), struct((1, features), F32), struct((1, features), F32)]
        + [struct((rows, features), F32)]
        + [struct((rows, features), BF16)] * (side.size - 1),
        scratch_shapes=[pltpu.VMEM(x.shape, x.dtype) for x in args] + [pltpu.SemaphoreType.DMA((4 + steps,))],
        compiler_params=params(12),
        cost_estimate=cost(2 * tokens * weight.size, 2 * weight.size),
        name="project",
    )(*[in_hbm(x) for x in args])


def add_up(keep, got, parts, kind, name, beside=None, after=()):
    rows, columns = keep.shape
    part = rows // parts
    extra = [] if beside is None else [beside]
    width = columns + sum(b.shape[1] for b in extra)

    def kernel(*refs):
        ins, outs = refs[: 1 + len(got)], refs[-parts:]
        for p in range(parts):
            at = slice(p * part, (p + 1) * part)
            total = ins[0][at, :]
            for g in ins[1:]:
                total = total + g[at, :].astype(F32)
            outs[p][:, :columns] = total.astype(outs[p].dtype)
        if extra:
            outs[0][:, columns:] = refs[1 + len(got)][...]

    outs = [struct((part, width), kind)] + [struct((part, columns), BF16)] * (parts - 1)
    return small(kernel, outs, keep, *got, *extra, *after, name=name)


def group_sum(parts, own):
    size = len(parts)
    terms = []
    for k, part in enumerate(parts):
        pieces = [part[(j ^ k) * own : ((j ^ k) + 1) * own, :] for j in range(size)]
        terms.append(jnp.concatenate(pieces, axis=0) if size > 1 else part)
    while len(terms) > 1:
        half = len(terms) // 2
        terms = [terms[i] + terms[i + half] for i in range(half)]
    return terms[0]


def residual(parts, gain, after):
    rows = parts[0].shape[0]
    features = gain.shape[1]
    count = len(parts)
    own, quarter = rows // count, features // count

    def kernel(*refs):
        sums, gain, out = refs[:count], refs[count], refs[-1]
        projected = group_sum([p[:, :features].astype(F32) for p in sums], own)
        scale = lax.rsqrt(jnp.mean(projected * projected, axis=-1, keepdims=True) + EPSILON)
        packed = [p[:, features:].astype(F32) for p in sums]
        for q in range(count):
            at = slice(q * quarter, (q + 1) * quarter)
            before = jnp.concatenate([p[q * own : (q + 1) * own, :] for p in packed], axis=0)
            out[:, at] = (before + projected[:, at] * scale * gain[:, at]).astype(BF16)

    return small(kernel, [struct((rows, features), BF16)], *parts, gain, *after, name="residual")[0]


def chunk_at(group, key, width):
    place = 0
    for split, k in zip(group.splits, key):
        place = place * split.size + (split.place() ^ k)
    return pl.multiple_of(place * width, LANES)


def split_columns(keep, got, group, after):
    rows, columns = keep.shape
    width = columns // group.size

    def kernel(*refs):
        ins, outs = refs[: 1 + len(got)], refs[-group.size :]
        for key, out in zip(group.keys, outs):
            at = pl.ds(chunk_at(group, key, width), width)
            total = ins[0][:, at]
            for g in ins[1:]:
                total = total + g[:, at].astype(F32)
            out[...] = total.astype(out.dtype)

    outs = [struct((rows, width), F32)] + [struct((rows, width), BF16)] * (group.size - 1)
    return small(kernel, outs, keep, *got, *after, name="recon")


def fewest(rows):
    return 8 if rows % 8 == 0 else rows


def lay(out, x):
    rows, width = x.shape
    height = out.shape[0]
    for i in range(rows // height):
        out[:, i * width : (i + 1) * width] = x[i * height : (i + 1) * height, :]


def unlaid(x, rows, width):
    height = x.shape[0]
    return jnp.concatenate([x[:, i * width : (i + 1) * width] for i in range(rows // height)], axis=0)


def put_number(out, at, value):
    high = value.astype(BF16)
    low = (value - high.astype(F32)).astype(BF16)
    half = LANES // 2
    out[:, at : at + half] = jnp.broadcast_to(high, (out.shape[0], half))
    out[:, at + half : at + LANES] = jnp.broadcast_to(low, (out.shape[0], half))


def get_number(x, at):
    half = LANES // 2
    return x[:1, at : at + 1].astype(F32) + x[:1, at + half : at + half + 1].astype(F32)


def with_penalty(keep, got, penalties):
    rows, width = keep.shape

    def kernel(*refs):
        ins, numbers, out = refs[: 1 + len(got)], refs[1 + len(got) : -1], refs[-1]
        total = ins[0][...]
        for g in ins[1:]:
            total = total + g[...].astype(F32)
        lay(out, total.astype(BF16))
        penalty = numbers[0][:1, :1]
        for n in numbers[1:]:
            penalty = penalty + n[:1, :1]
        put_number(out, length, penalty)

    height = fewest(rows)
    length = rows // height * width
    return small(kernel, [struct((height, length + LANES), BF16)], keep, *got, *penalties, name="recon")[0]


def tree(terms):
    terms = list(terms)
    while len(terms) > 1:
        half = len(terms) // 2
        terms = [terms[i] + terms[i + half] for i in range(half)]
    return terms[0]


def error_of(parts, resid, bias, group, rows, after):
    height, length = parts[0].shape
    length -= LANES
    width = resid.shape[1] // group.size

    def kernel(*refs):
        sums, resid, bias, out = refs[: len(parts)], refs[len(parts)], refs[len(parts) + 1], refs[-1]
        at = pl.ds(chunk_at(group, group.keys[0], width), width)
        total = unlaid(tree([p[:, :length].astype(F32) for p in sums]), rows, width)
        lay(out, (total + bias[:, at] - resid[:rows, at].astype(F32)).astype(BF16))
        put_number(out, length, tree([get_number(p, length) for p in sums]))

    return small(kernel, [struct((height, length + LANES), BF16)], *parts, resid, bias, *after, name="error")[0]


def stack(pieces, after=()):
    rows, columns = sum(p.shape[0] for p in pieces), pieces[0].shape[1]

    def kernel(*refs):
        row = 0
        for ref in refs[: len(pieces)]:
            refs[-1][row : row + ref.shape[0], :] = ref[...]
            row += ref.shape[0]

    return small(kernel, [struct((rows, columns), pieces[0].dtype)], *pieces, *after, name="stack")[0]


def gather(stages, *pieces):
    pieces = list(pieces)
    for group in reversed(stages):
        if len(pieces) > 4:
            pieces = [stack(pieces)]
        pieces = pieces + [group.swap(p, key) for key in group.keys[1:] for p in pieces]
    return pieces


def copy_rows(source, first, here, sems, start, step=384):
    rows = here.shape[0]
    step = max(b for b in range(16, step + 1, 16) if rows % b == 0)
    return [
        pltpu.make_async_copy(source.at[pl.ds(first + r, step)], here.at[pl.ds(r, step)], sems.at[start + r // step])
        for r in range(0, rows, step)
    ]


MOST_COPIES = 32


def in_order(copies, act):
    def body(_, carry):
        for copy in copies:
            copy.start() if act == "start" else copy.wait()
        return carry

    lax.fori_loop(0, jnp.minimum(lax.axis_index("fsdp") + 1, 1), body, 0)


def load(items, after, name):
    def kernel(*refs):
        sources, results, sems = refs[: len(items)], refs[len(items) + 1 : -1], refs[-1]
        copies = []
        for source, here, (_, first, _) in zip(sources, results, items):
            copies += copy_rows(source, first, here, sems, len(copies))
        for copy in copies:
            copy.start()
        results[-1][...] = jnp.zeros_like(results[-1])
        for copy in copies:
            copy.wait()

    return pl.pallas_call(
        kernel,
        in_specs=anywhere(len(items)) + resident(1),
        out_specs=resident(len(items) + 1),
        out_shape=[pltpu.VMEM((rows, source.shape[1]), source.dtype) for source, _, rows in items]
        + [struct((8, LANES), F32)],
        scratch_shapes=[pltpu.SemaphoreType.DMA((MOST_COPIES,))],
        compiler_params=params(4),
        cost_estimate=cost(0, sum(2 * rows * source.shape[1] for source, _, rows in items)),
        name=name,
    )(*[in_hbm(item[0]) for item in items], after)


def norms(weights, usages, after):
    rows, features = weights.shape
    step = math.gcd(rows, 256)

    def kernel(weight, usage, after, coef, norm_row, penalty):
        total = jnp.zeros((1, 1), F32)
        for r in range(0, rows, step):
            at = slice(r, r + step)
            squares = jnp.zeros((step, LANES), F32)
            for c in range(0, features, LANES):
                w = weight[at, c : c + LANES].astype(F32)
                squares = squares + w * w
            norm = jnp.sqrt(jnp.sum(squares, axis=1, keepdims=True) + EPSILON)
            used = usage[at, :]
            coef[at, :] = SPARSITY * (used / norm)
            norm_row[:, at] = jnp.broadcast_to(norm, (step, LANES)).T[:1, :]
            total = total + jnp.sum(used * norm, axis=0, keepdims=True)
        penalty[...] = jnp.broadcast_to(total, penalty.shape)

    return pl.pallas_call(
        kernel,
        in_specs=resident(3),
        out_specs=resident(3),
        out_shape=[struct((rows, 1), F32), struct((1, rows), F32), struct((8, LANES), F32)],
        compiler_params=params(6),
        cost_estimate=cost(0, 6 * rows * features),
        name="norms",
    )(in_vmem(weights), usages, after)


def encode(parts, held, bias, dec_weight, first, cut, mask_of):
    starts = range(first, dec_weight.shape[0], cut)
    tokens = sum(p.shape[0] for p in parts)
    features = parts[0].shape[1]
    latents = held[0].shape[1]
    wide = block_of(latents, 256)

    def kernel(*refs):
        parts_in, weights = refs[: len(parts)], refs[len(parts) : len(parts) + len(held)]
        bias, source, preact, resid, *here, stacked, sems = refs[len(parts) + len(held) :]
        copies = []
        for start, piece in zip(starts, here):
            copies += copy_rows(source, start, piece, sems, len(copies))
        in_order(copies, "start")
        row = 0
        for part in parts_in:
            stacked[row : row + part.shape[0], :] = part[...]
            row += part.shape[0]
        to = lax.broadcasted_iota(jnp.int32, (tokens, tokens), 0)
        source_row = lax.broadcasted_iota(jnp.int32, (tokens, tokens), 1)
        pick = jnp.where(source_row == (to ^ mask_of()), 1.0, 0.0).astype(BF16)
        block = block_of(features, 512)
        for c in range(0, features, block):
            at = slice(c, c + block)
            resid[:, at] = jnp.dot(pick, stacked[:, at], preferred_element_type=F32).astype(BF16)
        row = bias[...].reshape(1, latents)
        for c in range(0, latents, wide):
            at = slice(c, c + wide)
            total, start = row[:, at], 0
            for w in weights:
                span = w.shape[0]
                total = total + jnp.dot(resid[:, start : start + span], w[:, at], preferred_element_type=F32)
                start += span
            preact[:, at] = total
        in_order(copies, "wait")

    return pl.pallas_call(
        kernel,
        in_specs=resident(len(parts) + len(held) + 1) + anywhere(1),
        out_specs=resident(2 + len(starts)),
        out_shape=[struct((tokens, latents), F32), struct((tokens, features), BF16)]
        + [pltpu.VMEM((cut, features), BF16)] * len(starts),
        scratch_shapes=[pltpu.VMEM((tokens, features), BF16), pltpu.SemaphoreType.DMA((MOST_COPIES,))],
        compiler_params=params(6),
        cost_estimate=cost(2 * tokens * features * latents, 2 * tokens * features),
        name="encode",
    )(*parts, *[in_vmem(w) for w in held], bias, in_hbm(dec_weight))


def decode(preact, held, parts):
    tokens, latents = preact.shape
    features = held[0].shape[1]
    kept = tokens // parts
    sent = max(tokens - kept, 8)
    count = len(held)
    wide = block_of(features, 512)
    sizes = [w.shape[0] for w in held]
    step = math.gcd(*sizes, 256)

    def kernel(preact, *refs):
        weights, keep, send, latents_t = refs[:count], *refs[count : count + 3]
        usages, latents_b = refs[count + 3 : -1], refs[-1]
        for i, (p, r) in enumerate(row_blocks(weights, step)):
            at = slice(i * step, (i + 1) * step)
            value = jnp.maximum(preact[:, at], 0.0)
            latents_b[:, at] = value.astype(BF16)
            turned = value.T
            latents_t[at, :] = turned.astype(BF16)
            usages[p][r : r + step, :] = jnp.sum(turned, axis=1, keepdims=True)
        for c in range(0, features, wide):
            at = slice(c, c + wide)
            part, start = None, 0
            for w, span in zip(weights, sizes):
                term = jnp.dot(latents_b[:, start : start + span], w[:, at], preferred_element_type=F32)
                part = term if part is None else part + term
                start += span
            keep[:, at] = part[:kept]
            if kept < tokens:
                send[:, at] = part[kept:].astype(BF16)

    return pl.pallas_call(
        kernel,
        in_specs=resident(1 + count),
        out_specs=resident(3 + count),
        out_shape=[
            struct((kept, features), F32),
            struct((sent, features), BF16),
            struct((latents, tokens), BF16),
        ]
        + [struct((size, 1), F32) for size in sizes],
        scratch_shapes=[pltpu.VMEM((tokens, latents), BF16)],
        compiler_params=params(6),
        cost_estimate=cost(2 * tokens * features * latents, 6 * tokens * features),
        name="decode",
    )(preact, *[in_vmem(w) for w in held])


def turn(x, after):
    def kernel(x, after, out):
        out[...] = x[...].astype(F32).T.astype(BF16)

    return small(kernel, [struct(x.shape[::-1], BF16)], x, after, name="turn")[0]


def row_blocks(weights, rows):
    return [(p, r) for p, w in enumerate(weights) for r in range(0, w.shape[0], rows)]


def fold(x):
    n = x.shape[0]
    while n > 1 and n % 2 == 0:
        n //= 2
        x = x[:n] + x[n:]
    return x if n == 1 else jnp.sum(x, axis=0, keepdims=True)


def row_blocks(weights, rows):
    return [(p, r) for p, w in enumerate(weights) for r in range(0, w.shape[0], rows)]


def units(refs, height):
    return [ref.at[pl.ds(r, height)] for ref in refs for r in range(0, ref.shape[0], height)]


def assemble(messages, error, width):
    height = messages[0].shape[0]
    groups = error.shape[0] // len(messages) // height
    for i, message in enumerate(messages):
        for g in range(groups):
            at = (i * groups + g) * height
            error[at : at + height, :] = message[:, g * width : (g + 1) * width]


def spans(width):
    wide = min(width, 512)
    return [(c, min(wide, width - c)) for c in range(0, width, wide)]


def outer(latents_t, error, coef, weight):
    return (jnp.dot(latents_t, error, preferred_element_type=F32) + coef * weight.astype(F32)).astype(BF16)


def back_product(error, weight):
    return lax.dot_general(error, weight, (((1,), (1,)), ((), ())), preferred_element_type=F32)


def first_back(parts, height, weights, group):
    features = weights[0].shape[1]
    width = features // group.size
    tokens = sum(p.shape[0] * (p.shape[1] // width) for p in parts)
    latents = sum(w.shape[0] for w in weights)
    rows = math.gcd(*[w.shape[0] for w in weights], 256)

    def kernel(*refs):
        pieces, held = refs[: len(parts)], refs[len(parts) : len(parts) + len(weights)]
        back, error = refs[-2:]
        columns = chunk_at(group, group.keys[0], width)
        assemble(units(pieces, height), error, width)
        for i, (p, r) in enumerate(row_blocks(held, rows)):
            weight = held[p][r : r + rows, pl.ds(columns, width)]
            back[:, i * rows : (i + 1) * rows] = back_product(error[...], weight)

    return pl.pallas_call(
        kernel,
        in_specs=resident(len(parts) + len(weights)),
        out_specs=pl.BlockSpec(memory_space=pltpu.VMEM),
        out_shape=struct((tokens, latents), F32),
        scratch_shapes=[pltpu.VMEM((tokens, width), BF16)],
        compiler_params=params(8),
        cost_estimate=cost(2 * tokens * width * latents, 4 * width * latents),
        name="first_back",
    )(*parts, *[in_vmem(w) for w in weights])


def first_outer(parts, height, latents_t, coefs, weights, group, after):
    latents, tokens = latents_t.shape
    features = weights[0].shape[1]
    width = features // group.size
    count = len(weights)
    rows = math.gcd(*[w.shape[0] for w in weights], 256)

    def kernel(*refs):
        pieces, refs = refs[: len(parts)], refs[len(parts) :]
        coef, held = refs[:count], refs[count : 2 * count]
        latents_t, _, dec_grad, ready, error, stage, sems = refs[2 * count :]
        ready[...] = jnp.zeros_like(ready)
        columns = chunk_at(group, group.keys[0], width)
        assemble(units(pieces, height), error, width)
        copies = []
        for i, (p, r) in enumerate(row_blocks(held, rows)):
            at, inside = slice(i * rows, (i + 1) * rows), slice(r, r + rows)
            for c, wide in spans(width):
                over = pl.ds(pl.multiple_of(columns + c, LANES), wide)
                stage[at, c : c + wide] = outer(
                    latents_t[at, :], error[:, c : c + wide], coef[p][inside, :], held[p][inside, over]
                )
            at = pl.ds(i * rows, rows)
            copies.append(
                pltpu.make_async_copy(stage.at[at], dec_grad.at[at, pl.ds(columns, width)], sems.at[i])
            )
            copies[-1].start()
        for copy in copies:
            copy.wait()

    return pl.pallas_call(
        kernel,
        in_specs=resident(len(parts) + 2 * count + 2),
        out_specs=anywhere(1) + resident(1),
        out_shape=[struct((latents, features), BF16), struct((8, LANES), F32)],
        scratch_shapes=[
            pltpu.VMEM((tokens, width), BF16),
            pltpu.VMEM((latents, width), BF16),
            pltpu.SemaphoreType.DMA((latents // rows,)),
        ],
        compiler_params=params(10),
        cost_estimate=cost(2 * tokens * width * latents, 4 * width * latents),
        name="first_outer",
    )(*parts, *coefs, *[in_vmem(w) for w in weights], latents_t, after)


def gradients(first, others, height, resid_t, preact, latents_t, coefs, weights, norm_rows, dec_grad, back, group):
    tokens, latents = preact.shape
    features = weights[0].shape[1]
    width = features // group.size
    count, size = len(weights), group.size
    pieces = len(first)
    rows = math.gcd(*[w.shape[0] for w in weights], 256)
    span = math.gcd(latents, 512)
    deep = block_of(features, 1152)
    dec_slots, enc_slots = 3, 6
    flat = first + others

    def kernel(*refs):
        chunks = [units(refs[:pieces], height)]
        chunks += [units(refs[pieces : len(flat)], height)[k :: size - 1] for k in range(size - 1)]
        refs = refs[len(flat) :]
        coef, held, norm_row, refs = refs[:count], refs[count : 2 * count], refs[2 * count : 3 * count], refs[3 * count :]
        (resid_t, preact, latents_t, back, _, dec_grad, enc_grad, bias_grad, column_sum, loss,
         error, pulled, sums, dec_stage, enc_stage, dec_sem, enc_sem) = refs
        columns = [chunk_at(group, key, width) for key in group.keys]
        for k in range(size):
            assemble(chunks[k], error.at[k], width)
        where = row_blocks(held, rows)
        dec_copies, enc_copies = [], []

        def products(i):
            p, r = where[i]
            at, inside = slice(i * rows, (i + 1) * rows), slice(r, r + rows)
            total = back[:, at]
            for k in range(1, size):
                for c, wide in spans(width):
                    part = error[k, :, c : c + wide]
                    weight = held[p][inside, pl.ds(pl.multiple_of(columns[k] + c, LANES), wide)]
                    dec_stage[i % dec_slots, k - 1, :, c : c + wide] = outer(
                        latents_t[at, :], part, coef[p][inside, :], weight
                    )
                    total = total + back_product(part, weight)
            total = (total + SPARSITY * norm_row[p][:, inside]) * jax.nn.sigmoid(preact[:, at] / SMOOTHING)
            bias_grad[:, at] = jnp.sum(total, axis=0, keepdims=True)
            pulled[:, at] = total.astype(BF16)

        def send_rows(i):
            slot = i % dec_slots
            for k in range(1, size):
                copy = pltpu.make_async_copy(
                    dec_stage.at[slot, k - 1],
                    dec_grad.at[pl.ds(i * rows, rows), pl.ds(columns[k], width)],
                    dec_sem.at[slot, k - 1],
                )
                copy.start()
                dec_copies.append(copy)

        blocks = [(first, j) for first in range(0, latents, span) for j in range(0, features, deep)]

        def block(n):
            first, j = blocks[n]
            enc_stage[n % enc_slots] = jnp.dot(
                resid_t[j : j + deep, :], pulled[:, first : first + span], preferred_element_type=F32
            ).astype(BF16)

        def send_block(n):
            (first, j), slot = blocks[n], n % enc_slots
            copy = pltpu.make_async_copy(
                enc_stage.at[slot], enc_grad.at[pl.ds(j, deep), pl.ds(first, span)], enc_sem.at[slot]
            )
            copy.start()
            enc_copies.append(copy)

        def free_block(n):
            if n >= enc_slots:
                enc_copies[n - enc_slots].wait()

        each, per = span // rows, features // deep
        done = 0
        for i in range(latents // rows):
            if i >= dec_slots:
                for k in range(1, size):
                    dec_copies[(i - dec_slots) * (size - 1) + k - 1].wait()
            upto = min(done + -(-per // each), i // each * per)
            for n in range(done, upto):
                free_block(n)
            products(i)
            for n in range(done, upto):
                block(n)
            send_rows(i)
            for n in range(done, upto):
                send_block(n)
            done = upto
        for n in range(done, len(blocks)):
            free_block(n)
            block(n)
            send_block(n)

        squares, penalties = [], []
        for k in range(size):
            total = jnp.zeros((1, 1), F32)
            for c, wide in spans(width):
                e = error[k, :, c : c + wide].astype(F32)
                sums[:, pl.ds(pl.multiple_of(columns[k] + c, LANES), wide)] = fold(e)
                total = total + jnp.sum(fold(e * e), axis=1, keepdims=True)
            squares.append(total)
            penalties += [get_number(piece[...], piece.shape[1] - LANES) for piece in chunks[k]]
        column_sum[...] = sums[...].reshape(features)
        value = (0.5 * tree(squares) + SPARSITY * tree(penalties)) / (tokens * features)
        loss[0, 0] = jnp.sum(value)
        for copy in dec_copies[-dec_slots * (size - 1) :] + enc_copies[-enc_slots:]:
            copy.wait()

    return pl.pallas_call(
        kernel,
        in_specs=resident(len(flat) + 3 * count + 4) + anywhere(1),
        out_specs=anywhere(2) + resident(2) + [pl.BlockSpec(memory_space=pltpu.SMEM)],
        out_shape=[
            struct((latents, features), BF16),
            struct((features, latents), BF16),
            struct((1, latents), F32),
            struct((features,), F32),
            struct((1, 1), F32),
        ],
        scratch_shapes=[
            pltpu.VMEM((size, tokens, width), BF16),
            pltpu.VMEM((tokens, latents), BF16),
            pltpu.VMEM((1, features), F32),
            pltpu.VMEM((dec_slots, max(size - 1, 1), rows, width), BF16),
            pltpu.VMEM((enc_slots, deep, span), BF16),
            pltpu.SemaphoreType.DMA((dec_slots, max(size - 1, 1))),
            pltpu.SemaphoreType.DMA((enc_slots,)),
        ],
        input_output_aliases={len(flat) + 3 * count + 4: 0},
        compiler_params=params(18),
        cost_estimate=cost(6 * tokens * features * latents, 4 * features * latents),
        name="gradients",
    )(*flat, *coefs, *[in_vmem(w) for w in weights], *norm_rows, resid_t, preact, latents_t, back, dec_grad)


def make_body(mesh):
    dp, fsdp = mesh.shape["dp"], mesh.shape["fsdp"]
    cores = 2 if dp % 2 == 0 else 1
    depth = 4 if fsdp % 4 == 0 else 1
    core_split, across_split = Split("dp", 1, cores), Split("dp", cores, dp // cores)
    deep_split, side_split = Split("fsdp", fsdp // depth, depth), Split("fsdp", 1, fsdp // depth)
    core, deep, side = Group(mesh, core_split), Group(mesh, deep_split), Group(mesh, side_split)
    if across_split.size * side_split.size <= 4:
        by_token, by_feature = [core], Group(mesh, across_split, side_split)
    else:
        by_token, by_feature = [core, Group(mesh, across_split)], side
    stages = by_token + [by_feature]

    def body(attn_heads, out_proj, resid_pre, post_gain, enc_weight, enc_bias, dec_weight, dec_bias):
        own = resid_pre.shape[0]
        latents, features = dec_weight.shape
        cut = max(latents // 4, LANES)
        depth = features // 3

        def mask():
            place = 0
            for split in (across_split, side_split):
                shared = any(split is s for s in by_feature.splits)
                place = place * split.size + (split.place() if shared else 0)
            return (place * deep_split.size + deep_split.place()) * own

        packed, gain, bias, keep, *send = project(
            attn_heads, out_proj, resid_pre, post_gain, dec_bias, deep_split, side_split
        )
        got = side.swaps(send)
        enc_first, ready = load([(enc_weight, 0, depth)], send[0] if send else keep, "load_first")
        summed = add_up(keep, got, 1, BF16, "heads_y", packed, [ready])[0]
        sums = deep.spread(summed)
        enc_second, enc_third, dec_first, ready = load(
            [(enc_weight, depth, depth), (enc_weight, 2 * depth, depth), (dec_weight, 0, cut)], summed, "load_second"
        )
        resid_own = residual(sums, gain, [ready])
        near = by_feature.spread(resid_own)
        held, ready = [dec_first], []
        if latents == 4 * cut:
            dec_next, *ready = load([(dec_weight, cut, cut)], resid_own, "load_third")
            held.append(dec_next)
        near = near[:1] + [stack(near[1:], ready)] * (len(near) > 1)
        resid_parts = gather(by_token, *near)

        preact, resid_all, *dec_last = encode(
            resid_parts, [enc_first, enc_second, enc_third], enc_bias, dec_weight, cut * len(held), cut, mask
        )
        held += dec_last
        keep, send, latents_t, *used = decode(preact, held, core.size)
        send = [send]
        found = [norms(held[0], used[0], send[0])]
        for i, group in enumerate(by_token):
            got = group.swaps(send)
            if i + 1 < len(by_token):
                keep, *send = add_up(keep, got, by_token[i + 1].size, F32, "recon")
            else:
                keep, *send = split_columns(keep, got, by_feature, found[0][2:])
        got = by_feature.swaps(send)
        found += [norms(w, u, keep) for w, u in zip(held[1:], used[1:])]
        coefs, norm_rows, penalties = [list(x) for x in zip(*found)]
        rows = keep.shape[0]
        keep = with_penalty(keep, got, penalties)
        sums = deep.spread(keep)
        resid_t = turn(resid_all, keep)
        error_own = error_of(sums, resid_all, bias, by_feature, rows, [resid_t])

        others = by_feature.spread(error_own)[1:]
        first, height = gather(by_token, error_own), error_own.shape[0]
        back = first_back(first, height, held, by_feature)
        dec_grad, ready = first_outer(first, height, latents_t, coefs, held, by_feature, back)
        others = gather(by_token, stack(others, [ready])) if others else []
        dec_grad, enc_grad, bias_grad, column_sum, loss = gradients(
            first, others, height, resid_t, preact, latents_t, coefs, held, norm_rows, dec_grad, back, by_feature
        )
        return (enc_grad, bias_grad.reshape(-1), dec_grad, column_sum, loss.reshape(()))

    return body


def solution(mesh):
    placed = (
        P("dp", "fsdp"),
        P("fsdp", None),
        P(("dp", "fsdp"), None),
        P(),
        P(None, ("dp", "fsdp")),
        P(("dp", "fsdp")),
        P(("dp", "fsdp"), None),
        P(),
    )
    return jax.shard_map(
        make_body(mesh),
        mesh=mesh,
        in_specs=placed,
        out_specs=(P(None, ("dp", "fsdp")), P(("dp", "fsdp")), P(("dp", "fsdp"), None), P(), P()),
        check_vma=False,
    )
```

time: 459 us -> 82.7 us (0.18)
  waiting for transfers between devices: 194 us -> 9.19 us
  blocking collectives: 174 us -> 0 us
  matrix products: 58.7 us -> 0 us
  Pallas kernels: 0 us -> 48.7 us
  starting transfers between devices: 0.08 us -> 23.6 us
  between operations: 17.3 us -> 1.03 us
  other arithmetic: 12.5 us -> 0 us
    unnamed x4 -> x0, waiting for transfers between devices: 194 us -> none
    all_gather x2 -> x0, blocking collectives: 137 us -> none  [the longest x1 68.8 us: body(): error_all = lax.all_gather(error_b, ('dp', 'fsdp'), axis=0, tiled=True)]
    dot_general x6 -> x0, matrix products: 58.7 us -> none  [the longest x1 13.2 us: body(): lax.dot_general(latents_b, error_all, (((0,), (0,)), ((), ())), preferred...]
    pallas_call x0 -> x21, Pallas kernels: none -> 48.7 us  [the longest x1 16.9 us: gradients(): pl.pallas_call(kernel, in_specs=resident(len(flat) + 3 * count + 4) + any...]
    psum x1 -> x0, blocking collectives: 37.1 us -> none  [body(): error_total = lax.psum(error_local, ('dp', 'fsdp'))]
    ppermute x0 -> x21, starting transfers between devices: none -> 23.6 us  [swap(): return lax.ppermute(x, ('dp', 'fsdp'), pairs)]
    reduce_sum x4 -> x0, other arithmetic: 11.4 us -> none  [the longest x1 8.03 us: body(): jnp.sum(jnp.square(dec_weight.astype(jnp.float32)), axis=1) + EPSILON]
    ppermute x0 -> x21, waiting for transfers between devices: none -> 9.19 us  [swap(): return lax.ppermute(x, ('dp', 'fsdp'), pairs)]
  transfers between devices with their start and end apart: 2 -> 21, of which waited for: 2 -> 9; matrix products, arithmetic and copies ran while one was open for 2% -> 0% of each run, Pallas kernels for 0% -> 26%
where the time goes in v3:
time: 82.7 us; the launch traced here: 82.4 us
  Pallas kernels  48.7 us (59%)
  starting transfers between devices  23.6 us (29%)
  waiting for transfers between devices  9.19 us (11%)
  between operations  1.03 us (1%)
    ppermute x21, starting transfers between devices, swap(): return lax.ppermute(x, ('dp', 'fsdp'), pairs)  23.6 us
    pallas_call x1, Pallas kernels, gradients(): pl.pallas_call(kernel, in_specs=resident(len(flat) + 3 * count + 4) + any...  16.9 us
    pallas_call x3, Pallas kernels, load(): pl.pallas_call(kernel, in_specs=anywhere(len(items)) + resident(1), out_s...  12.1 us
    ppermute x21, waiting for transfers between devices, swap(): return lax.ppermute(x, ('dp', 'fsdp'), pairs)  9.19 us
    pallas_call x4, Pallas kernels, norms(): pl.pallas_call(kernel, in_specs=resident(3), out_specs=resident(3), out_s...  4.44 us
    pallas_call x1, Pallas kernels, encode(): pl.pallas_call(kernel, in_specs=resident(len(parts) + len(held) + 1) + an...  4.11 us
    pallas_call x1, Pallas kernels, decode(): pl.pallas_call(kernel, in_specs=resident(1 + count), out_specs=resident(3...  3.36 us
    pallas_call x1, Pallas kernels, project(): pl.pallas_call(kernel, in_specs=anywhere(5), out_specs=resident(3 + side....  2.73 us
  transfers between devices with their start and end apart: 21, of which 9 were waited for; matrix products, arithmetic and copies ran while one was open for 0% of the time, Pallas kernels for 26%

profile of v3, /device:TPU:0, one launch (start us, length us, event | category | flops | bytes accessed | tf_op | source)
XLA Modules:
  0.0 82.4 jit_solution(16977188895381386770)
XLA Ops:
  0.6 2.7 %project.1 = (bf16[8,1152]{1,0:T(8,128)(2,1)S(1)}, f32[1,4608]{1,0:T(1,128)S(1)}, f32[1,4608]{1,0:T(1,128)S(1)}, f32[8,4608]{1,0:T(8,128)S(1)}, bf16[8,4608]{1,0:T(8,128)(2,1)S(1)}) custom-call(bf16[16,512]{1,0:T(8,128)(2,1)} %refs_0_.4, bf16[512,4608]{1,0:T(8,128)(2,1)} %refs_1_.2, bf16[2,4608]{1,0:T(2,128)(2,1)} %refs_2_.2, f32[4608]{0:T(1024)} %refs_3_.1, ...), custom_call_target="tpu_custom_call" | custom-call | flops 75497472 | bytes 4718592 | tf_op jit(solution)/shard_map/project/pallas_call | solution.py:147
  3.4 3.0 %collective-permute-start = (bf16[8,4608]{1,0:T(8,128)(2,1)S(1)}, bf16[8,4608]{1,0:T(8,128)(2,1)S(1)}, u32[]{:S(2)}, u32[]{:S(2)}) collective-permute-start(bf16[8,4608]{1,0:T(8,128)(2,1)S(1)} %get-tuple-element.53.refs_1_), channel_id=1, source_target_pairs={{0,1},{1,0},{2,3},{3,2},{4,5},{5,4},{6,7},{7,6},{8,9},{9,8},{10,11... | collective-permute-start | bytes 221192 | tf_op jit(solution)/shard_map/ppermute | solution.py:45
  6.4 3.1 %load_first.1 = (bf16[1536,2048]{1,0:T(8,128)(2,1)S(1)}, f32[8,128]{1,0:T(8,128)S(1)}) custom-call(bf16[4608,2048]{1,0:T(8,128)(2,1)} %refs_1_.3, bf16[8,4608]{1,0:T(8,128)(2,1)S(1)} %get-tuple-element.53.refs_1_), custom_call_target="tpu_custom_call" | custom-call | bytes 6291456 | tf_op jit(solution)/shard_map/load_first/pallas_call | solution.py:362
  9.5 0.0 collective-permute-done.refs_1_
  9.6 3.7 %collective-permute-start.3 = (bf16[8,5760]{1,0:T(8,128)(2,1)S(1)}, bf16[8,5760]{1,0:T(8,128)(2,1)S(1)}, u32[]{:S(2)}, u32[]{:S(2)}) collective-permute-start(bf16[8,5760]{1,0:T(8,128)(2,1)S(1)} %heads_y.1.refs_3_.refs_0_), channel_id=1, source_target_pairs={{0,6},{1,7},{2,4},{3,5},{4,2},{5,3},{6,0},{7,1},{8,14},{9,15},{10,... | collective-permute-start | bytes 276488 | tf_op jit(solution)/shard_map/ppermute | solution.py:45
  13.2 0.8 collective-permute-start.1
  14.0 6.3 %load_second.1 = (bf16[1536,2048]{1,0:T(8,128)(2,1)S(1)}, bf16[1536,2048]{1,0:T(8,128)(2,1)S(1)}, bf16[512,4608]{1,0:T(8,128)(2,1)S(1)}, f32[8,128]{1,0:T(8,128)S(1)}) custom-call(bf16[4608,2048]{1,0:T(8,128)(2,1)} %refs_1_.3, bf16[4608,2048]{1,0:T(8,128)(2,1)} %refs_1_.3, bf16[2048,4608]{1,0:T(8,128)(2,1)} %refs_8_.1, ...), custom_call_target="tpu_custom_call" | custom-call | bytes 17301504 | tf_op jit(solution)/shard_map/load_second/pallas_call | solution.py:362
  20.3 0.4 collective-permute-done.2.refs_2_
  20.7 0.2 residual.1.refs_1_.refs_0_
  20.9 0.0 copy-start
  20.9 1.9 %collective-permute-start.6 = (bf16[8,4608]{1,0:T(8,128)(2,1)S(1)}, bf16[8,4608]{1,0:T(8,128)(2,1)S(1)}, u32[]{:S(2)}, u32[]{:S(2)}) collective-permute-start(bf16[8,4608]{1,0:T(8,128)(2,1)S(1)} %residual.1.refs_1_.refs_0_), channel_id=1, source_target_pairs={{0,17},{1,16},{2,19},{3,18},{4,21},{5,20},{6,23},{7,22},{8,25},{9,... | collective-permute-start | bytes 221192 | tf_op jit(solution)/shard_map/ppermute | solution.py:45
  22.8 0.5 collective-permute-start.5
  23.3 1.1 %collective-permute-start.4 = (bf16[8,4608]{1,0:T(8,128)(2,1)S(1)}, bf16[8,4608]{1,0:T(8,128)(2,1)S(1)}, u32[]{:S(2)}, u32[]{:S(2)}) collective-permute-start(bf16[8,4608]{1,0:T(8,128)(2,1)S(1)} %residual.1.refs_1_.refs_0_), channel_id=1, source_target_pairs={{0,1},{1,0},{2,3},{3,2},{4,5},{5,4},{6,7},{7,6},{8,9},{9,8},{10,11... | collective-permute-start | bytes 221192 | tf_op jit(solution)/shard_map/ppermute | solution.py:45
  24.5 2.7 %load_third.1 = (bf16[512,4608]{1,0:T(8,128)(2,1)S(1)}, f32[8,128]{1,0:T(8,128)S(1)}) custom-call(bf16[2048,4608]{1,0:T(8,128)(2,1)} %refs_8_.1, bf16[8,4608]{1,0:T(8,128)(2,1)S(1)} %residual.1.refs_1_.refs_0_), custom_call_target="tpu_custom_call" | custom-call | bytes 4718592 | tf_op jit(solution)/shard_map/load_third/pallas_call | solution.py:362
  27.2 0.5 collective-permute-done.4.refs_0_
  27.7 0.1 collective-permute-start.8
  27.8 0.5 collective-permute-start.7
  28.3 1.1 %collective-permute-done.7.refs_2_ = bf16[8,4608]{1,0:T(8,128)(2,1)S(1)} collective-permute-done((bf16[8,4608]{1,0:T(8,128)(2,1)S(1)}, bf16[8,4608]{1,0:T(8,128)(2,1)S(1)}, u32[]{:S(2)}, u32[]{:S(2)}) %collective-permute-start.7) | collective-permute-done | bytes 73760 | tf_op jit(solution)/shard_map/ppermute | solution.py:45
  29.4 4.1 %encode.1 = (f32[64,2048]{1,0:T(8,128)S(1)}, bf16[64,4608]{1,0:T(8,128)(2,1)S(1)}, bf16[512,4608]{1,0:T(8,128)(2,1)S(1)}, bf16[512,4608]{1,0:T(8,128)(2,1)S(1)}) custom-call(bf16[8,4608]{1,0:T(8,128)(2,1)S(1)} %residual.1.refs_1_.refs_0_, bf16[24,4608]{1,0:T(8,128)(2,1)S(1)} %stack.2.refs_1_, bf16[8,4608]{1,0:T(8,128)(2,1)S(1)} %collective-permute-done.7.refs_2_, ...), custom_call_target="tpu_custom_call" | custom-call | flops 1207959552 | bytes 589824 | tf_op jit(solution)/shard_map/encode/pallas_call | solution.py:441
  33.5 3.4 %decode.1 = (f32[32,4608]{1,0:T(8,128)S(1)}, bf16[32,4608]{1,0:T(8,128)(2,1)S(1)}, bf16[2048,64]{1,0:T(8,128)(2,1)S(1)}, f32[512,1]{1,0:T(8,128)S(1)}, f32[512,1...) custom-call(f32[64,2048]{1,0:T(8,128)S(1)} %get-tuple-element.62.preact.refs_17_, ...), custom_call_target="tpu_custom_call" | custom-call | flops 1207959552 | bytes 1769472 | tf_op jit(solution)/shard_map/decode/pallas_call | solution.py:485
  36.9 0.2 collective-permute-start.9
  37.1 1.1 %norms.4 = (f32[512,1]{1,0:T(8,128)S(1)}, f32[1,512]{1,0:T(1,128)S(1)}, f32[8,128]{1,0:T(8,128)S(1)}) custom-call(bf16[512,4608]{1,0:T(8,128)(2,1)S(1)} %get-tuple-element.63.refs_0_.weight.refs_2_.refs_6_.refs_8_, f32[512,1]{1,0:T(8,128)S(1)} %get-tuple-element.69.usage, bf16[32,4608]{1,0:T(8,128)(2,1)S(1)} %get-tuple-element.68.after), custom_call_target="tpu_custom_call" | custom-call | bytes 14155776 | tf_op jit(solution)/shard_map/norms/pallas_call | solution.py:394
  38.2 0.3 collective-permute-done.9.refs_1_
  38.5 0.1 recon.2
  38.6 1.2 %collective-permute-start.10 = (bf16[32,1152]{1,0:T(8,128)(2,1)S(1)}, bf16[32,1152]{1,0:T(8,128)(2,1)S(1)}, u32[]{:S(2)}, u32[]{:S(2)}) collective-permute-start(bf16[32,1152]{1,0:T(8,128)(2,1)S(1)} %get-tuple-element.72), channel_id=1, source_target_pairs={{0,1},{1,0},{2,3},{3,2},{4,5},{5,4},{6,7},{7,6},{8,9},{9,8},{10,11... | collective-permute-start | bytes 221192 | tf_op jit(solution)/shard_map/ppermute | solution.py:45
  39.8 1.5 %collective-permute-start.11 = (bf16[32,1152]{1,0:T(8,128)(2,1)S(1)}, bf16[32,1152]{1,0:T(8,128)(2,1)S(1)}, u32[]{:S(2)}, u32[]{:S(2)}) collective-permute-start(bf16[32,1152]{1,0:T(8,128)(2,1)S(1)} %get-tuple-element.73), channel_id=1, source_target_pairs={{0,16},{1,17},{2,18},{3,19},{4,20},{5,21},{6,22},{7,23},{8,24},{9,... | collective-permute-start | bytes 221192 | tf_op jit(solution)/shard_map/ppermute | solution.py:45
  41.3 0.9 %collective-permute-start.12 = (bf16[32,1152]{1,0:T(8,128)(2,1)S(1)}, bf16[32,1152]{1,0:T(8,128)(2,1)S(1)}, u32[]{:S(2)}, u32[]{:S(2)}) collective-permute-start(bf16[32,1152]{1,0:T(8,128)(2,1)S(1)} %get-tuple-element.74), channel_id=1, source_target_pairs={{0,17},{1,16},{2,19},{3,18},{4,21},{5,20},{6,23},{7,22},{8,25},{9,... | collective-permute-start | bytes 221192 | tf_op jit(solution)/shard_map/ppermute | solution.py:45
  42.1 1.1 %norms.7 = (f32[512,1]{1,0:T(8,128)S(1)}, f32[1,512]{1,0:T(1,128)S(1)}, f32[8,128]{1,0:T(8,128)S(1)}) custom-call(bf16[512,4608]{1,0:T(8,128)(2,1)S(1)} %get-tuple-element.66.refs_3_.weight.refs_5_.refs_9_.refs_11_, f32[512,1]{1,0:T(8,128)S(1)} %get-tuple-element.79.usage, f32[32,1152]{1,0:T(8,128)S(1)} %get-tuple-element.71.after.refs_0_), custom_call_target="tpu_custom_call" | custom-call | bytes 14155776 | tf_op jit(solution)/shard_map/norms/pallas_call | solution.py:394
  43.2 1.1 %norms.6 = (f32[512,1]{1,0:T(8,128)S(1)}, f32[1,512]{1,0:T(1,128)S(1)}, f32[8,128]{1,0:T(8,128)S(1)}) custom-call(bf16[512,4608]{1,0:T(8,128)(2,1)S(1)} %get-tuple-element.65.refs_2_.weight.refs_4_.refs_8_.refs_10_, f32[512,1]{1,0:T(8,128)S(1)} %get-tuple-element.77.usage, f32[32,1152]{1,0:T(8,128)S(1)} %get-tuple-element.71.after.refs_0_), custom_call_target="tpu_custom_call" | custom-call | bytes 14155776 | tf_op jit(solution)/shard_map/norms/pallas_call | solution.py:394
  44.4 1.1 %norms.5 = (f32[512,1]{1,0:T(8,128)S(1)}, f32[1,512]{1,0:T(1,128)S(1)}, f32[8,128]{1,0:T(8,128)S(1)}) custom-call(bf16[512,4608]{1,0:T(8,128)(2,1)S(1)} %get-tuple-element.64.refs_1_.weight.refs_3_.refs_7_.refs_9_, f32[512,1]{1,0:T(8,128)S(1)} %get-tuple-element.75.usage, f32[32,1152]{1,0:T(8,128)S(1)} %get-tuple-element.71.after.refs_0_), custom_call_target="tpu_custom_call" | custom-call | bytes 14155776 | tf_op jit(solution)/shard_map/norms/pallas_call | solution.py:394
  45.5 1.1 %collective-permute-done.12.refs_3_ = bf16[32,1152]{1,0:T(8,128)(2,1)S(1)} collective-permute-done((bf16[32,1152]{1,0:T(8,128)(2,1)S(1)}, bf16[32,1152]{1,0:T(8,128)(2,1)S(1)}, u32[]{:S(2)}, u32[]{:S(2)}) %collective-permute-start.12) | collective-permute-done | bytes 73760 | tf_op jit(solution)/shard_map/ppermute | solution.py:45
  46.5 0.1 recon.3.after.refs_0_
  46.6 3.3 %collective-permute-start.15 = (bf16[8,4736]{1,0:T(8,128)(2,1)S(1)}, bf16[8,4736]{1,0:T(8,128)(2,1)S(1)}, u32[]{:S(2)}, u32[]{:S(2)}) collective-permute-start(bf16[8,4736]{1,0:T(8,128)(2,1)S(1)} %recon.3.after.refs_0_), channel_id=1, source_target_pairs={{0,6},{1,7},{2,4},{3,5},{4,2},{5,3},{6,0},{7,1},{8,14},{9,15},{10,... | collective-permute-start | bytes 227336 | tf_op jit(solution)/shard_map/ppermute | solution.py:45
  50.0 1.1 %collective-permute-start.13 = (bf16[8,4736]{1,0:T(8,128)(2,1)S(1)}, bf16[8,4736]{1,0:T(8,128)(2,1)S(1)}, u32[]{:S(2)}, u32[]{:S(2)}) collective-permute-start(bf16[8,4736]{1,0:T(8,128)(2,1)S(1)} %recon.3.after.refs_0_), channel_id=1, source_target_pairs={{0,2},{1,3},{2,0},{3,1},{4,6},{5,7},{6,4},{7,5},{8,10},{9,11},{10,... | collective-permute-start | bytes 227336 | tf_op jit(solution)/shard_map/ppermute | solution.py:45
  51.1 0.4 turn.1.refs_6_.refs_16_
  51.5 1.5 %collective-permute-done.15.refs_3_ = bf16[8,4736]{1,0:T(8,128)(2,1)S(1)} collective-permute-done((bf16[8,4736]{1,0:T(8,128)(2,1)S(1)}, bf16[8,4736]{1,0:T(8,128)(2,1)S(1)}, u32[]{:S(2)}, u32[]{:S(2)}) %collective-permute-start.15) | collective-permute-done | bytes 75808 | tf_op jit(solution)/shard_map/ppermute | solution.py:45
  53.0 2.6 %collective-permute-done.14.refs_2_ = bf16[8,4736]{1,0:T(8,128)(2,1)S(1)} collective-permute-done((bf16[8,4736]{1,0:T(8,128)(2,1)S(1)}, bf16[8,4736]{1,0:T(8,128)(2,1)S(1)}, u32[]{:S(2)}, u32[]{:S(2)}) %collective-permute-start.14) | collective-permute-done | bytes 75808 | tf_op jit(solution)/shard_map/ppermute | solution.py:45
  55.6 0.3 collective-permute-done.13.refs_1_
  55.9 0.1 error.1.refs_0_
  56.0 0.1 collective-permute-start.16
  56.1 1.4 %collective-permute-start.19 = (bf16[8,4736]{1,0:T(8,128)(2,1)S(1)}, bf16[8,4736]{1,0:T(8,128)(2,1)S(1)}, u32[]{:S(2)}, u32[]{:S(2)}) collective-permute-start(bf16[8,4736]{1,0:T(8,128)(2,1)S(1)} %error.1.refs_0_), channel_id=1, source_target_pairs={{0,17},{1,16},{2,19},{3,18},{4,21},{5,20},{6,23},{7,22},{8,25},{9,... | collective-permute-start | bytes 227336 | tf_op jit(solution)/shard_map/ppermute | solution.py:45
  57.5 1.0 %collective-permute-start.18 = (bf16[8,4736]{1,0:T(8,128)(2,1)S(1)}, bf16[8,4736]{1,0:T(8,128)(2,1)S(1)}, u32[]{:S(2)}, u32[]{:S(2)}) collective-permute-start(bf16[8,4736]{1,0:T(8,128)(2,1)S(1)} %error.1.refs_0_), channel_id=1, source_target_pairs={{0,16},{1,17},{2,18},{3,19},{4,20},{5,21},{6,22},{7,23},{8,24},{9,... | collective-permute-start | bytes 227336 | tf_op jit(solution)/shard_map/ppermute | solution.py:45
  58.5 1.1 %collective-permute-start.17 = (bf16[8,4736]{1,0:T(8,128)(2,1)S(1)}, bf16[8,4736]{1,0:T(8,128)(2,1)S(1)}, u32[]{:S(2)}, u32[]{:S(2)}) collective-permute-start(bf16[8,4736]{1,0:T(8,128)(2,1)S(1)} %error.1.refs_0_), channel_id=1, source_target_pairs={{0,1},{1,0},{2,3},{3,2},{4,5},{5,4},{6,7},{7,6},{8,9},{9,8},{10,11... | collective-permute-start | bytes 227336 | tf_op jit(solution)/shard_map/ppermute | solution.py:45
  59.6 1.5 %first_back.1.refs_11_.refs_19_ = f32[64,2048]{1,0:T(8,128)S(1)} custom-call(bf16[8,4736]{1,0:T(8,128)(2,1)S(1)} %error.1.refs_0_, bf16[8,4736]{1,0:T(8,128)(2,1)S(1)} %collective-permute-done.16.refs_1_, bf16[512,4608]{1,0:T(8,128)(2,1)S(1)} %get-tuple-element.63.refs_0_.weight.refs_2_.refs_6_.refs_8_, ...), custom_call_target="tpu_custom_call" | custom-call | flops 301989888 | bytes 9437184 | tf_op jit(solution)/shard_map/first_back/pallas_call | solution.py:567
  61.2 2.6 %first_outer.1 = (bf16[2048,4608]{1,0:T(8,128)(2,1)}, f32[8,128]{1,0:T(8,128)S(1)}) custom-call(bf16[8,4736]{1,0:T(8,128)(2,1)S(1)} %error.1.refs_0_, bf16[8,4736]{1,0:T(8,128)(2,1)S(1)} %collective-permute-done.16.refs_1_, f32[512,1]{1,0:T(8,128)S(1)} %get-tuple-element.83.refs_2_.refs_4_, f32[512,1]{1,0:T(8,128)S(1)} %get-tuple-element.84.refs_3_.refs_5_, ...), custom_call_target="tpu_custom_call" | custom-call | flops 301989888 | bytes 9437184 | tf_op jit(solution)/shard_map/first_outer/pallas_call | solution.py:609
  63.8 0.1 collective-permute-start.20
  63.9 1.5 %collective-permute-done.20.refs_3_ = bf16[24,4736]{1,0:T(8,128)(2,1)S(1)} collective-permute-done((bf16[24,4736]{1,0:T(8,128)(2,1)S(1)}, bf16[24,4736]{1,0:T(8,128)(2,1)S(1)}, u32[]{:S(2)}, u32[]{:S(2)}) %collective-permute-start.20) | collective-permute-done | bytes 227360 | tf_op jit(solution)/shard_map/ppermute | solution.py:45
  65.4 16.9 %gradients.1 = (bf16[2048,4608]{1,0:T(8,128)(2,1)}, bf16[4608,2048]{1,0:T(8,128)(2,1)}, f32[1,2048]{1,0:T(1,128)}, f32[4608]{0:T(1024)}, f32[1,1]{1,0:T(1,128)}) custom-call(bf16[8,4736]{1,0:T(8,128)(2,1)S(1)} %error.1.refs_0_, bf16[8,4736]{1,0:T(8,128)(2,1)S(1)} %collective-permute-done.16.refs_1_, ...), custom_call_target="tpu_custom_call", output_to_operand_aliasing={{0}: (20, {})} | custom-call | flops 3623878656 | bytes 37748736 | tf_op jit(solution)/shard_map/gradients/pallas_call | solution.py:733
  (17 shorter events, 0.1 us)
Async XLA Ops:
  3.4 6.2 %collective-permute-start = (bf16[8,4608]{1,0:T(8,128)(2,1)S(1)}, bf16[8,4608]{1,0:T(8,128)(2,1)S(1)}, u32[]{:S(2)}, u32[]{:S(2)}) collective-permute-start(bf16[8,4608]{1,0:T(8,128)(2,1)S(1)} %get-tuple-element.53.refs_1_), channel_id=1, source_target_pairs={{0,1},{1,0},{2,3},{3,2},{4,5},{5,4},{6,7},{7,6},{8,9},{9,8},{10,11... | collective-permute-start | bytes 221192 | tf_op jit(solution)/shard_map/ppermute | solution.py:45
  9.6 10.8 %collective-permute-start.3 = (bf16[8,5760]{1,0:T(8,128)(2,1)S(1)}, bf16[8,5760]{1,0:T(8,128)(2,1)S(1)}, u32[]{:S(2)}, u32[]{:S(2)}) collective-permute-start(bf16[8,5760]{1,0:T(8,128)(2,1)S(1)} %heads_y.1.refs_3_.refs_0_), channel_id=1, source_target_pairs={{0,6},{1,7},{2,4},{3,5},{4,2},{5,3},{6,0},{7,1},{8,14},{9,15},{10,... | collective-permute-start | bytes 276488 | tf_op jit(solution)/shard_map/ppermute | solution.py:45
  13.2 7.5 %collective-permute-start.2 = (bf16[8,5760]{1,0:T(8,128)(2,1)S(1)}, bf16[8,5760]{1,0:T(8,128)(2,1)S(1)}, u32[]{:S(2)}, u32[]{:S(2)}) collective-permute-start(bf16[8,5760]{1,0:T(8,128)(2,1)S(1)} %heads_y.1.refs_3_.refs_0_), channel_id=1, source_target_pairs={{0,4},{1,5},{2,6},{3,7},{4,0},{5,1},{6,2},{7,3},{8,12},{9,13},{10,... | collective-permute-start | bytes 276488 | tf_op jit(solution)/shard_map/ppermute | solution.py:45
  13.2 7.5 %collective-permute-start.1 = (bf16[8,5760]{1,0:T(8,128)(2,1)S(1)}, bf16[8,5760]{1,0:T(8,128)(2,1)S(1)}, u32[]{:S(2)}, u32[]{:S(2)}) collective-permute-start(bf16[8,5760]{1,0:T(8,128)(2,1)S(1)} %heads_y.1.refs_3_.refs_0_), channel_id=1, source_target_pairs={{0,2},{1,3},{2,0},{3,1},{4,6},{5,7},{6,4},{7,5},{8,10},{9,11},{10,... | collective-permute-start | bytes 276488 | tf_op jit(solution)/shard_map/ppermute | solution.py:45
  20.9 8.4 %copy-start = (f32[2048]{0:T(1024)S(1)}, f32[2048]{0:T(1024)}, u32[]{:S(2)}) copy-start(f32[2048]{0:T(1024)} %refs_7_.1) | copy-start | bytes 24580
  20.9 6.2 %collective-permute-start.6 = (bf16[8,4608]{1,0:T(8,128)(2,1)S(1)}, bf16[8,4608]{1,0:T(8,128)(2,1)S(1)}, u32[]{:S(2)}, u32[]{:S(2)}) collective-permute-start(bf16[8,4608]{1,0:T(8,128)(2,1)S(1)} %residual.1.refs_1_.refs_0_), channel_id=1, source_target_pairs={{0,17},{1,16},{2,19},{3,18},{4,21},{5,20},{6,23},{7,22},{8,25},{9,... | collective-permute-start | bytes 221192 | tf_op jit(solution)/shard_map/ppermute | solution.py:45
  22.8 4.4 %collective-permute-start.5 = (bf16[8,4608]{1,0:T(8,128)(2,1)S(1)}, bf16[8,4608]{1,0:T(8,128)(2,1)S(1)}, u32[]{:S(2)}, u32[]{:S(2)}) collective-permute-start(bf16[8,4608]{1,0:T(8,128)(2,1)S(1)} %residual.1.refs_1_.refs_0_), channel_id=1, source_target_pairs={{0,16},{1,17},{2,18},{3,19},{4,20},{5,21},{6,22},{7,23},{8,24},{9,... | collective-permute-start | bytes 221192 | tf_op jit(solution)/shard_map/ppermute | solution.py:45
  23.3 4.4 %collective-permute-start.4 = (bf16[8,4608]{1,0:T(8,128)(2,1)S(1)}, bf16[8,4608]{1,0:T(8,128)(2,1)S(1)}, u32[]{:S(2)}, u32[]{:S(2)}) collective-permute-start(bf16[8,4608]{1,0:T(8,128)(2,1)S(1)} %residual.1.refs_1_.refs_0_), channel_id=1, source_target_pairs={{0,1},{1,0},{2,3},{3,2},{4,5},{5,4},{6,7},{7,6},{8,9},{9,8},{10,11... | collective-permute-start | bytes 221192 | tf_op jit(solution)/shard_map/ppermute | solution.py:45
  27.7 1.7 %collective-permute-start.8 = (bf16[24,4608]{1,0:T(8,128)(2,1)S(1)}, bf16[24,4608]{1,0:T(8,128)(2,1)S(1)}, u32[]{:S(2)}, u32[]{:S(2)}) collective-permute-start(bf16[24,4608]{1,0:T(8,128)(2,1)S(1)} %stack.2.refs_1_), channel_id=1, source_target_pairs={{0,8},{1,9},{2,10},{3,11},{4,12},{5,13},{6,14},{7,15},{8,0},{9,1},... | collective-permute-start | bytes 663560 | tf_op jit(solution)/shard_map/ppermute | solution.py:45
  27.8 1.6 %collective-permute-start.7 = (bf16[8,4608]{1,0:T(8,128)(2,1)S(1)}, bf16[8,4608]{1,0:T(8,128)(2,1)S(1)}, u32[]{:S(2)}, u32[]{:S(2)}) collective-permute-start(bf16[8,4608]{1,0:T(8,128)(2,1)S(1)} %residual.1.refs_1_.refs_0_), channel_id=1, source_target_pairs={{0,8},{1,9},{2,10},{3,11},{4,12},{5,13},{6,14},{7,15},{8,0},{9,1},... | collective-permute-start | bytes 221192 | tf_op jit(solution)/shard_map/ppermute | solution.py:45
  36.9 1.6 %collective-permute-start.9 = (bf16[32,4608]{1,0:T(8,128)(2,1)S(1)}, bf16[32,4608]{1,0:T(8,128)(2,1)S(1)}, u32[]{:S(2)}, u32[]{:S(2)}) collective-permute-start(bf16[32,4608]{1,0:T(8,128)(2,1)S(1)} %get-tuple-element.68.after), channel_id=1, source_target_pairs={{0,8},{1,9},{2,10},{3,11},{4,12},{5,13},{6,14},{7,15},{8,0},{9,1},... | collective-permute-start | bytes 884744 | tf_op jit(solution)/shard_map/ppermute | solution.py:45
  38.6 6.9 %collective-permute-start.10 = (bf16[32,1152]{1,0:T(8,128)(2,1)S(1)}, bf16[32,1152]{1,0:T(8,128)(2,1)S(1)}, u32[]{:S(2)}, u32[]{:S(2)}) collective-permute-start(bf16[32,1152]{1,0:T(8,128)(2,1)S(1)} %get-tuple-element.72), channel_id=1, source_target_pairs={{0,1},{1,0},{2,3},{3,2},{4,5},{5,4},{6,7},{7,6},{8,9},{9,8},{10,11... | collective-permute-start | bytes 221192 | tf_op jit(solution)/shard_map/ppermute | solution.py:45
  39.8 5.7 %collective-permute-start.11 = (bf16[32,1152]{1,0:T(8,128)(2,1)S(1)}, bf16[32,1152]{1,0:T(8,128)(2,1)S(1)}, u32[]{:S(2)}, u32[]{:S(2)}) collective-permute-start(bf16[32,1152]{1,0:T(8,128)(2,1)S(1)} %get-tuple-element.73), channel_id=1, source_target_pairs={{0,16},{1,17},{2,18},{3,19},{4,20},{5,21},{6,22},{7,23},{8,24},{9,... | collective-permute-start | bytes 221192 | tf_op jit(solution)/shard_map/ppermute | solution.py:45
  41.3 5.3 %collective-permute-start.12 = (bf16[32,1152]{1,0:T(8,128)(2,1)S(1)}, bf16[32,1152]{1,0:T(8,128)(2,1)S(1)}, u32[]{:S(2)}, u32[]{:S(2)}) collective-permute-start(bf16[32,1152]{1,0:T(8,128)(2,1)S(1)} %get-tuple-element.74), channel_id=1, source_target_pairs={{0,17},{1,16},{2,19},{3,18},{4,21},{5,20},{6,23},{7,22},{8,25},{9,... | collective-permute-start | bytes 221192 | tf_op jit(solution)/shard_map/ppermute | solution.py:45
  46.6 6.3 %collective-permute-start.15 = (bf16[8,4736]{1,0:T(8,128)(2,1)S(1)}, bf16[8,4736]{1,0:T(8,128)(2,1)S(1)}, u32[]{:S(2)}, u32[]{:S(2)}) collective-permute-start(bf16[8,4736]{1,0:T(8,128)(2,1)S(1)} %recon.3.after.refs_0_), channel_id=1, source_target_pairs={{0,6},{1,7},{2,4},{3,5},{4,2},{5,3},{6,0},{7,1},{8,14},{9,15},{10,... | collective-permute-start | bytes 227336 | tf_op jit(solution)/shard_map/ppermute | solution.py:45
  50.0 5.6 %collective-permute-start.14 = (bf16[8,4736]{1,0:T(8,128)(2,1)S(1)}, bf16[8,4736]{1,0:T(8,128)(2,1)S(1)}, u32[]{:S(2)}, u32[]{:S(2)}) collective-permute-start(bf16[8,4736]{1,0:T(8,128)(2,1)S(1)} %recon.3.after.refs_0_), channel_id=1, source_target_pairs={{0,4},{1,5},{2,6},{3,7},{4,0},{5,1},{6,2},{7,3},{8,12},{9,13},{10,... | collective-permute-start | bytes 227336 | tf_op jit(solution)/shard_map/ppermute | solution.py:45
  50.0 5.9 %collective-permute-start.13 = (bf16[8,4736]{1,0:T(8,128)(2,1)S(1)}, bf16[8,4736]{1,0:T(8,128)(2,1)S(1)}, u32[]{:S(2)}, u32[]{:S(2)}) collective-permute-start(bf16[8,4736]{1,0:T(8,128)(2,1)S(1)} %recon.3.after.refs_0_), channel_id=1, source_target_pairs={{0,2},{1,3},{2,0},{3,1},{4,6},{5,7},{6,4},{7,5},{8,10},{9,11},{10,... | collective-permute-start | bytes 227336 | tf_op jit(solution)/shard_map/ppermute | solution.py:45
  56.0 3.6 %collective-permute-start.16 = (bf16[8,4736]{1,0:T(8,128)(2,1)S(1)}, bf16[8,4736]{1,0:T(8,128)(2,1)S(1)}, u32[]{:S(2)}, u32[]{:S(2)}) collective-permute-start(bf16[8,4736]{1,0:T(8,128)(2,1)S(1)} %error.1.refs_0_), channel_id=1, source_target_pairs={{0,8},{1,9},{2,10},{3,11},{4,12},{5,13},{6,14},{7,15},{8,0},{9,1},... | collective-permute-start | bytes 227336 | tf_op jit(solution)/shard_map/ppermute | solution.py:45
  56.1 7.7 %collective-permute-start.19 = (bf16[8,4736]{1,0:T(8,128)(2,1)S(1)}, bf16[8,4736]{1,0:T(8,128)(2,1)S(1)}, u32[]{:S(2)}, u32[]{:S(2)}) collective-permute-start(bf16[8,4736]{1,0:T(8,128)(2,1)S(1)} %error.1.refs_0_), channel_id=1, source_target_pairs={{0,17},{1,16},{2,19},{3,18},{4,21},{5,20},{6,23},{7,22},{8,25},{9,... | collective-permute-start | bytes 227336 | tf_op jit(solution)/shard_map/ppermute | solution.py:45
  57.5 6.3 %collective-permute-start.18 = (bf16[8,4736]{1,0:T(8,128)(2,1)S(1)}, bf16[8,4736]{1,0:T(8,128)(2,1)S(1)}, u32[]{:S(2)}, u32[]{:S(2)}) collective-permute-start(bf16[8,4736]{1,0:T(8,128)(2,1)S(1)} %error.1.refs_0_), channel_id=1, source_target_pairs={{0,16},{1,17},{2,18},{3,19},{4,20},{5,21},{6,22},{7,23},{8,24},{9,... | collective-permute-start | bytes 227336 | tf_op jit(solution)/shard_map/ppermute | solution.py:45
  58.5 5.3 %collective-permute-start.17 = (bf16[8,4736]{1,0:T(8,128)(2,1)S(1)}, bf16[8,4736]{1,0:T(8,128)(2,1)S(1)}, u32[]{:S(2)}, u32[]{:S(2)}) collective-permute-start(bf16[8,4736]{1,0:T(8,128)(2,1)S(1)} %error.1.refs_0_), channel_id=1, source_target_pairs={{0,1},{1,0},{2,3},{3,2},{4,5},{5,4},{6,7},{7,6},{8,9},{9,8},{10,11... | collective-permute-start | bytes 227336 | tf_op jit(solution)/shard_map/ppermute | solution.py:45
  63.8 1.6 %collective-permute-start.20 = (bf16[24,4736]{1,0:T(8,128)(2,1)S(1)}, bf16[24,4736]{1,0:T(8,128)(2,1)S(1)}, u32[]{:S(2)}, u32[]{:S(2)}) collective-permute-start(bf16[24,4736]{1,0:T(8,128)(2,1)S(1)} %stack.3.refs_2_), channel_id=1, source_target_pairs={{0,8},{1,9},{2,10},{3,11},{4,12},{5,13},{6,14},{7,15},{8,0},{9,1},... | collective-permute-start | bytes 681992 | tf_op jit(solution)/shard_map/ppermute | solution.py:45

commit v4 on v3

--- a/solution.py
+++ b/solution.py
@@ -196,9 +196,10 @@
     features = gain.shape[1]
     count = len(parts)
     own, quarter = rows // count, features // count
-
-    def kernel(*refs):
-        sums, gain, out = refs[:count], refs[count], refs[-1]
+    parts, places = in_turn(parts)
+
+    def kernel(*refs):
+        sums, gain, out = [refs[i] for i in places], refs[count], refs[-1]
         projected = group_sum([p[:, :features].astype(F32) for p in sums], own)
         scale = lax.rsqrt(jnp.mean(projected * projected, axis=-1, keepdims=True) + EPSILON)
         packed = [p[:, features:].astype(F32) for p in sums]
@@ -290,7 +291,13 @@
     return terms[0]
 
 
+def in_turn(parts):
+    order = [0, 1, 3, 2] if len(parts) == 4 else list(range(len(parts)))
+    return [parts[i] for i in order], [order.index(i) for i in range(len(parts))]
+
+
 def error_of(parts, resid, bias, group, rows, after):
+    parts, places = in_turn(parts)
     height, length = parts[0].shape
     length -= LANES
     width = resid.shape[1] // group.size
@@ -298,6 +305,7 @@
     def kernel(*refs):
         sums, resid, bias, out = refs[: len(parts)], refs[len(parts)], refs[len(parts) + 1], refs[-1]
         at = pl.ds(chunk_at(group, group.keys[0], width), width)
+        sums = [sums[i] for i in places]
         total = unlaid(tree([p[:, :length].astype(F32) for p in sums]), rows, width)
         lay(out, (total + bias[:, at] - resid[:rows, at].astype(F32)).astype(BF16))
         put_number(out, length, tree([get_number(p, length) for p in sums]))
@@ -540,6 +548,10 @@
     return [(c, min(wide, width - c)) for c in range(0, width, wide)]
 
 
+def whole_tiles(width):
+    return width // 256 * 256
+
+
 def outer(latents_t, error, coef, weight):
     return (jnp.dot(latents_t, error, preferred_element_type=F32) + coef * weight.astype(F32)).astype(BF16)
 
@@ -632,6 +644,8 @@
     span = math.gcd(latents, 512)
     deep = block_of(features, 1152)
     dec_slots, enc_slots = 3, 6
+    main = whole_tiles(width)
+    half = math.gcd(span, 256)
     flat = first + others
 
     def kernel(*refs):
@@ -640,10 +654,13 @@
         refs = refs[len(flat) :]
         coef, held, norm_row, refs = refs[:count], refs[count : 2 * count], refs[2 * count : 3 * count], refs[3 * count :]
         (resid_t, preact, latents_t, back, _, dec_grad, enc_grad, bias_grad, column_sum, loss,
-         error, pulled, sums, dec_stage, enc_stage, dec_sem, enc_sem) = refs
+         error, ends, pulled, sums, dec_stage, enc_stage, dec_sem, enc_sem) = refs
         columns = [chunk_at(group, key, width) for key in group.keys]
         for k in range(size):
             assemble(chunks[k], error.at[k], width)
+        for k in range(1, size):
+            if main < width:
+                ends[:, (k - 1) * (width - main) : k * (width - main)] = error[k, :, main:]
         where = row_blocks(held, rows)
         dec_copies, enc_copies = [], []
 
@@ -652,13 +669,26 @@
             at, inside = slice(i * rows, (i + 1) * rows), slice(r, r + rows)
             total = back[:, at]
             for k in range(1, size):
-                for c, wide in spans(width):
+                for c, wide in spans(main):
                     part = error[k, :, c : c + wide]
                     weight = held[p][inside, pl.ds(pl.multiple_of(columns[k] + c, LANES), wide)]
                     dec_stage[i % dec_slots, k - 1, :, c : c + wide] = outer(
                         latents_t[at, :], part, coef[p][inside, :], weight
                     )
                     total = total + back_product(part, weight)
+            if main < width and size > 1:
+                weight = jnp.concatenate(
+                    [
+                        held[p][inside, pl.ds(pl.multiple_of(columns[k] + main, LANES), width - main)]
+                        for k in range(1, size)
+                    ],
+                    axis=1,
+                )
+                product = outer(latents_t[at, :], ends[...], coef[p][inside, :], weight)
+                for k in range(1, size):
+                    over = slice((k - 1) * (width - main), k * (width - main))
+                    dec_stage[i % dec_slots, k - 1, :, main:] = product[:, over]
+                total = total + back_product(ends[...], weight)
             total = (total + SPARSITY * norm_row[p][:, inside]) * jax.nn.sigmoid(preact[:, at] / SMOOTHING)
             bias_grad[:, at] = jnp.sum(total, axis=0, keepdims=True)
             pulled[:, at] = total.astype(BF16)
@@ -678,9 +708,14 @@
 
         def block(n):
             first, j = blocks[n]
-            enc_stage[n % enc_slots] = jnp.dot(
-                resid_t[j : j + deep, :], pulled[:, first : first + span], preferred_element_type=F32
-            ).astype(BF16)
+            part = block_of(deep, 384)
+            for r in range(0, deep, part):
+                for c in range(0, span, half):
+                    enc_stage[n % enc_slots, r : r + part, c : c + half] = jnp.dot(
+                        resid_t[j + r : j + r + part, :],
+                        pulled[:, first + c : first + c + half],
+                        preferred_element_type=F32,
+                    ).astype(BF16)
 
         def send_block(n):
             (first, j), slot = blocks[n], n % enc_slots
@@ -743,6 +778,7 @@
         ],
         scratch_shapes=[
             pltpu.VMEM((size, tokens, width), BF16),
+            pltpu.VMEM((tokens, max(size - 1, 1) * max(width - main, LANES)), BF16),
             pltpu.VMEM((tokens, latents), BF16),
             pltpu.VMEM((1, features), F32),
             pltpu.VMEM((dec_slots, max(size - 1, 1), rows, width), BF16),
@@ -819,7 +855,7 @@
         found += [norms(w, u, keep) for w, u in zip(held[1:], used[1:])]
         coefs, norm_rows, penalties = [list(x) for x in zip(*found)]
         rows = keep.shape[0]
-        keep = with_penalty(keep, got, penalties)
+        keep = with_penalty(keep, got[::-1], penalties)
         sums = deep.spread(keep)
         resid_t = turn(resid_all, keep)
         error_own = error_of(sums, resid_all, bias, by_feature, rows, [resid_t])

time: 82.7 us -> 81.6 us (0.987)
  transfers between devices with their start and end apart: 21 -> 21, of which waited for: 9 -> 8; matrix products, arithmetic and copies ran while one was open for 0% -> 0% of each run, Pallas kernels for 26% -> 26%
where the time goes in v4:
time: 81.6 us; the launch traced here: 81.4 us
  Pallas kernels  48.4 us (59%)
  starting transfers between devices  23.1 us (28%)
  waiting for transfers between devices  8.81 us (11%)
  between operations  1.04 us (1%)
    ppermute x21, starting transfers between devices, swap(): return lax.ppermute(x, ('dp', 'fsdp'), pairs)  23.1 us
    pallas_call x1, Pallas kernels, gradients(): pl.pallas_call(kernel, in_specs=resident(len(flat) + 3 * count + 4) + any...  16.6 us
    pallas_call x3, Pallas kernels, load(): pl.pallas_call(kernel, in_specs=anywhere(len(items)) + resident(1), out_s...  12.1 us
    ppermute x21, waiting for transfers between devices, swap(): return lax.ppermute(x, ('dp', 'fsdp'), pairs)  8.81 us
    pallas_call x4, Pallas kernels, norms(): pl.pallas_call(kernel, in_specs=resident(3), out_specs=resident(3), out_s...  4.44 us
    pallas_call x1, Pallas kernels, encode(): pl.pallas_call(kernel, in_specs=resident(len(parts) + len(held) + 1) + an...  4.11 us
    pallas_call x1, Pallas kernels, decode(): pl.pallas_call(kernel, in_specs=resident(1 + count), out_specs=resident(3...  3.36 us
    pallas_call x1, Pallas kernels, project(): pl.pallas_call(kernel, in_specs=anywhere(5), out_specs=resident(3 + side....  2.73 us
  transfers between devices with their start and end apart: 21, of which 8 were waited for; matrix products, arithmetic and copies ran while one was open for 0% of the time, Pallas kernels for 26%

profile of v4, /device:TPU:0, one launch (start us, length us, event | category | flops | bytes accessed | tf_op | source)
XLA Modules:
  0.0 81.4 jit_solution(13712431065093725278)
XLA Ops:
  0.6 2.7 %project.1 = (bf16[8,1152]{1,0:T(8,128)(2,1)S(1)}, f32[1,4608]{1,0:T(1,128)S(1)}, f32[1,4608]{1,0:T(1,128)S(1)}, f32[8,4608]{1,0:T(8,128)S(1)}, bf16[8,4608]{1,0:T(8,128)(2,1)S(1)}) custom-call(bf16[16,512]{1,0:T(8,128)(2,1)} %refs_0_.4, bf16[512,4608]{1,0:T(8,128)(2,1)} %refs_1_.2, bf16[2,4608]{1,0:T(2,128)(2,1)} %refs_2_.2, f32[4608]{0:T(1024)} %refs_3_.1, ...), custom_call_target="tpu_custom_call" | custom-call | flops 75497472 | bytes 4718592 | tf_op jit(solution)/shard_map/project/pallas_call | solution.py:147
  3.4 3.0 %collective-permute-start = (bf16[8,4608]{1,0:T(8,128)(2,1)S(1)}, bf16[8,4608]{1,0:T(8,128)(2,1)S(1)}, u32[]{:S(2)}, u32[]{:S(2)}) collective-permute-start(bf16[8,4608]{1,0:T(8,128)(2,1)S(1)} %get-tuple-element.53.refs_1_), channel_id=1, source_target_pairs={{0,1},{1,0},{2,3},{3,2},{4,5},{5,4},{6,7},{7,6},{8,9},{9,8},{10,11... | collective-permute-start | bytes 221192 | tf_op jit(solution)/shard_map/ppermute | solution.py:45
  6.4 3.1 %load_first.1 = (bf16[1536,2048]{1,0:T(8,128)(2,1)S(1)}, f32[8,128]{1,0:T(8,128)S(1)}) custom-call(bf16[4608,2048]{1,0:T(8,128)(2,1)} %refs_1_.3, bf16[8,4608]{1,0:T(8,128)(2,1)S(1)} %get-tuple-element.53.refs_1_), custom_call_target="tpu_custom_call" | custom-call | bytes 6291456 | tf_op jit(solution)/shard_map/load_first/pallas_call | solution.py:370
  9.6 2.7 %collective-permute-start.3 = (bf16[8,5760]{1,0:T(8,128)(2,1)S(1)}, bf16[8,5760]{1,0:T(8,128)(2,1)S(1)}, u32[]{:S(2)}, u32[]{:S(2)}) collective-permute-start(bf16[8,5760]{1,0:T(8,128)(2,1)S(1)} %heads_y.1.refs_3_.refs_0_), channel_id=1, source_target_pairs={{0,4},{1,5},{2,6},{3,7},{4,0},{5,1},{6,2},{7,3},{8,12},{9,13},{10,... | collective-permute-start | bytes 276488 | tf_op jit(solution)/shard_map/ppermute | solution.py:45
  12.2 1.3 %collective-permute-start.2 = (bf16[8,5760]{1,0:T(8,128)(2,1)S(1)}, bf16[8,5760]{1,0:T(8,128)(2,1)S(1)}, u32[]{:S(2)}, u32[]{:S(2)}) collective-permute-start(bf16[8,5760]{1,0:T(8,128)(2,1)S(1)} %heads_y.1.refs_3_.refs_0_), channel_id=1, source_target_pairs={{0,6},{1,7},{2,4},{3,5},{4,2},{5,3},{6,0},{7,1},{8,14},{9,15},{10,... | collective-permute-start | bytes 276488 | tf_op jit(solution)/shard_map/ppermute | solution.py:45
  13.6 0.2 collective-permute-start.1
  13.8 6.3 %load_second.1 = (bf16[1536,2048]{1,0:T(8,128)(2,1)S(1)}, bf16[1536,2048]{1,0:T(8,128)(2,1)S(1)}, bf16[512,4608]{1,0:T(8,128)(2,1)S(1)}, f32[8,128]{1,0:T(8,128)S(1)}) custom-call(bf16[4608,2048]{1,0:T(8,128)(2,1)} %refs_1_.3, bf16[4608,2048]{1,0:T(8,128)(2,1)} %refs_1_.3, bf16[2048,4608]{1,0:T(8,128)(2,1)} %refs_8_.1, ...), custom_call_target="tpu_custom_call" | custom-call | bytes 17301504 | tf_op jit(solution)/shard_map/load_second/pallas_call | solution.py:370
  20.1 0.2 residual.1.refs_1_.refs_0_
  20.4 0.0 copy-start
  20.4 2.2 %collective-permute-start.6 = (bf16[8,4608]{1,0:T(8,128)(2,1)S(1)}, bf16[8,4608]{1,0:T(8,128)(2,1)S(1)}, u32[]{:S(2)}, u32[]{:S(2)}) collective-permute-start(bf16[8,4608]{1,0:T(8,128)(2,1)S(1)} %residual.1.refs_1_.refs_0_), channel_id=1, source_target_pairs={{0,17},{1,16},{2,19},{3,18},{4,21},{5,20},{6,23},{7,22},{8,25},{9,... | collective-permute-start | bytes 221192 | tf_op jit(solution)/shard_map/ppermute | solution.py:45
  22.6 0.5 collective-permute-start.5
  23.1 0.8 collective-permute-start.4
  23.9 2.7 %load_third.1 = (bf16[512,4608]{1,0:T(8,128)(2,1)S(1)}, f32[8,128]{1,0:T(8,128)S(1)}) custom-call(bf16[2048,4608]{1,0:T(8,128)(2,1)} %refs_8_.1, bf16[8,4608]{1,0:T(8,128)(2,1)S(1)} %residual.1.refs_1_.refs_0_), custom_call_target="tpu_custom_call" | custom-call | bytes 4718592 | tf_op jit(solution)/shard_map/load_third/pallas_call | solution.py:370
  26.6 0.3 collective-permute-done.5.refs_1_
  26.9 0.5 collective-permute-done.4.refs_0_
  27.5 0.1 collective-permute-start.8
  27.6 0.5 collective-permute-start.7
  28.1 1.1 %collective-permute-done.7.refs_2_ = bf16[8,4608]{1,0:T(8,128)(2,1)S(1)} collective-permute-done((bf16[8,4608]{1,0:T(8,128)(2,1)S(1)}, bf16[8,4608]{1,0:T(8,128)(2,1)S(1)}, u32[]{:S(2)}, u32[]{:S(2)}) %collective-permute-start.7) | collective-permute-done | bytes 73760 | tf_op jit(solution)/shard_map/ppermute | solution.py:45
  29.2 4.1 %encode.1 = (f32[64,2048]{1,0:T(8,128)S(1)}, bf16[64,4608]{1,0:T(8,128)(2,1)S(1)}, bf16[512,4608]{1,0:T(8,128)(2,1)S(1)}, bf16[512,4608]{1,0:T(8,128)(2,1)S(1)}) custom-call(bf16[8,4608]{1,0:T(8,128)(2,1)S(1)} %residual.1.refs_1_.refs_0_, bf16[24,4608]{1,0:T(8,128)(2,1)S(1)} %stack.2.refs_1_, bf16[8,4608]{1,0:T(8,128)(2,1)S(1)} %collective-permute-done.7.refs_2_, ...), custom_call_target="tpu_custom_call" | custom-call | flops 1207959552 | bytes 589824 | tf_op jit(solution)/shard_map/encode/pallas_call | solution.py:449
  33.3 3.4 %decode.1 = (f32[32,4608]{1,0:T(8,128)S(1)}, bf16[32,4608]{1,0:T(8,128)(2,1)S(1)}, bf16[2048,64]{1,0:T(8,128)(2,1)S(1)}, f32[512,1]{1,0:T(8,128)S(1)}, f32[512,1...) custom-call(f32[64,2048]{1,0:T(8,128)S(1)} %get-tuple-element.62.preact.refs_17_, ...), custom_call_target="tpu_custom_call" | custom-call | flops 1207959552 | bytes 1769472 | tf_op jit(solution)/shard_map/decode/pallas_call | solution.py:493
  36.6 0.2 collective-permute-start.9
  36.9 1.1 %norms.4 = (f32[512,1]{1,0:T(8,128)S(1)}, f32[1,512]{1,0:T(1,128)S(1)}, f32[8,128]{1,0:T(8,128)S(1)}) custom-call(bf16[512,4608]{1,0:T(8,128)(2,1)S(1)} %get-tuple-element.63.refs_0_.weight.refs_2_.refs_6_.refs_8_, f32[512,1]{1,0:T(8,128)S(1)} %get-tuple-element.69.usage, bf16[32,4608]{1,0:T(8,128)(2,1)S(1)} %get-tuple-element.68.after), custom_call_target="tpu_custom_call" | custom-call | bytes 14155776 | tf_op jit(solution)/shard_map/norms/pallas_call | solution.py:402
  38.0 0.3 collective-permute-done.9.refs_1_
  38.3 0.1 recon.2
  38.4 1.8 %collective-permute-start.10 = (bf16[32,1152]{1,0:T(8,128)(2,1)S(1)}, bf16[32,1152]{1,0:T(8,128)(2,1)S(1)}, u32[]{:S(2)}, u32[]{:S(2)}) collective-permute-start(bf16[32,1152]{1,0:T(8,128)(2,1)S(1)} %get-tuple-element.72), channel_id=1, source_target_pairs={{0,17},{1,16},{2,19},{3,18},{4,21},{5,20},{6,23},{7,22},{8,25},{9,... | collective-permute-start | bytes 221192 | tf_op jit(solution)/shard_map/ppermute | solution.py:45
  40.2 0.5 collective-permute-start.11
  40.7 1.2 %collective-permute-start.12 = (bf16[32,1152]{1,0:T(8,128)(2,1)S(1)}, bf16[32,1152]{1,0:T(8,128)(2,1)S(1)}, u32[]{:S(2)}, u32[]{:S(2)}) collective-permute-start(bf16[32,1152]{1,0:T(8,128)(2,1)S(1)} %get-tuple-element.74), channel_id=1, source_target_pairs={{0,1},{1,0},{2,3},{3,2},{4,5},{5,4},{6,7},{7,6},{8,9},{9,8},{10,11... | collective-permute-start | bytes 221192 | tf_op jit(solution)/shard_map/ppermute | solution.py:45
  41.9 1.1 %norms.7 = (f32[512,1]{1,0:T(8,128)S(1)}, f32[1,512]{1,0:T(1,128)S(1)}, f32[8,128]{1,0:T(8,128)S(1)}) custom-call(bf16[512,4608]{1,0:T(8,128)(2,1)S(1)} %get-tuple-element.66.refs_3_.weight.refs_5_.refs_9_.refs_11_, f32[512,1]{1,0:T(8,128)S(1)} %get-tuple-element.79.usage, f32[32,1152]{1,0:T(8,128)S(1)} %get-tuple-element.71.after.refs_0_), custom_call_target="tpu_custom_call" | custom-call | bytes 14155776 | tf_op jit(solution)/shard_map/norms/pallas_call | solution.py:402
  43.0 1.1 %norms.6 = (f32[512,1]{1,0:T(8,128)S(1)}, f32[1,512]{1,0:T(1,128)S(1)}, f32[8,128]{1,0:T(8,128)S(1)}) custom-call(bf16[512,4608]{1,0:T(8,128)(2,1)S(1)} %get-tuple-element.65.refs_2_.weight.refs_4_.refs_8_.refs_10_, f32[512,1]{1,0:T(8,128)S(1)} %get-tuple-element.77.usage, f32[32,1152]{1,0:T(8,128)S(1)} %get-tuple-element.71.after.refs_0_), custom_call_target="tpu_custom_call" | custom-call | bytes 14155776 | tf_op jit(solution)/shard_map/norms/pallas_call | solution.py:402
  44.1 1.1 %norms.5 = (f32[512,1]{1,0:T(8,128)S(1)}, f32[1,512]{1,0:T(1,128)S(1)}, f32[8,128]{1,0:T(8,128)S(1)}) custom-call(bf16[512,4608]{1,0:T(8,128)(2,1)S(1)} %get-tuple-element.64.refs_1_.weight.refs_3_.refs_7_.refs_9_, f32[512,1]{1,0:T(8,128)S(1)} %get-tuple-element.75.usage, f32[32,1152]{1,0:T(8,128)S(1)} %get-tuple-element.71.after.refs_0_), custom_call_target="tpu_custom_call" | custom-call | bytes 14155776 | tf_op jit(solution)/shard_map/norms/pallas_call | solution.py:402
  45.3 0.0 collective-permute-done.12.refs_3_
  45.3 0.1 recon.3.after.refs_0_
  45.4 2.9 %collective-permute-start.15 = (bf16[8,4736]{1,0:T(8,128)(2,1)S(1)}, bf16[8,4736]{1,0:T(8,128)(2,1)S(1)}, u32[]{:S(2)}, u32[]{:S(2)}) collective-permute-start(bf16[8,4736]{1,0:T(8,128)(2,1)S(1)} %recon.3.after.refs_0_), channel_id=1, source_target_pairs={{0,4},{1,5},{2,6},{3,7},{4,0},{5,1},{6,2},{7,3},{8,12},{9,13},{10,... | collective-permute-start | bytes 227336 | tf_op jit(solution)/shard_map/ppermute | solution.py:45
  48.3 1.3 %collective-permute-start.14 = (bf16[8,4736]{1,0:T(8,128)(2,1)S(1)}, bf16[8,4736]{1,0:T(8,128)(2,1)S(1)}, u32[]{:S(2)}, u32[]{:S(2)}) collective-permute-start(bf16[8,4736]{1,0:T(8,128)(2,1)S(1)} %recon.3.after.refs_0_), channel_id=1, source_target_pairs={{0,6},{1,7},{2,4},{3,5},{4,2},{5,3},{6,0},{7,1},{8,14},{9,15},{10,... | collective-permute-start | bytes 227336 | tf_op jit(solution)/shard_map/ppermute | solution.py:45
  49.6 0.4 turn.1.refs_6_.refs_16_
  50.0 3.7 %collective-permute-done.15.refs_3_ = bf16[8,4736]{1,0:T(8,128)(2,1)S(1)} collective-permute-done((bf16[8,4736]{1,0:T(8,128)(2,1)S(1)}, bf16[8,4736]{1,0:T(8,128)(2,1)S(1)}, u32[]{:S(2)}, u32[]{:S(2)}) %collective-permute-start.15) | collective-permute-done | bytes 75808 | tf_op jit(solution)/shard_map/ppermute | solution.py:45
  53.7 0.9 %collective-permute-done.14.refs_2_ = bf16[8,4736]{1,0:T(8,128)(2,1)S(1)} collective-permute-done((bf16[8,4736]{1,0:T(8,128)(2,1)S(1)}, bf16[8,4736]{1,0:T(8,128)(2,1)S(1)}, u32[]{:S(2)}, u32[]{:S(2)}) %collective-permute-start.14) | collective-permute-done | bytes 75808 | tf_op jit(solution)/shard_map/ppermute | solution.py:45
  54.6 0.4 collective-permute-done.13.refs_1_
  55.0 0.1 error.1.refs_0_
  55.2 0.1 collective-permute-start.16
  55.2 1.9 %collective-permute-start.19 = (bf16[8,4736]{1,0:T(8,128)(2,1)S(1)}, bf16[8,4736]{1,0:T(8,128)(2,1)S(1)}, u32[]{:S(2)}, u32[]{:S(2)}) collective-permute-start(bf16[8,4736]{1,0:T(8,128)(2,1)S(1)} %error.1.refs_0_), channel_id=1, source_target_pairs={{0,17},{1,16},{2,19},{3,18},{4,21},{5,20},{6,23},{7,22},{8,25},{9,... | collective-permute-start | bytes 227336 | tf_op jit(solution)/shard_map/ppermute | solution.py:45
  57.2 0.5 collective-permute-start.18
  57.6 1.2 %collective-permute-start.17 = (bf16[8,4736]{1,0:T(8,128)(2,1)S(1)}, bf16[8,4736]{1,0:T(8,128)(2,1)S(1)}, u32[]{:S(2)}, u32[]{:S(2)}) collective-permute-start(bf16[8,4736]{1,0:T(8,128)(2,1)S(1)} %error.1.refs_0_), channel_id=1, source_target_pairs={{0,1},{1,0},{2,3},{3,2},{4,5},{5,4},{6,7},{7,6},{8,9},{9,8},{10,11... | collective-permute-start | bytes 227336 | tf_op jit(solution)/shard_map/ppermute | solution.py:45
  58.8 1.5 %first_back.1.refs_11_.refs_19_ = f32[64,2048]{1,0:T(8,128)S(1)} custom-call(bf16[8,4736]{1,0:T(8,128)(2,1)S(1)} %error.1.refs_0_, bf16[8,4736]{1,0:T(8,128)(2,1)S(1)} %collective-permute-done.16.refs_1_, bf16[512,4608]{1,0:T(8,128)(2,1)S(1)} %get-tuple-element.63.refs_0_.weight.refs_2_.refs_6_.refs_8_, ...), custom_call_target="tpu_custom_call" | custom-call | flops 301989888 | bytes 9437184 | tf_op jit(solution)/shard_map/first_back/pallas_call | solution.py:579
  60.4 2.6 %first_outer.1 = (bf16[2048,4608]{1,0:T(8,128)(2,1)}, f32[8,128]{1,0:T(8,128)S(1)}) custom-call(bf16[8,4736]{1,0:T(8,128)(2,1)S(1)} %error.1.refs_0_, bf16[8,4736]{1,0:T(8,128)(2,1)S(1)} %collective-permute-done.16.refs_1_, f32[512,1]{1,0:T(8,128)S(1)} %get-tuple-element.83.refs_2_.refs_4_, f32[512,1]{1,0:T(8,128)S(1)} %get-tuple-element.84.refs_3_.refs_5_, ...), custom_call_target="tpu_custom_call" | custom-call | flops 301989888 | bytes 9437184 | tf_op jit(solution)/shard_map/first_outer/pallas_call | solution.py:621
  63.0 0.1 collective-permute-start.20
  63.1 1.5 %collective-permute-done.20.refs_3_ = bf16[24,4736]{1,0:T(8,128)(2,1)S(1)} collective-permute-done((bf16[24,4736]{1,0:T(8,128)(2,1)S(1)}, bf16[24,4736]{1,0:T(8,128)(2,1)S(1)}, u32[]{:S(2)}, u32[]{:S(2)}) %collective-permute-start.20) | collective-permute-done | bytes 227360 | tf_op jit(solution)/shard_map/ppermute | solution.py:45
  64.6 16.6 %gradients.1 = (bf16[2048,4608]{1,0:T(8,128)(2,1)}, bf16[4608,2048]{1,0:T(8,128)(2,1)}, f32[1,2048]{1,0:T(1,128)}, f32[4608]{0:T(1024)}, f32[1,1]{1,0:T(1,128)}) custom-call(bf16[8,4736]{1,0:T(8,128)(2,1)S(1)} %error.1.refs_0_, bf16[8,4736]{1,0:T(8,128)(2,1)S(1)} %collective-permute-done.16.refs_1_, ...), custom_call_target="tpu_custom_call", output_to_operand_aliasing={{0}: (20, {})} | custom-call | flops 3623878656 | bytes 37748736 | tf_op jit(solution)/shard_map/gradients/pallas_call | solution.py:768
  (17 shorter events, 0.1 us)
Async XLA Ops:
  3.4 6.2 %collective-permute-start = (bf16[8,4608]{1,0:T(8,128)(2,1)S(1)}, bf16[8,4608]{1,0:T(8,128)(2,1)S(1)}, u32[]{:S(2)}, u32[]{:S(2)}) collective-permute-start(bf16[8,4608]{1,0:T(8,128)(2,1)S(1)} %get-tuple-element.53.refs_1_), channel_id=1, source_target_pairs={{0,1},{1,0},{2,3},{3,2},{4,5},{5,4},{6,7},{7,6},{8,9},{9,8},{10,11... | collective-permute-start | bytes 221192 | tf_op jit(solution)/shard_map/ppermute | solution.py:45
  9.6 10.5 %collective-permute-start.3 = (bf16[8,5760]{1,0:T(8,128)(2,1)S(1)}, bf16[8,5760]{1,0:T(8,128)(2,1)S(1)}, u32[]{:S(2)}, u32[]{:S(2)}) collective-permute-start(bf16[8,5760]{1,0:T(8,128)(2,1)S(1)} %heads_y.1.refs_3_.refs_0_), channel_id=1, source_target_pairs={{0,4},{1,5},{2,6},{3,7},{4,0},{5,1},{6,2},{7,3},{8,12},{9,13},{10,... | collective-permute-start | bytes 276488 | tf_op jit(solution)/shard_map/ppermute | solution.py:45
  12.2 7.9 %collective-permute-start.2 = (bf16[8,5760]{1,0:T(8,128)(2,1)S(1)}, bf16[8,5760]{1,0:T(8,128)(2,1)S(1)}, u32[]{:S(2)}, u32[]{:S(2)}) collective-permute-start(bf16[8,5760]{1,0:T(8,128)(2,1)S(1)} %heads_y.1.refs_3_.refs_0_), channel_id=1, source_target_pairs={{0,6},{1,7},{2,4},{3,5},{4,2},{5,3},{6,0},{7,1},{8,14},{9,15},{10,... | collective-permute-start | bytes 276488 | tf_op jit(solution)/shard_map/ppermute | solution.py:45
  13.6 6.6 %collective-permute-start.1 = (bf16[8,5760]{1,0:T(8,128)(2,1)S(1)}, bf16[8,5760]{1,0:T(8,128)(2,1)S(1)}, u32[]{:S(2)}, u32[]{:S(2)}) collective-permute-start(bf16[8,5760]{1,0:T(8,128)(2,1)S(1)} %heads_y.1.refs_3_.refs_0_), channel_id=1, source_target_pairs={{0,2},{1,3},{2,0},{3,1},{4,6},{5,7},{6,4},{7,5},{8,10},{9,11},{10,... | collective-permute-start | bytes 276488 | tf_op jit(solution)/shard_map/ppermute | solution.py:45
  20.4 8.8 %copy-start = (f32[2048]{0:T(1024)S(1)}, f32[2048]{0:T(1024)}, u32[]{:S(2)}) copy-start(f32[2048]{0:T(1024)} %refs_7_.1) | copy-start | bytes 24580
  20.4 6.2 %collective-permute-start.6 = (bf16[8,4608]{1,0:T(8,128)(2,1)S(1)}, bf16[8,4608]{1,0:T(8,128)(2,1)S(1)}, u32[]{:S(2)}, u32[]{:S(2)}) collective-permute-start(bf16[8,4608]{1,0:T(8,128)(2,1)S(1)} %residual.1.refs_1_.refs_0_), channel_id=1, source_target_pairs={{0,17},{1,16},{2,19},{3,18},{4,21},{5,20},{6,23},{7,22},{8,25},{9,... | collective-permute-start | bytes 221192 | tf_op jit(solution)/shard_map/ppermute | solution.py:45
  22.6 4.4 %collective-permute-start.5 = (bf16[8,4608]{1,0:T(8,128)(2,1)S(1)}, bf16[8,4608]{1,0:T(8,128)(2,1)S(1)}, u32[]{:S(2)}, u32[]{:S(2)}) collective-permute-start(bf16[8,4608]{1,0:T(8,128)(2,1)S(1)} %residual.1.refs_1_.refs_0_), channel_id=1, source_target_pairs={{0,16},{1,17},{2,18},{3,19},{4,20},{5,21},{6,22},{7,23},{8,24},{9,... | collective-permute-start | bytes 221192 | tf_op jit(solution)/shard_map/ppermute | solution.py:45
  23.1 4.4 %collective-permute-start.4 = (bf16[8,4608]{1,0:T(8,128)(2,1)S(1)}, bf16[8,4608]{1,0:T(8,128)(2,1)S(1)}, u32[]{:S(2)}, u32[]{:S(2)}) collective-permute-start(bf16[8,4608]{1,0:T(8,128)(2,1)S(1)} %residual.1.refs_1_.refs_0_), channel_id=1, source_target_pairs={{0,1},{1,0},{2,3},{3,2},{4,5},{5,4},{6,7},{7,6},{8,9},{9,8},{10,11... | collective-permute-start | bytes 221192 | tf_op jit(solution)/shard_map/ppermute | solution.py:45
  27.5 1.7 %collective-permute-start.8 = (bf16[24,4608]{1,0:T(8,128)(2,1)S(1)}, bf16[24,4608]{1,0:T(8,128)(2,1)S(1)}, u32[]{:S(2)}, u32[]{:S(2)}) collective-permute-start(bf16[24,4608]{1,0:T(8,128)(2,1)S(1)} %stack.2.refs_1_), channel_id=1, source_target_pairs={{0,8},{1,9},{2,10},{3,11},{4,12},{5,13},{6,14},{7,15},{8,0},{9,1},... | collective-permute-start | bytes 663560 | tf_op jit(solution)/shard_map/ppermute | solution.py:45
  27.6 1.6 %collective-permute-start.7 = (bf16[8,4608]{1,0:T(8,128)(2,1)S(1)}, bf16[8,4608]{1,0:T(8,128)(2,1)S(1)}, u32[]{:S(2)}, u32[]{:S(2)}) collective-permute-start(bf16[8,4608]{1,0:T(8,128)(2,1)S(1)} %residual.1.refs_1_.refs_0_), channel_id=1, source_target_pairs={{0,8},{1,9},{2,10},{3,11},{4,12},{5,13},{6,14},{7,15},{8,0},{9,1},... | collective-permute-start | bytes 221192 | tf_op jit(solution)/shard_map/ppermute | solution.py:45
  36.6 1.6 %collective-permute-start.9 = (bf16[32,4608]{1,0:T(8,128)(2,1)S(1)}, bf16[32,4608]{1,0:T(8,128)(2,1)S(1)}, u32[]{:S(2)}, u32[]{:S(2)}) collective-permute-start(bf16[32,4608]{1,0:T(8,128)(2,1)S(1)} %get-tuple-element.68.after), channel_id=1, source_target_pairs={{0,8},{1,9},{2,10},{3,11},{4,12},{5,13},{6,14},{7,15},{8,0},{9,1},... | collective-permute-start | bytes 884744 | tf_op jit(solution)/shard_map/ppermute | solution.py:45
  38.4 6.9 %collective-permute-start.10 = (bf16[32,1152]{1,0:T(8,128)(2,1)S(1)}, bf16[32,1152]{1,0:T(8,128)(2,1)S(1)}, u32[]{:S(2)}, u32[]{:S(2)}) collective-permute-start(bf16[32,1152]{1,0:T(8,128)(2,1)S(1)} %get-tuple-element.72), channel_id=1, source_target_pairs={{0,17},{1,16},{2,19},{3,18},{4,21},{5,20},{6,23},{7,22},{8,25},{9,... | collective-permute-start | bytes 221192 | tf_op jit(solution)/shard_map/ppermute | solution.py:45
  40.2 5.1 %collective-permute-start.11 = (bf16[32,1152]{1,0:T(8,128)(2,1)S(1)}, bf16[32,1152]{1,0:T(8,128)(2,1)S(1)}, u32[]{:S(2)}, u32[]{:S(2)}) collective-permute-start(bf16[32,1152]{1,0:T(8,128)(2,1)S(1)} %get-tuple-element.73), channel_id=1, source_target_pairs={{0,16},{1,17},{2,18},{3,19},{4,20},{5,21},{6,22},{7,23},{8,24},{9,... | collective-permute-start | bytes 221192 | tf_op jit(solution)/shard_map/ppermute | solution.py:45
  40.7 4.6 %collective-permute-start.12 = (bf16[32,1152]{1,0:T(8,128)(2,1)S(1)}, bf16[32,1152]{1,0:T(8,128)(2,1)S(1)}, u32[]{:S(2)}, u32[]{:S(2)}) collective-permute-start(bf16[32,1152]{1,0:T(8,128)(2,1)S(1)} %get-tuple-element.74), channel_id=1, source_target_pairs={{0,1},{1,0},{2,3},{3,2},{4,5},{5,4},{6,7},{7,6},{8,9},{9,8},{10,11... | collective-permute-start | bytes 221192 | tf_op jit(solution)/shard_map/ppermute | solution.py:45
  45.4 8.3 %collective-permute-start.15 = (bf16[8,4736]{1,0:T(8,128)(2,1)S(1)}, bf16[8,4736]{1,0:T(8,128)(2,1)S(1)}, u32[]{:S(2)}, u32[]{:S(2)}) collective-permute-start(bf16[8,4736]{1,0:T(8,128)(2,1)S(1)} %recon.3.after.refs_0_), channel_id=1, source_target_pairs={{0,4},{1,5},{2,6},{3,7},{4,0},{5,1},{6,2},{7,3},{8,12},{9,13},{10,... | collective-permute-start | bytes 227336 | tf_op jit(solution)/shard_map/ppermute | solution.py:45
  48.3 6.3 %collective-permute-start.14 = (bf16[8,4736]{1,0:T(8,128)(2,1)S(1)}, bf16[8,4736]{1,0:T(8,128)(2,1)S(1)}, u32[]{:S(2)}, u32[]{:S(2)}) collective-permute-start(bf16[8,4736]{1,0:T(8,128)(2,1)S(1)} %recon.3.after.refs_0_), channel_id=1, source_target_pairs={{0,6},{1,7},{2,4},{3,5},{4,2},{5,3},{6,0},{7,1},{8,14},{9,15},{10,... | collective-permute-start | bytes 227336 | tf_op jit(solution)/shard_map/ppermute | solution.py:45
  49.6 5.5 %collective-permute-start.13 = (bf16[8,4736]{1,0:T(8,128)(2,1)S(1)}, bf16[8,4736]{1,0:T(8,128)(2,1)S(1)}, u32[]{:S(2)}, u32[]{:S(2)}) collective-permute-start(bf16[8,4736]{1,0:T(8,128)(2,1)S(1)} %recon.3.after.refs_0_), channel_id=1, source_target_pairs={{0,2},{1,3},{2,0},{3,1},{4,6},{5,7},{6,4},{7,5},{8,10},{9,11},{10,... | collective-permute-start | bytes 227336 | tf_op jit(solution)/shard_map/ppermute | solution.py:45
  55.2 3.6 %collective-permute-start.16 = (bf16[8,4736]{1,0:T(8,128)(2,1)S(1)}, bf16[8,4736]{1,0:T(8,128)(2,1)S(1)}, u32[]{:S(2)}, u32[]{:S(2)}) collective-permute-start(bf16[8,4736]{1,0:T(8,128)(2,1)S(1)} %error.1.refs_0_), channel_id=1, source_target_pairs={{0,8},{1,9},{2,10},{3,11},{4,12},{5,13},{6,14},{7,15},{8,0},{9,1},... | collective-permute-start | bytes 227336 | tf_op jit(solution)/shard_map/ppermute | solution.py:45
  55.2 7.7 %collective-permute-start.19 = (bf16[8,4736]{1,0:T(8,128)(2,1)S(1)}, bf16[8,4736]{1,0:T(8,128)(2,1)S(1)}, u32[]{:S(2)}, u32[]{:S(2)}) collective-permute-start(bf16[8,4736]{1,0:T(8,128)(2,1)S(1)} %error.1.refs_0_), channel_id=1, source_target_pairs={{0,17},{1,16},{2,19},{3,18},{4,21},{5,20},{6,23},{7,22},{8,25},{9,... | collective-permute-start | bytes 227336 | tf_op jit(solution)/shard_map/ppermute | solution.py:45
  57.2 5.8 %collective-permute-start.18 = (bf16[8,4736]{1,0:T(8,128)(2,1)S(1)}, bf16[8,4736]{1,0:T(8,128)(2,1)S(1)}, u32[]{:S(2)}, u32[]{:S(2)}) collective-permute-start(bf16[8,4736]{1,0:T(8,128)(2,1)S(1)} %error.1.refs_0_), channel_id=1, source_target_pairs={{0,16},{1,17},{2,18},{3,19},{4,20},{5,21},{6,22},{7,23},{8,24},{9,... | collective-permute-start | bytes 227336 | tf_op jit(solution)/shard_map/ppermute | solution.py:45
  57.6 5.3 %collective-permute-start.17 = (bf16[8,4736]{1,0:T(8,128)(2,1)S(1)}, bf16[8,4736]{1,0:T(8,128)(2,1)S(1)}, u32[]{:S(2)}, u32[]{:S(2)}) collective-permute-start(bf16[8,4736]{1,0:T(8,128)(2,1)S(1)} %error.1.refs_0_), channel_id=1, source_target_pairs={{0,1},{1,0},{2,3},{3,2},{4,5},{5,4},{6,7},{7,6},{8,9},{9,8},{10,11... | collective-permute-start | bytes 227336 | tf_op jit(solution)/shard_map/ppermute | solution.py:45
  63.0 1.6 %collective-permute-start.20 = (bf16[24,4736]{1,0:T(8,128)(2,1)S(1)}, bf16[24,4736]{1,0:T(8,128)(2,1)S(1)}, u32[]{:S(2)}, u32[]{:S(2)}) collective-permute-start(bf16[24,4736]{1,0:T(8,128)(2,1)S(1)} %stack.3.refs_2_), channel_id=1, source_target_pairs={{0,8},{1,9},{2,10},{3,11},{4,12},{5,13},{6,14},{7,15},{8,0},{9,1},... | collective-permute-start | bytes 681992 | tf_op jit(solution)/shard_map/ppermute | solution.py:45

commit v5 on v4

--- a/solution.py
+++ b/solution.py
@@ -560,35 +560,7 @@
     return lax.dot_general(error, weight, (((1,), (1,)), ((), ())), preferred_element_type=F32)
 
 
-def first_back(parts, height, weights, group):
-    features = weights[0].shape[1]
-    width = features // group.size
-    tokens = sum(p.shape[0] * (p.shape[1] // width) for p in parts)
-    latents = sum(w.shape[0] for w in weights)
-    rows = math.gcd(*[w.shape[0] for w in weights], 256)
-
-    def kernel(*refs):
-        pieces, held = refs[: len(parts)], refs[len(parts) : len(parts) + len(weights)]
-        back, error = refs[-2:]
-        columns = chunk_at(group, group.keys[0], width)
-        assemble(units(pieces, height), error, width)
-        for i, (p, r) in enumerate(row_blocks(held, rows)):
-            weight = held[p][r : r + rows, pl.ds(columns, width)]
-            back[:, i * rows : (i + 1) * rows] = back_product(error[...], weight)
-
-    return pl.pallas_call(
-        kernel,
-        in_specs=resident(len(parts) + len(weights)),
-        out_specs=pl.BlockSpec(memory_space=pltpu.VMEM),
-        out_shape=struct((tokens, latents), F32),
-        scratch_shapes=[pltpu.VMEM((tokens, width), BF16)],
-        compiler_params=params(8),
-        cost_estimate=cost(2 * tokens * width * latents, 4 * width * latents),
-        name="first_back",
-    )(*parts, *[in_vmem(w) for w in weights])
-
-
-def first_outer(parts, height, latents_t, coefs, weights, group, after):
+def first_gradients(parts, height, latents_t, coefs, weights, group):
     latents, tokens = latents_t.shape
     features = weights[0].shape[1]
     width = features // group.size
@@ -598,8 +570,7 @@
     def kernel(*refs):
         pieces, refs = refs[: len(parts)], refs[len(parts) :]
         coef, held = refs[:count], refs[count : 2 * count]
-        latents_t, _, dec_grad, ready, error, stage, sems = refs[2 * count :]
-        ready[...] = jnp.zeros_like(ready)
+        latents_t, dec_grad, back, error, stage, sems = refs[2 * count :]
         columns = chunk_at(group, group.keys[0], width)
         assemble(units(pieces, height), error, width)
         copies = []
@@ -614,24 +585,26 @@
             copies.append(
                 pltpu.make_async_copy(stage.at[at], dec_grad.at[at, pl.ds(columns, width)], sems.at[i])
             )
-            copies[-1].start()
-        for copy in copies:
-            copy.wait()
+        in_order(copies, "start")
+        for i, (p, r) in enumerate(row_blocks(held, rows)):
+            weight = held[p][r : r + rows, pl.ds(columns, width)]
+            back[:, i * rows : (i + 1) * rows] = back_product(error[...], weight)
+        in_order(copies, "wait")
 
     return pl.pallas_call(
         kernel,
-        in_specs=resident(len(parts) + 2 * count + 2),
+        in_specs=resident(len(parts) + 2 * count + 1),
         out_specs=anywhere(1) + resident(1),
-        out_shape=[struct((latents, features), BF16), struct((8, LANES), F32)],
+        out_shape=[struct((latents, features), BF16), struct((tokens, latents), F32)],
         scratch_shapes=[
             pltpu.VMEM((tokens, width), BF16),
             pltpu.VMEM((latents, width), BF16),
             pltpu.SemaphoreType.DMA((latents // rows,)),
         ],
         compiler_params=params(10),
-        cost_estimate=cost(2 * tokens * width * latents, 4 * width * latents),
-        name="first_outer",
-    )(*parts, *coefs, *[in_vmem(w) for w in weights], latents_t, after)
+        cost_estimate=cost(4 * tokens * width * latents, 4 * width * latents),
+        name="first_gradients",
+    )(*parts, *coefs, *[in_vmem(w) for w in weights], latents_t)
 
 
 def gradients(first, others, height, resid_t, preact, latents_t, coefs, weights, norm_rows, dec_grad, back, group):
@@ -862,9 +835,8 @@
 
         others = by_feature.spread(error_own)[1:]
         first, height = gather(by_token, error_own), error_own.shape[0]
-        back = first_back(first, height, held, by_feature)
-        dec_grad, ready = first_outer(first, height, latents_t, coefs, held, by_feature, back)
-        others = gather(by_token, stack(others, [ready])) if others else []
+        dec_grad, back = first_gradients(first, height, latents_t, coefs, held, by_feature)
+        others = gather(by_token, stack(others, [back])) if others else []
         dec_grad, enc_grad, bias_grad, column_sum, loss = gradients(
             first, others, height, resid_t, preact, latents_t, coefs, held, norm_rows, dec_grad, back, by_feature
         )

time: 81.6 us -> 81 us (level)
    pallas_call x2 -> x1, Pallas kernels: 4.14 us -> 3.73 us  [first_gradients(): pl.pallas_call(kernel, in_specs=resident(len(parts) + 2 * count + 1), out...]
where the time goes in v5:
time: 81 us; the launch traced here: 80.7 us
  Pallas kernels  47.8 us (59%)
  starting transfers between devices  23.1 us (29%)
  waiting for transfers between devices  8.81 us (11%)
  between operations  1.03 us (1%)
    ppermute x21, starting transfers between devices, swap(): return lax.ppermute(x, ('dp', 'fsdp'), pairs)  23.1 us
    pallas_call x1, Pallas kernels, gradients(): pl.pallas_call(kernel, in_specs=resident(len(flat) + 3 * count + 4) + any...  16.4 us
    pallas_call x3, Pallas kernels, load(): pl.pallas_call(kernel, in_specs=anywhere(len(items)) + resident(1), out_s...  12.1 us
    ppermute x21, waiting for transfers between devices, swap(): return lax.ppermute(x, ('dp', 'fsdp'), pairs)  8.81 us
    pallas_call x4, Pallas kernels, norms(): pl.pallas_call(kernel, in_specs=resident(3), out_specs=resident(3), out_s...  4.44 us
    pallas_call x1, Pallas kernels, encode(): pl.pallas_call(kernel, in_specs=resident(len(parts) + len(held) + 1) + an...  4.11 us
    pallas_call x1, Pallas kernels, first_gradients(): pl.pallas_call(kernel, in_specs=resident(len(parts) + 2 * count + 1), out...  3.73 us
    pallas_call x1, Pallas kernels, decode(): pl.pallas_call(kernel, in_specs=resident(1 + count), out_specs=resident(3...  3.36 us
  transfers between devices with their start and end apart: 21, of which 8 were waited for; matrix products, arithmetic and copies ran while one was open for 0% of the time, Pallas kernels for 26%

profile of v5, /device:TPU:0, one launch (start us, length us, event | category | flops | bytes accessed | tf_op | source)
XLA Modules:
  0.0 80.7 jit_solution(2258951498343898626)
XLA Ops:
  0.6 2.7 %project.1 = (bf16[8,1152]{1,0:T(8,128)(2,1)S(1)}, f32[1,4608]{1,0:T(1,128)S(1)}, f32[1,4608]{1,0:T(1,128)S(1)}, f32[8,4608]{1,0:T(8,128)S(1)}, bf16[8,4608]{1,0:T(8,128)(2,1)S(1)}) custom-call(bf16[16,512]{1,0:T(8,128)(2,1)} %refs_0_.4, bf16[512,4608]{1,0:T(8,128)(2,1)} %refs_1_.2, bf16[2,4608]{1,0:T(2,128)(2,1)} %refs_2_.2, f32[4608]{0:T(1024)} %refs_3_.1, ...), custom_call_target="tpu_custom_call" | custom-call | flops 75497472 | bytes 4718592 | tf_op jit(solution)/shard_map/project/pallas_call | solution.py:147
  3.4 3.0 %collective-permute-start = (bf16[8,4608]{1,0:T(8,128)(2,1)S(1)}, bf16[8,4608]{1,0:T(8,128)(2,1)S(1)}, u32[]{:S(2)}, u32[]{:S(2)}) collective-permute-start(bf16[8,4608]{1,0:T(8,128)(2,1)S(1)} %get-tuple-element.53.refs_1_), channel_id=1, source_target_pairs={{0,1},{1,0},{2,3},{3,2},{4,5},{5,4},{6,7},{7,6},{8,9},{9,8},{10,11... | collective-permute-start | bytes 221192 | tf_op jit(solution)/shard_map/ppermute | solution.py:45
  6.4 3.1 %load_first.1 = (bf16[1536,2048]{1,0:T(8,128)(2,1)S(1)}, f32[8,128]{1,0:T(8,128)S(1)}) custom-call(bf16[4608,2048]{1,0:T(8,128)(2,1)} %refs_1_.3, bf16[8,4608]{1,0:T(8,128)(2,1)S(1)} %get-tuple-element.53.refs_1_), custom_call_target="tpu_custom_call" | custom-call | bytes 6291456 | tf_op jit(solution)/shard_map/load_first/pallas_call | solution.py:370
  9.6 2.7 %collective-permute-start.3 = (bf16[8,5760]{1,0:T(8,128)(2,1)S(1)}, bf16[8,5760]{1,0:T(8,128)(2,1)S(1)}, u32[]{:S(2)}, u32[]{:S(2)}) collective-permute-start(bf16[8,5760]{1,0:T(8,128)(2,1)S(1)} %heads_y.1.refs_3_.refs_0_), channel_id=1, source_target_pairs={{0,4},{1,5},{2,6},{3,7},{4,0},{5,1},{6,2},{7,3},{8,12},{9,13},{10,... | collective-permute-start | bytes 276488 | tf_op jit(solution)/shard_map/ppermute | solution.py:45
  12.2 1.3 %collective-permute-start.2 = (bf16[8,5760]{1,0:T(8,128)(2,1)S(1)}, bf16[8,5760]{1,0:T(8,128)(2,1)S(1)}, u32[]{:S(2)}, u32[]{:S(2)}) collective-permute-start(bf16[8,5760]{1,0:T(8,128)(2,1)S(1)} %heads_y.1.refs_3_.refs_0_), channel_id=1, source_target_pairs={{0,6},{1,7},{2,4},{3,5},{4,2},{5,3},{6,0},{7,1},{8,14},{9,15},{10,... | collective-permute-start | bytes 276488 | tf_op jit(solution)/shard_map/ppermute | solution.py:45
  13.6 0.2 collective-permute-start.1
  13.8 6.3 %load_second.1 = (bf16[1536,2048]{1,0:T(8,128)(2,1)S(1)}, bf16[1536,2048]{1,0:T(8,128)(2,1)S(1)}, bf16[512,4608]{1,0:T(8,128)(2,1)S(1)}, f32[8,128]{1,0:T(8,128)S(1)}) custom-call(bf16[4608,2048]{1,0:T(8,128)(2,1)} %refs_1_.3, bf16[4608,2048]{1,0:T(8,128)(2,1)} %refs_1_.3, bf16[2048,4608]{1,0:T(8,128)(2,1)} %refs_8_.1, ...), custom_call_target="tpu_custom_call" | custom-call | bytes 17301504 | tf_op jit(solution)/shard_map/load_second/pallas_call | solution.py:370
  20.1 0.0 collective-permute-done.3.refs_3_
  20.1 0.2 residual.1.refs_1_.refs_0_
  20.4 0.0 copy-start
  20.4 2.2 %collective-permute-start.6 = (bf16[8,4608]{1,0:T(8,128)(2,1)S(1)}, bf16[8,4608]{1,0:T(8,128)(2,1)S(1)}, u32[]{:S(2)}, u32[]{:S(2)}) collective-permute-start(bf16[8,4608]{1,0:T(8,128)(2,1)S(1)} %residual.1.refs_1_.refs_0_), channel_id=1, source_target_pairs={{0,17},{1,16},{2,19},{3,18},{4,21},{5,20},{6,23},{7,22},{8,25},{9,... | collective-permute-start | bytes 221192 | tf_op jit(solution)/shard_map/ppermute | solution.py:45
  22.6 0.5 collective-permute-start.5
  23.1 0.8 %collective-permute-start.4 = (bf16[8,4608]{1,0:T(8,128)(2,1)S(1)}, bf16[8,4608]{1,0:T(8,128)(2,1)S(1)}, u32[]{:S(2)}, u32[]{:S(2)}) collective-permute-start(bf16[8,4608]{1,0:T(8,128)(2,1)S(1)} %residual.1.refs_1_.refs_0_), channel_id=1, source_target_pairs={{0,1},{1,0},{2,3},{3,2},{4,5},{5,4},{6,7},{7,6},{8,9},{9,8},{10,11... | collective-permute-start | bytes 221192 | tf_op jit(solution)/shard_map/ppermute | solution.py:45
  23.9 2.7 %load_third.1 = (bf16[512,4608]{1,0:T(8,128)(2,1)S(1)}, f32[8,128]{1,0:T(8,128)S(1)}) custom-call(bf16[2048,4608]{1,0:T(8,128)(2,1)} %refs_8_.1, bf16[8,4608]{1,0:T(8,128)(2,1)S(1)} %residual.1.refs_1_.refs_0_), custom_call_target="tpu_custom_call" | custom-call | bytes 4718592 | tf_op jit(solution)/shard_map/load_third/pallas_call | solution.py:370
  26.6 0.3 collective-permute-done.5.refs_1_
  26.9 0.5 collective-permute-done.4.refs_0_
  27.5 0.1 collective-permute-start.8
  27.6 0.5 collective-permute-start.7
  28.1 1.1 %collective-permute-done.7.refs_2_ = bf16[8,4608]{1,0:T(8,128)(2,1)S(1)} collective-permute-done((bf16[8,4608]{1,0:T(8,128)(2,1)S(1)}, bf16[8,4608]{1,0:T(8,128)(2,1)S(1)}, u32[]{:S(2)}, u32[]{:S(2)}) %collective-permute-start.7) | collective-permute-done | bytes 73760 | tf_op jit(solution)/shard_map/ppermute | solution.py:45
  29.2 4.1 %encode.1 = (f32[64,2048]{1,0:T(8,128)S(1)}, bf16[64,4608]{1,0:T(8,128)(2,1)S(1)}, bf16[512,4608]{1,0:T(8,128)(2,1)S(1)}, bf16[512,4608]{1,0:T(8,128)(2,1)S(1)}) custom-call(bf16[8,4608]{1,0:T(8,128)(2,1)S(1)} %residual.1.refs_1_.refs_0_, bf16[24,4608]{1,0:T(8,128)(2,1)S(1)} %stack.2.refs_1_, bf16[8,4608]{1,0:T(8,128)(2,1)S(1)} %collective-permute-done.7.refs_2_, ...), custom_call_target="tpu_custom_call" | custom-call | flops 1207959552 | bytes 589824 | tf_op jit(solution)/shard_map/encode/pallas_call | solution.py:449
  33.3 3.4 %decode.1 = (f32[32,4608]{1,0:T(8,128)S(1)}, bf16[32,4608]{1,0:T(8,128)(2,1)S(1)}, bf16[2048,64]{1,0:T(8,128)(2,1)S(1)}, f32[512,1]{1,0:T(8,128)S(1)}, f32[512,1...) custom-call(f32[64,2048]{1,0:T(8,128)S(1)} %get-tuple-element.62.preact.refs_17_, ...), custom_call_target="tpu_custom_call" | custom-call | flops 1207959552 | bytes 1769472 | tf_op jit(solution)/shard_map/decode/pallas_call | solution.py:493
  36.6 0.2 collective-permute-start.9
  36.9 1.1 %norms.4 = (f32[512,1]{1,0:T(8,128)S(1)}, f32[1,512]{1,0:T(1,128)S(1)}, f32[8,128]{1,0:T(8,128)S(1)}) custom-call(bf16[512,4608]{1,0:T(8,128)(2,1)S(1)} %get-tuple-element.63.refs_0_.weight.refs_6_.refs_8_, f32[512,1]{1,0:T(8,128)S(1)} %get-tuple-element.69.usage, bf16[32,4608]{1,0:T(8,128)(2,1)S(1)} %get-tuple-element.68.after), custom_call_target="tpu_custom_call" | custom-call | bytes 14155776 | tf_op jit(solution)/shard_map/norms/pallas_call | solution.py:402
  38.0 0.3 collective-permute-done.9.refs_1_
  38.3 0.1 recon.2
  38.4 1.8 %collective-permute-start.10 = (bf16[32,1152]{1,0:T(8,128)(2,1)S(1)}, bf16[32,1152]{1,0:T(8,128)(2,1)S(1)}, u32[]{:S(2)}, u32[]{:S(2)}) collective-permute-start(bf16[32,1152]{1,0:T(8,128)(2,1)S(1)} %get-tuple-element.72), channel_id=1, source_target_pairs={{0,17},{1,16},{2,19},{3,18},{4,21},{5,20},{6,23},{7,22},{8,25},{9,... | collective-permute-start | bytes 221192 | tf_op jit(solution)/shard_map/ppermute | solution.py:45
  40.2 0.5 collective-permute-start.11
  40.7 1.2 %collective-permute-start.12 = (bf16[32,1152]{1,0:T(8,128)(2,1)S(1)}, bf16[32,1152]{1,0:T(8,128)(2,1)S(1)}, u32[]{:S(2)}, u32[]{:S(2)}) collective-permute-start(bf16[32,1152]{1,0:T(8,128)(2,1)S(1)} %get-tuple-element.74), channel_id=1, source_target_pairs={{0,1},{1,0},{2,3},{3,2},{4,5},{5,4},{6,7},{7,6},{8,9},{9,8},{10,11... | collective-permute-start | bytes 221192 | tf_op jit(solution)/shard_map/ppermute | solution.py:45
  41.9 1.1 %norms.7 = (f32[512,1]{1,0:T(8,128)S(1)}, f32[1,512]{1,0:T(1,128)S(1)}, f32[8,128]{1,0:T(8,128)S(1)}) custom-call(bf16[512,4608]{1,0:T(8,128)(2,1)S(1)} %get-tuple-element.66.refs_3_.weight.refs_9_.refs_11_, f32[512,1]{1,0:T(8,128)S(1)} %get-tuple-element.79.usage, f32[32,1152]{1,0:T(8,128)S(1)} %get-tuple-element.71.after.refs_0_), custom_call_target="tpu_custom_call" | custom-call | bytes 14155776 | tf_op jit(solution)/shard_map/norms/pallas_call | solution.py:402
  43.0 1.1 %norms.6 = (f32[512,1]{1,0:T(8,128)S(1)}, f32[1,512]{1,0:T(1,128)S(1)}, f32[8,128]{1,0:T(8,128)S(1)}) custom-call(bf16[512,4608]{1,0:T(8,128)(2,1)S(1)} %get-tuple-element.65.refs_2_.weight.refs_8_.refs_10_, f32[512,1]{1,0:T(8,128)S(1)} %get-tuple-element.77.usage, f32[32,1152]{1,0:T(8,128)S(1)} %get-tuple-element.71.after.refs_0_), custom_call_target="tpu_custom_call" | custom-call | bytes 14155776 | tf_op jit(solution)/shard_map/norms/pallas_call | solution.py:402
  44.1 1.1 %norms.5 = (f32[512,1]{1,0:T(8,128)S(1)}, f32[1,512]{1,0:T(1,128)S(1)}, f32[8,128]{1,0:T(8,128)S(1)}) custom-call(bf16[512,4608]{1,0:T(8,128)(2,1)S(1)} %get-tuple-element.64.refs_1_.weight.refs_7_.refs_9_, f32[512,1]{1,0:T(8,128)S(1)} %get-tuple-element.75.usage, f32[32,1152]{1,0:T(8,128)S(1)} %get-tuple-element.71.after.refs_0_), custom_call_target="tpu_custom_call" | custom-call | bytes 14155776 | tf_op jit(solution)/shard_map/norms/pallas_call | solution.py:402
  45.3 0.0 collective-permute-done.12.refs_3_
  45.3 0.1 recon.3.after.refs_0_
  45.4 2.9 %collective-permute-start.15 = (bf16[8,4736]{1,0:T(8,128)(2,1)S(1)}, bf16[8,4736]{1,0:T(8,128)(2,1)S(1)}, u32[]{:S(2)}, u32[]{:S(2)}) collective-permute-start(bf16[8,4736]{1,0:T(8,128)(2,1)S(1)} %recon.3.after.refs_0_), channel_id=1, source_target_pairs={{0,4},{1,5},{2,6},{3,7},{4,0},{5,1},{6,2},{7,3},{8,12},{9,13},{10,... | collective-permute-start | bytes 227336 | tf_op jit(solution)/shard_map/ppermute | solution.py:45
  48.3 1.3 %collective-permute-start.14 = (bf16[8,4736]{1,0:T(8,128)(2,1)S(1)}, bf16[8,4736]{1,0:T(8,128)(2,1)S(1)}, u32[]{:S(2)}, u32[]{:S(2)}) collective-permute-start(bf16[8,4736]{1,0:T(8,128)(2,1)S(1)} %recon.3.after.refs_0_), channel_id=1, source_target_pairs={{0,6},{1,7},{2,4},{3,5},{4,2},{5,3},{6,0},{7,1},{8,14},{9,15},{10,... | collective-permute-start | bytes 227336 | tf_op jit(solution)/shard_map/ppermute | solution.py:45
  49.6 0.4 turn.1.refs_6_.refs_16_
  50.0 3.7 %collective-permute-done.15.refs_3_ = bf16[8,4736]{1,0:T(8,128)(2,1)S(1)} collective-permute-done((bf16[8,4736]{1,0:T(8,128)(2,1)S(1)}, bf16[8,4736]{1,0:T(8,128)(2,1)S(1)}, u32[]{:S(2)}, u32[]{:S(2)}) %collective-permute-start.15) | collective-permute-done | bytes 75808 | tf_op jit(solution)/shard_map/ppermute | solution.py:45
  53.7 0.9 %collective-permute-done.14.refs_2_ = bf16[8,4736]{1,0:T(8,128)(2,1)S(1)} collective-permute-done((bf16[8,4736]{1,0:T(8,128)(2,1)S(1)}, bf16[8,4736]{1,0:T(8,128)(2,1)S(1)}, u32[]{:S(2)}, u32[]{:S(2)}) %collective-permute-start.14) | collective-permute-done | bytes 75808 | tf_op jit(solution)/shard_map/ppermute | solution.py:45
  54.6 0.4 collective-permute-done.13.refs_1_
  55.0 0.1 error.1.refs_0_
  55.2 0.1 collective-permute-start.16
  55.2 1.9 %collective-permute-start.19 = (bf16[8,4736]{1,0:T(8,128)(2,1)S(1)}, bf16[8,4736]{1,0:T(8,128)(2,1)S(1)}, u32[]{:S(2)}, u32[]{:S(2)}) collective-permute-start(bf16[8,4736]{1,0:T(8,128)(2,1)S(1)} %error.1.refs_0_), channel_id=1, source_target_pairs={{0,17},{1,16},{2,19},{3,18},{4,21},{5,20},{6,23},{7,22},{8,25},{9,... | collective-permute-start | bytes 227336 | tf_op jit(solution)/shard_map/ppermute | solution.py:45
  57.2 0.5 collective-permute-start.18
  57.6 1.2 %collective-permute-start.17 = (bf16[8,4736]{1,0:T(8,128)(2,1)S(1)}, bf16[8,4736]{1,0:T(8,128)(2,1)S(1)}, u32[]{:S(2)}, u32[]{:S(2)}) collective-permute-start(bf16[8,4736]{1,0:T(8,128)(2,1)S(1)} %error.1.refs_0_), channel_id=1, source_target_pairs={{0,1},{1,0},{2,3},{3,2},{4,5},{5,4},{6,7},{7,6},{8,9},{9,8},{10,11... | collective-permute-start | bytes 227336 | tf_op jit(solution)/shard_map/ppermute | solution.py:45
  58.8 3.7 %first_gradients.1 = (bf16[2048,4608]{1,0:T(8,128)(2,1)}, f32[64,2048]{1,0:T(8,128)S(1)}) custom-call(bf16[8,4736]{1,0:T(8,128)(2,1)S(1)} %error.1.refs_0_, bf16[8,4736]{1,0:T(8,128)(2,1)S(1)} %collective-permute-done.16.refs_1_, f32[512,1]{1,0:T(8,128)S(1)} %get-tuple-element.83.refs_2_.refs_4_, f32[512,1]{1,0:T(8,128)S(1)} %get-tuple-element.84.refs_3_.refs_5_, ...), custom_call_target="tpu_custom_call" | custom-call | flops 603979776 | bytes 9437184 | tf_op jit(solution)/shard_map/first_gradients/pallas_call | solution.py:594
  62.6 0.1 collective-permute-start.20
  62.7 1.5 %collective-permute-done.20.refs_3_ = bf16[24,4736]{1,0:T(8,128)(2,1)S(1)} collective-permute-done((bf16[24,4736]{1,0:T(8,128)(2,1)S(1)}, bf16[24,4736]{1,0:T(8,128)(2,1)S(1)}, u32[]{:S(2)}, u32[]{:S(2)}) %collective-permute-start.20) | collective-permute-done | bytes 227360 | tf_op jit(solution)/shard_map/ppermute | solution.py:45
  64.2 16.4 %gradients.1 = (bf16[2048,4608]{1,0:T(8,128)(2,1)}, bf16[4608,2048]{1,0:T(8,128)(2,1)}, f32[1,2048]{1,0:T(1,128)}, f32[4608]{0:T(1024)}, f32[1,1]{1,0:T(1,128)}) custom-call(bf16[8,4736]{1,0:T(8,128)(2,1)S(1)} %error.1.refs_0_, bf16[8,4736]{1,0:T(8,128)(2,1)S(1)} %collective-permute-done.16.refs_1_, ...), custom_call_target="tpu_custom_call", output_to_operand_aliasing={{0}: (20, {})} | custom-call | flops 3623878656 | bytes 37748736 | tf_op jit(solution)/shard_map/gradients/pallas_call | solution.py:741
  (16 shorter events, 0.1 us)
Async XLA Ops:
  3.4 6.2 %collective-permute-start = (bf16[8,4608]{1,0:T(8,128)(2,1)S(1)}, bf16[8,4608]{1,0:T(8,128)(2,1)S(1)}, u32[]{:S(2)}, u32[]{:S(2)}) collective-permute-start(bf16[8,4608]{1,0:T(8,128)(2,1)S(1)} %get-tuple-element.53.refs_1_), channel_id=1, source_target_pairs={{0,1},{1,0},{2,3},{3,2},{4,5},{5,4},{6,7},{7,6},{8,9},{9,8},{10,11... | collective-permute-start | bytes 221192 | tf_op jit(solution)/shard_map/ppermute | solution.py:45
  9.6 10.5 %collective-permute-start.3 = (bf16[8,5760]{1,0:T(8,128)(2,1)S(1)}, bf16[8,5760]{1,0:T(8,128)(2,1)S(1)}, u32[]{:S(2)}, u32[]{:S(2)}) collective-permute-start(bf16[8,5760]{1,0:T(8,128)(2,1)S(1)} %heads_y.1.refs_3_.refs_0_), channel_id=1, source_target_pairs={{0,4},{1,5},{2,6},{3,7},{4,0},{5,1},{6,2},{7,3},{8,12},{9,13},{10,... | collective-permute-start | bytes 276488 | tf_op jit(solution)/shard_map/ppermute | solution.py:45
  12.2 7.9 %collective-permute-start.2 = (bf16[8,5760]{1,0:T(8,128)(2,1)S(1)}, bf16[8,5760]{1,0:T(8,128)(2,1)S(1)}, u32[]{:S(2)}, u32[]{:S(2)}) collective-permute-start(bf16[8,5760]{1,0:T(8,128)(2,1)S(1)} %heads_y.1.refs_3_.refs_0_), channel_id=1, source_target_pairs={{0,6},{1,7},{2,4},{3,5},{4,2},{5,3},{6,0},{7,1},{8,14},{9,15},{10,... | collective-permute-start | bytes 276488 | tf_op jit(solution)/shard_map/ppermute | solution.py:45
  13.6 6.6 %collective-permute-start.1 = (bf16[8,5760]{1,0:T(8,128)(2,1)S(1)}, bf16[8,5760]{1,0:T(8,128)(2,1)S(1)}, u32[]{:S(2)}, u32[]{:S(2)}) collective-permute-start(bf16[8,5760]{1,0:T(8,128)(2,1)S(1)} %heads_y.1.refs_3_.refs_0_), channel_id=1, source_target_pairs={{0,2},{1,3},{2,0},{3,1},{4,6},{5,7},{6,4},{7,5},{8,10},{9,11},{10,... | collective-permute-start | bytes 276488 | tf_op jit(solution)/shard_map/ppermute | solution.py:45
  20.4 8.8 %copy-start = (f32[2048]{0:T(1024)S(1)}, f32[2048]{0:T(1024)}, u32[]{:S(2)}) copy-start(f32[2048]{0:T(1024)} %refs_7_.1) | copy-start | bytes 24580
  20.4 6.2 %collective-permute-start.6 = (bf16[8,4608]{1,0:T(8,128)(2,1)S(1)}, bf16[8,4608]{1,0:T(8,128)(2,1)S(1)}, u32[]{:S(2)}, u32[]{:S(2)}) collective-permute-start(bf16[8,4608]{1,0:T(8,128)(2,1)S(1)} %residual.1.refs_1_.refs_0_), channel_id=1, source_target_pairs={{0,17},{1,16},{2,19},{3,18},{4,21},{5,20},{6,23},{7,22},{8,25},{9,... | collective-permute-start | bytes 221192 | tf_op jit(solution)/shard_map/ppermute | solution.py:45
  22.6 4.4 %collective-permute-start.5 = (bf16[8,4608]{1,0:T(8,128)(2,1)S(1)}, bf16[8,4608]{1,0:T(8,128)(2,1)S(1)}, u32[]{:S(2)}, u32[]{:S(2)}) collective-permute-start(bf16[8,4608]{1,0:T(8,128)(2,1)S(1)} %residual.1.refs_1_.refs_0_), channel_id=1, source_target_pairs={{0,16},{1,17},{2,18},{3,19},{4,20},{5,21},{6,22},{7,23},{8,24},{9,... | collective-permute-start | bytes 221192 | tf_op jit(solution)/shard_map/ppermute | solution.py:45
  23.1 4.4 %collective-permute-start.4 = (bf16[8,4608]{1,0:T(8,128)(2,1)S(1)}, bf16[8,4608]{1,0:T(8,128)(2,1)S(1)}, u32[]{:S(2)}, u32[]{:S(2)}) collective-permute-start(bf16[8,4608]{1,0:T(8,128)(2,1)S(1)} %residual.1.refs_1_.refs_0_), channel_id=1, source_target_pairs={{0,1},{1,0},{2,3},{3,2},{4,5},{5,4},{6,7},{7,6},{8,9},{9,8},{10,11... | collective-permute-start | bytes 221192 | tf_op jit(solution)/shard_map/ppermute | solution.py:45
  27.5 1.7 %collective-permute-start.8 = (bf16[24,4608]{1,0:T(8,128)(2,1)S(1)}, bf16[24,4608]{1,0:T(8,128)(2,1)S(1)}, u32[]{:S(2)}, u32[]{:S(2)}) collective-permute-start(bf16[24,4608]{1,0:T(8,128)(2,1)S(1)} %stack.2.refs_1_), channel_id=1, source_target_pairs={{0,8},{1,9},{2,10},{3,11},{4,12},{5,13},{6,14},{7,15},{8,0},{9,1},... | collective-permute-start | bytes 663560 | tf_op jit(solution)/shard_map/ppermute | solution.py:45
  27.6 1.6 %collective-permute-start.7 = (bf16[8,4608]{1,0:T(8,128)(2,1)S(1)}, bf16[8,4608]{1,0:T(8,128)(2,1)S(1)}, u32[]{:S(2)}, u32[]{:S(2)}) collective-permute-start(bf16[8,4608]{1,0:T(8,128)(2,1)S(1)} %residual.1.refs_1_.refs_0_), channel_id=1, source_target_pairs={{0,8},{1,9},{2,10},{3,11},{4,12},{5,13},{6,14},{7,15},{8,0},{9,1},... | collective-permute-start | bytes 221192 | tf_op jit(solution)/shard_map/ppermute | solution.py:45
  36.6 1.6 %collective-permute-start.9 = (bf16[32,4608]{1,0:T(8,128)(2,1)S(1)}, bf16[32,4608]{1,0:T(8,128)(2,1)S(1)}, u32[]{:S(2)}, u32[]{:S(2)}) collective-permute-start(bf16[32,4608]{1,0:T(8,128)(2,1)S(1)} %get-tuple-element.68.after), channel_id=1, source_target_pairs={{0,8},{1,9},{2,10},{3,11},{4,12},{5,13},{6,14},{7,15},{8,0},{9,1},... | collective-permute-start | bytes 884744 | tf_op jit(solution)/shard_map/ppermute | solution.py:45
  38.4 6.9 %collective-permute-start.10 = (bf16[32,1152]{1,0:T(8,128)(2,1)S(1)}, bf16[32,1152]{1,0:T(8,128)(2,1)S(1)}, u32[]{:S(2)}, u32[]{:S(2)}) collective-permute-start(bf16[32,1152]{1,0:T(8,128)(2,1)S(1)} %get-tuple-element.72), channel_id=1, source_target_pairs={{0,17},{1,16},{2,19},{3,18},{4,21},{5,20},{6,23},{7,22},{8,25},{9,... | collective-permute-start | bytes 221192 | tf_op jit(solution)/shard_map/ppermute | solution.py:45
  40.2 5.1 %collective-permute-start.11 = (bf16[32,1152]{1,0:T(8,128)(2,1)S(1)}, bf16[32,1152]{1,0:T(8,128)(2,1)S(1)}, u32[]{:S(2)}, u32[]{:S(2)}) collective-permute-start(bf16[32,1152]{1,0:T(8,128)(2,1)S(1)} %get-tuple-element.73), channel_id=1, source_target_pairs={{0,16},{1,17},{2,18},{3,19},{4,20},{5,21},{6,22},{7,23},{8,24},{9,... | collective-permute-start | bytes 221192 | tf_op jit(solution)/shard_map/ppermute | solution.py:45
  40.7 4.6 %collective-permute-start.12 = (bf16[32,1152]{1,0:T(8,128)(2,1)S(1)}, bf16[32,1152]{1,0:T(8,128)(2,1)S(1)}, u32[]{:S(2)}, u32[]{:S(2)}) collective-permute-start(bf16[32,1152]{1,0:T(8,128)(2,1)S(1)} %get-tuple-element.74), channel_id=1, source_target_pairs={{0,1},{1,0},{2,3},{3,2},{4,5},{5,4},{6,7},{7,6},{8,9},{9,8},{10,11... | collective-permute-start | bytes 221192 | tf_op jit(solution)/shard_map/ppermute | solution.py:45
  45.4 8.3 %collective-permute-start.15 = (bf16[8,4736]{1,0:T(8,128)(2,1)S(1)}, bf16[8,4736]{1,0:T(8,128)(2,1)S(1)}, u32[]{:S(2)}, u32[]{:S(2)}) collective-permute-start(bf16[8,4736]{1,0:T(8,128)(2,1)S(1)} %recon.3.after.refs_0_), channel_id=1, source_target_pairs={{0,4},{1,5},{2,6},{3,7},{4,0},{5,1},{6,2},{7,3},{8,12},{9,13},{10,... | collective-permute-start | bytes 227336 | tf_op jit(solution)/shard_map/ppermute | solution.py:45
  48.3 6.3 %collective-permute-start.14 = (bf16[8,4736]{1,0:T(8,128)(2,1)S(1)}, bf16[8,4736]{1,0:T(8,128)(2,1)S(1)}, u32[]{:S(2)}, u32[]{:S(2)}) collective-permute-start(bf16[8,4736]{1,0:T(8,128)(2,1)S(1)} %recon.3.after.refs_0_), channel_id=1, source_target_pairs={{0,6},{1,7},{2,4},{3,5},{4,2},{5,3},{6,0},{7,1},{8,14},{9,15},{10,... | collective-permute-start | bytes 227336 | tf_op jit(solution)/shard_map/ppermute | solution.py:45
  49.6 5.5 %collective-permute-start.13 = (bf16[8,4736]{1,0:T(8,128)(2,1)S(1)}, bf16[8,4736]{1,0:T(8,128)(2,1)S(1)}, u32[]{:S(2)}, u32[]{:S(2)}) collective-permute-start(bf16[8,4736]{1,0:T(8,128)(2,1)S(1)} %recon.3.after.refs_0_), channel_id=1, source_target_pairs={{0,2},{1,3},{2,0},{3,1},{4,6},{5,7},{6,4},{7,5},{8,10},{9,11},{10,... | collective-permute-start | bytes 227336 | tf_op jit(solution)/shard_map/ppermute | solution.py:45
  55.2 3.6 %collective-permute-start.16 = (bf16[8,4736]{1,0:T(8,128)(2,1)S(1)}, bf16[8,4736]{1,0:T(8,128)(2,1)S(1)}, u32[]{:S(2)}, u32[]{:S(2)}) collective-permute-start(bf16[8,4736]{1,0:T(8,128)(2,1)S(1)} %error.1.refs_0_), channel_id=1, source_target_pairs={{0,8},{1,9},{2,10},{3,11},{4,12},{5,13},{6,14},{7,15},{8,0},{9,1},... | collective-permute-start | bytes 227336 | tf_op jit(solution)/shard_map/ppermute | solution.py:45
  55.2 7.3 %collective-permute-start.19 = (bf16[8,4736]{1,0:T(8,128)(2,1)S(1)}, bf16[8,4736]{1,0:T(8,128)(2,1)S(1)}, u32[]{:S(2)}, u32[]{:S(2)}) collective-permute-start(bf16[8,4736]{1,0:T(8,128)(2,1)S(1)} %error.1.refs_0_), channel_id=1, source_target_pairs={{0,17},{1,16},{2,19},{3,18},{4,21},{5,20},{6,23},{7,22},{8,25},{9,... | collective-permute-start | bytes 227336 | tf_op jit(solution)/shard_map/ppermute | solution.py:45
  57.2 5.4 %collective-permute-start.18 = (bf16[8,4736]{1,0:T(8,128)(2,1)S(1)}, bf16[8,4736]{1,0:T(8,128)(2,1)S(1)}, u32[]{:S(2)}, u32[]{:S(2)}) collective-permute-start(bf16[8,4736]{1,0:T(8,128)(2,1)S(1)} %error.1.refs_0_), channel_id=1, source_target_pairs={{0,16},{1,17},{2,18},{3,19},{4,20},{5,21},{6,22},{7,23},{8,24},{9,... | collective-permute-start | bytes 227336 | tf_op jit(solution)/shard_map/ppermute | solution.py:45
  57.6 4.9 %collective-permute-start.17 = (bf16[8,4736]{1,0:T(8,128)(2,1)S(1)}, bf16[8,4736]{1,0:T(8,128)(2,1)S(1)}, u32[]{:S(2)}, u32[]{:S(2)}) collective-permute-start(bf16[8,4736]{1,0:T(8,128)(2,1)S(1)} %error.1.refs_0_), channel_id=1, source_target_pairs={{0,1},{1,0},{2,3},{3,2},{4,5},{5,4},{6,7},{7,6},{8,9},{9,8},{10,11... | collective-permute-start | bytes 227336 | tf_op jit(solution)/shard_map/ppermute | solution.py:45
  62.6 1.6 %collective-permute-start.20 = (bf16[24,4736]{1,0:T(8,128)(2,1)S(1)}, bf16[24,4736]{1,0:T(8,128)(2,1)S(1)}, u32[]{:S(2)}, u32[]{:S(2)}) collective-permute-start(bf16[24,4736]{1,0:T(8,128)(2,1)S(1)} %stack.3.refs_2_), channel_id=1, source_target_pairs={{0,8},{1,9},{2,10},{3,11},{4,12},{5,13},{6,14},{7,15},{8,0},{9,1},... | collective-permute-start | bytes 681992 | tf_op jit(solution)/shard_map/ppermute | solution.py:45
